TPU v7x, 32 devices: a whole 2x2x4 slice. The times are simulated.
32 devices in a mesh: rep: 2 (over x), shard: 16 (over z, y, core).
Axes of the slice: x: 2, y: 2, z: 4, core: 2. Of those that a mesh axis runs over, the one named last changes fastest.
Arguments:
- hidden: bfloat16 [8192, 48], P(('rep', 'shard')), may hold values from -6 to 6
- cotangent: bfloat16 [8192, 5120], P(('rep', 'shard')), may hold values from -6 to 6
- master: float32 [48, 5120], P('shard'), may hold values from -0.078125 to 0.078125
- moment: float32 [48, 5120], P('shard'), may hold values from -6 to 6
- second: float32 [48, 5120], P('shard'), may hold values from 0.1 to 10
Outputs:
- input_grad: bfloat16 [8192, 48], P(('rep', 'shard'))
- master_new: float32 [48, 5120], P('shard')
- moment_new: float32 [48, 5120], P('shard')
- second_new: float32 [48, 5120], P('shard')
- updated_weights: bfloat16 [48, 5120], replicated
All inputs are finite; a program needn't handle non-finite values.
Results may differ from a plain program's by a relative error of at most 0.0059.
Values may be sent and summed in bfloat16 or wider, within the bound.
No kernel may reach another device: no remote copies, remote signals or barrier semaphores. Data moves between devices by JAX's collectives and lax.ppermute only.
A program may use at most 64 MiB of HBM per device.

v0:
```python
import math

import jax
import jax.numpy as jnp
from jax import lax
from jax.sharding import PartitionSpec as P


def adam_update(master, moment, second, gradient):
    moment_new = 0.9 * moment + 0.1 * gradient
    second_new = 0.95 * second + 0.05 * gradient * gradient
    first_fix = moment_new / (1.0 - 0.9**10)
    second_fix = second_new / (1.0 - 0.95**10)
    master_new = master - 0.01 * (first_fix / (jnp.sqrt(second_fix) + 1e-08) + 0.1 * master)
    return (master_new, moment_new, second_new)


def local(hidden, cotangent, master, moment, second):
    rep_count = lax.axis_size("rep")
    shard_count = lax.axis_size("shard")
    factor = 1.0 / math.sqrt(hidden.shape[0] * rep_count * shard_count)
    weights = master.astype(jnp.bfloat16)
    input_grad = lax.dot_general(
        cotangent,
        lax.all_gather(weights, "shard", axis=0, tiled=True),
        (((1,), (1,)), ((), ())),
        preferred_element_type=jnp.float32,
    ).astype(jnp.bfloat16)
    partial_rows = lax.psum_scatter(
        lax.dot_general(
            hidden, cotangent, (((0,), (0,)), ((), ())), preferred_element_type=jnp.float32
        ),
        "shard",
        scatter_dimension=0,
        tiled=True,
    )
    grad_part = lax.psum(partial_rows.astype(jnp.bfloat16), "rep").astype(jnp.float32)
    gradient = grad_part * factor
    master_new, moment_new, second_new = adam_update(master, moment, second, gradient)
    updated_weights = lax.all_gather(master_new.astype(jnp.bfloat16), "shard", axis=0, tiled=True)
    return (input_grad, master_new, moment_new, second_new, updated_weights)


def solution(mesh):
    placed = (
        P(("rep", "shard"), None),
        P(("rep", "shard"), None),
        P("shard", None),
        P("shard", None),
        P("shard", None),
    )
    return jax.shard_map(
        local,
        mesh=mesh,
        in_specs=placed,
        out_specs=(
            P(("rep", "shard"), None),
            P("shard", None),
            P("shard", None),
            P("shard", None),
            P(),
        ),
        check_vma=False,
    )
```

profile of v0, /device:TPU:0, one launch (start us, length us, event | category | flops | bytes accessed | tf_op | source)
XLA Modules:
  0.0 134.5 jit_solution(16548365927551502660)
XLA Ops:
  0.6 0.0 copy-start
  0.6 0.0 copy-start.4
  0.7 0.0 copy-start.1
  0.7 0.0 copy-start.2
  0.7 1.7 %copy-done = bf16[256,5120]{1,0:T(8,128)(2,1)S(1)} copy-done((bf16[256,5120]{1,0:T(8,128)(2,1)S(1)}, bf16[256,5120]{1,0:T(8,128)(2,1)}, u32[]{:S(2)}) %copy-start) | copy-done | bytes 2621464
  2.4 0.0 copy-start.3
  2.4 2.3 %fusion.5 = f32[48,5120]{1,0:T(8,128)} fusion(bf16[256,48]{0,1:T(8,128)(2,1)} %param.5, bf16[256,5120]{1,0:T(8,128)(2,1)S(1)} %copy-done), kind=kOutput, calls=%fused_computation.11 | convolution fusion | flops 125829120 | bytes 3629056 | tf_op jit(solution)/shard_map/dot_general | solution.py:30
  4.7 74.3 %all-reduce.2 = bf16[48,5120]{1,0:T(8,128)(2,1)S(1)} all-reduce(f32[48,5120]{1,0:T(8,128)} %fusion.5), channel_id=2, replica_groups=mesh['rep'=2,'shard'=16] {'shard'}, use_global_device_ids=true, to_apply=%region_0.0.clone | all-reduce | flops 245760 | bytes 1474560
  79.0 0.0 copy-done.4
  79.0 0.6 dynamic-slice
  80.3 8.5 %psum.7 = bf16[3,5120]{1,0:T(4,128)(2,1)S(1)} all-reduce(bf16[3,5120]{1,0:T(4,128)(2,1)S(1)} %dynamic-slice_convert_fusion), channel_id=1, replica_groups=mesh['rep'=2,'shard'=16] {'rep'}, use_global_device_ids=true, to_apply=%region_1.0 | all-reduce | flops 15360 | bytes 61440 | tf_op jit(solution)/shard_map/psum | solution.py:37
  88.8 0.0 copy-done.1
  88.8 0.0 copy-done.2
  88.8 0.0 copy-done.3
  88.8 0.8 convert_bitcast_fusion
  89.6 19.2 %all-gather = bf16[16,3,5120]{2,1,0:T(4,128)(2,1)S(1)} all-gather(bf16[1,3,5120]{2,1,0:T(4,128)(2,1)S(1)} %get-tuple-element.9), channel_id=1, replica_groups=mesh['rep'=2,'shard'=16] {'shard'}, dimensions={0}, use_global_device_ids=true | all-gather | bytes 522240 | tf_op jit(solution)/shard_map/all_gather | solution.py:25
  108.9 1.2 reshape.11
  110.1 2.5 %convolution_convert_fusion = bf16[256,48]{0,1:T(8,128)(2,1)} fusion(bf16[256,5120]{1,0:T(8,128)(2,1)S(1)} %copy-done, bf16[48,5120]{1,0:T(8,128)(2,1)} %reshape.11), kind=kOutput, calls=%fused_computation | convolution fusion | flops 125841408 | bytes 3137536 | tf_op jit(solution)/shard_map/dot_general | solution.py:23
  112.6 20.7 %all-gather.1 = bf16[16,3,5120]{2,1,0:T(4,128)(2,1)S(1)} all-gather(bf16[1,3,5120]{2,1,0:T(4,128)(2,1)S(1)} %get-tuple-element.5), channel_id=1, replica_groups=mesh['rep'=2,'shard'=16] {'shard'}, dimensions={0}, use_global_device_ids=true | all-gather | bytes 522240 | tf_op jit(solution)/shard_map/all_gather | solution.py:40
  133.3 1.2 reshape.13
  (1 shorter events, 0.0 us)
Async XLA Ops:
  0.6 1.7 %copy-start = (bf16[256,5120]{1,0:T(8,128)(2,1)S(1)}, bf16[256,5120]{1,0:T(8,128)(2,1)}, u32[]{:S(2)}) copy-start(bf16[256,5120]{1,0:T(8,128)(2,1)} %param.6) | copy-start | bytes 7864324
  0.6 78.3 %copy-start.4 = (u32[32]{0:T(128)S(1)}, u32[32]{0:T(128)}, u32[]{:S(2)}) copy-start(u32[32]{0:T(128)} %constant.28) | copy-start | bytes 388
  0.7 88.1 %copy-start.1 = (f32[3,5120]{1,0:T(4,128)S(1)}, f32[3,5120]{1,0:T(4,128)}, u32[]{:S(2)}) copy-start(f32[3,5120]{1,0:T(4,128)} %param.7) | copy-start | bytes 184324
  0.7 88.1 %copy-start.2 = (f32[3,5120]{1,0:T(4,128)S(1)}, f32[3,5120]{1,0:T(4,128)}, u32[]{:S(2)}) copy-start(f32[3,5120]{1,0:T(4,128)} %param.8) | copy-start | bytes 184324
  2.4 86.4 %copy-start.3 = (f32[3,5120]{1,0:T(4,128)S(1)}, f32[3,5120]{1,0:T(4,128)}, u32[]{:S(2)}) copy-start(f32[3,5120]{1,0:T(4,128)} %param.9) | copy-start | bytes 184324
where the time goes:
time: 135 us; the launch traced here: 134 us
  blocking collectives  123 us (91%)
  matrix products  4.83 us (4%)
  local copies, waits for them, and re-layouts  4.73 us (4%)
  between operations  1.38 us (1%)
    unnamed x1, blocking collectives  74.3 us
    all_gather x1, blocking collectives, local(): lax.all_gather(master_new.astype(jnp.bfloat16), 'shard', axis=0, tiled=True)  20.7 us
    all_gather x1, blocking collectives, local(): lax.all_gather(weights, 'shard', axis=0, tiled=True)  19.2 us
    psum x1, blocking collectives, local(): lax.psum(partial_rows.astype(jnp.bfloat16), 'rep').astype(jnp.float32)  8.49 us
    unnamed x13, local copies, waits for them, and re-layouts  4.69 us

commit v1 on v0

v1 whole, which is shorter than its diff:
```python
import functools
import math

import jax
import jax.numpy as jnp
from jax import lax
from jax.experimental import pallas as pl
from jax.experimental.pallas import tpu as pltpu
from jax.sharding import Mesh, PartitionSpec as P

F32 = jnp.float32
BF16 = jnp.bfloat16
VMEM = pl.BlockSpec(memory_space=pltpu.VMEM)
CORES = 2
LOW = 2
COT_COPIES = 4
OUT_COPIES = 5
MAIN = 3 * 10**9
CHIPS = ("rep", "high", "low")


def call(body, outs, name, ins, cost=1_000_000, **more):
    more = {"in_specs": [VMEM] * len(ins), "out_specs": (VMEM,) * len(outs), **more}
    return pl.pallas_call(
        body,
        out_shape=tuple(jax.ShapeDtypeStruct(*out) for out in outs),
        name=name,
        cost_estimate=pl.CostEstimate(flops=cost, bytes_accessed=1_000_000, transcendentals=0),
        compiler_params=pltpu.CompilerParams(vmem_limit_bytes=16 * 2**20),
        **more,
    )(*ins)


def parity(bits, chips):
    total = 0
    for i in range(chips.bit_length() - 1):
        total = total ^ ((bits >> i) & 1)
    return total


def swap(value, rep, chip, core=0):
    chips = lax.axis_size("high") * LOW
    bits = (rep * chips + chip) * CORES + (core ^ parity(chip, chips))
    count = lax.axis_size("rep") * chips * CORES
    return lax.ppermute(value, (*CHIPS, "core"), [(i, i ^ bits) for i in range(count)])


def one_hot(rows, per, high):
    at = lax.broadcasted_iota(jnp.int32, (rows, rows), 0)
    block = jnp.floor((at.astype(F32) + 0.5) * (1.0 / per)).astype(jnp.int32)
    chips = high * LOW
    low, here = lax.axis_index("low"), lax.axis_index("high")
    last = high.bit_length() - 2
    far = (block & 1) << last
    for i in range(last):
        far = far | ((((block >> (last - i)) & 1) ^ ((here >> i) & 1)) << i)
    chip = far * LOW + (low ^ ((block & (chips - 1)) // high))
    other = parity(chip ^ (here * LOW + low), chips)
    core = lax.axis_index("core") ^ (block // chips) ^ other
    source = (chip * CORES + core) * per + at - block * per
    return (lax.broadcasted_iota(jnp.int32, (rows, rows), 1) == source).astype(BF16)


def dot(a, b, ca, cb):
    return lax.dot_general(a, b, (((ca,), (cb,)), ((), ())), preferred_element_type=F32)


def columns(dx, width):
    return pl.ds(pl.multiple_of((lax.axis_index("rep") ^ dx) * width, 128), width)


def folds(rows, width):
    some = [f for f in range(1, 9) if width % (128 * f) == 0]
    return min(some, key=lambda f: (-(-rows * f // 8) * 8 * (width // f), f))


def folded(rows, width):
    f = folds(rows, width)
    return (rows * f, width // f)


def fold(value):
    f = folds(*value.shape)
    width = value.shape[1] // f
    return jnp.concatenate([value[:, i * width : (i + 1) * width] for i in range(f)], axis=0)


def unfold(value, rows):
    f = value.shape[0] // rows
    return jnp.concatenate([value[i * rows : (i + 1) * rows] for i in range(f)], axis=1)


def partial_body(per, high, hid_hbm, cot_hbm, keep_ref, send_ref, cot_ref, hid, sems):
    rows, width = hid.shape[0], cot_ref.shape[1]
    tile = width // COT_COPIES
    pieces = [(hid_hbm, hid)]
    pieces += [
        (cot_hbm.at[:, pl.ds(i * tile, tile)], cot_ref.at[:, pl.ds(i * tile, tile)])
        for i in range(COT_COPIES)
    ]
    copies = [pltpu.make_async_copy(a, b, sems.at[i]) for i, (a, b) in enumerate(pieces)]
    for copy in copies:
        copy.start()
    move = one_hot(rows, per, high)
    copies[0].wait()
    moved = dot(move, hid[...], 1, 0).astype(BF16)
    for i in range(COT_COPIES):
        copies[1 + i].wait()
        cols = pl.ds(i * tile, tile)
        g = dot(moved, cot_ref[:, cols], 1, 0)
        keep_ref[:, cols] = g[: rows // 2]
        send_ref[:, cols] = g[rows // 2 :].astype(BF16)


def middle_body(reps, near, keep_ref, recv_ref, master, moment, second, *outs):
    *outs, state_ref = outs
    width = keep_ref.shape[1] // reps
    rows = keep_ref.shape[0] // LOW
    for dx in range(reps):
        cols = columns(dx, width)
        total = keep_ref[:, cols] + recv_ref[:, cols].astype(F32)
        for low in range(LOW):
            piece = total[low * rows : (low + 1) * rows]
            out = outs[near.index((dx, low))]
            out[...] = (fold(piece) if dx or low else piece).astype(out.dtype)
    lines = [ref[:, columns(0, width)] for ref in (master, moment, second)]
    weights = lines[0].astype(BF16).astype(F32)
    lines[:1] = [weights, lines[0] - weights]
    lines += [master[:, columns(dx, width)] for dx in range(1, reps)]
    state_ref[...] = fold(jnp.concatenate(lines, axis=0)).astype(BF16)


def join(refs, rows):
    return jnp.concatenate([unfold(ref[...].astype(F32), rows) for ref in refs], axis=0)


def join_body(rows, mine, other, *refs):
    out = refs[-1]
    both = join([mine, other], rows)
    out[...] = (both if out.shape == both.shape else fold(both)).astype(BF16)


def add(refs):
    return sum(ref[...].astype(F32) for ref in refs)


def plane_body(count, *refs):
    ins, (keep, send) = refs[:count], refs[-2:]
    total = ins[0][...]
    for ref in ins[1:]:
        total = total + unfold(ref[...].astype(F32), total.shape[0])
    half = total.shape[0] // 2
    keep[...] = total[:half]
    send[...] = fold(total[half:]).astype(BF16)


def halve_body(mine, other, *outs):
    total = mine[...] + unfold(other[...].astype(F32), mine.shape[0])
    if len(outs) == 1:
        outs[0][...] = fold(total).astype(BF16)
    else:
        half = total.shape[0] // 2
        outs[0][...] = total[:half]
        outs[1][...] = fold(total[half:]).astype(BF16)


def is_second():
    return lax.axis_index("high") >= lax.axis_size("high") // 2


def arrange_body(reps, per, state, state_other, *refs):
    out, old = refs[-2:]
    mine, other = (unfold(ref[...].astype(F32), (reps + 3) * per) for ref in (state, state_other))
    first, second = jnp.where(is_second(), other, mine), jnp.where(is_second(), mine, other)
    lines = [
        jnp.concatenate([block[i * per : (i + 1) * per] for block in (first, second)], axis=0)
        for i in range(reps + 3)
    ]
    out[0] = lines[0] + lines[1]
    out[1] = lines[2]
    out[2] = lines[3]
    here, parts = lax.axis_index("rep"), [lines[0], *lines[4:]]
    rows = []
    for rep in range(reps):
        piece = parts[rep]
        for at in range(1, reps):
            piece = jnp.where(here == at, parts[rep ^ at], piece)
        rows.append(piece)
    old[...] = fold(jnp.concatenate(rows, axis=1)).astype(BF16)


def adam_update(master, moment, second, gradient):
    moment_new = 0.9 * moment + 0.1 * gradient
    second_new = 0.95 * second + 0.05 * gradient * gradient
    first_fix = moment_new / (1.0 - 0.9**10)
    second_fix = second_new / (1.0 - 0.95**10)
    master_new = master - 0.01 * (first_fix / (jnp.sqrt(second_fix) + 1e-08) + 0.1 * master)
    return (master_new, moment_new, second_new)


def own_body(factor, per, mine, other, state, grad_ref, new_ref):
    g = unfold(add([mine, other]), 2 * per) * factor
    g = g.astype(BF16).astype(F32)
    new_ref[...] = fold(adam_update(state[0], state[1], state[2], g)[0]).astype(BF16)
    grad_ref[...] = jnp.where(is_second(), g[per:], g[:per])


def copies_body(rows, mine, other, grad, small, large):
    new = join([mine, other], rows)
    small[...] = fold(new).astype(BF16)
    large[...] = fold(jnp.concatenate([new, grad[...]], axis=0)).astype(BF16)


def across_body(reps, near, per, *refs):
    _, *ins, grad, new, grad_out = refs
    width = new.shape[1] // reps
    rows = new.shape[0] // LOW
    for dx in range(reps):
        cols = columns(dx, width)
        held = [
            unfold(ins[near.index((dx, low))][...].astype(F32), rows + (per if dx and not low else 0))
            for low in range(LOW)
        ]
        new[:, cols] = jnp.concatenate([h[:rows] for h in held], axis=0).astype(BF16)
        grad_out[:, cols] = held[0][rows:] if dx else grad[...]


def product_body(old, old_other, cot, out):
    both = jnp.concatenate([old[...], old_other[...]], axis=0)
    out[...] = dot(both, cot[...], 1, 1)


def last_body(per, high, new, new_other, product, gradient, master, moment, second, *refs):
    outs, (out, grad, *states), sems = refs[:5], refs[5:10], refs[10]
    for ref, value in zip(states, adam_update(master[...], moment[...], second[...], gradient[...])):
        ref[...] = value
    move = one_hot(out.shape[0], per, high)
    grad[...] = dot(move, product[...].astype(BF16), 0, 0).astype(BF16)
    copies = [pltpu.make_async_copy(a, b, sems.at[i]) for i, (a, b) in enumerate(zip((grad, *states), outs[1:]))]
    for copy in copies:
        copy.start()
    tile = out.shape[1] // OUT_COPIES
    half = new.shape[0]
    for i in range(OUT_COPIES):
        cols = pl.ds(i * tile, tile)
        chunk = dot(move[:half], new[:, cols], 0, 0) + dot(move[half:], new_other[:, cols], 0, 0)
        out[:, cols] = chunk.astype(BF16)
        copies.append(pltpu.make_async_copy(out.at[:, cols], outs[0].at[:, cols], sems.at[4 + i]))
        copies[-1].start()
    for copy in copies:
        copy.wait()


def local(hidden, cotangent, master, moment, second):
    reps, high = lax.axis_size("rep"), lax.axis_size("high")
    shards = high * LOW * CORES
    per, width = master.shape
    rows, part, tokens = shards * per, width // reps, hidden.shape[0]
    block = high * per
    factor = 1.0 / math.sqrt(tokens * reps * shards)
    far = [1 << i for i in range(high.bit_length() - 1)]
    halved, last = far[:-1], far[-1]
    near = sorted(((dx, low) for dx in range(reps) for low in range(LOW)),
                  key=lambda c: (c != (0, 0), -bool(c[0]) - bool(c[1]), c))
    states = (master, moment, second)

    ins = [pltpu.with_memory_space_constraint(x, pltpu.HBM) for x in (hidden.T, cotangent)]
    keep, send, cot = call(
        functools.partial(partial_body, per, high),
        [((rows // 2, width), F32), ((rows // 2, width), BF16), (cotangent.shape, BF16)],
        "partial", ins,
        cost=2 * rows * width * tokens,
        in_specs=[pl.BlockSpec(memory_space=pltpu.HBM)] * 2,
        scratch_shapes=[pltpu.VMEM((rows, tokens), BF16), pltpu.SemaphoreType.DMA((COT_COPIES + 1,))],
    )

    recv = swap(send, 0, 0, 1)
    *pieces, state = call(
        functools.partial(middle_body, reps, near),
        [*((folded(block, part), BF16) if i else ((block, part), F32) for i in range(len(near))),
         (folded((reps + 3) * per, part), BF16)],
        "middle", [keep, recv, *states],
    )
    pieces = [pieces[0]] + [swap(p, dx, low) for p, (dx, low) in zip(pieces[1:], near[1:])]
    state_other = swap(state, 0, last * LOW)
    lines = block // 2
    body = functools.partial(plane_body, len(near))
    for bits in halved:
        keep, send = call(body, [((lines, part), F32), (folded(lines, part), BF16)], "halve", pieces)
        pieces, body, lines = [keep, swap(send, 0, bits * LOW)], halve_body, lines // 2
    (total,) = call(halve_body, [(folded(2 * per, part), BF16)], "whole", pieces)
    other = swap(total, 0, last * LOW)
    state, old = call(
        functools.partial(arrange_body, reps, per),
        [((3, 2 * per, part), F32), (folded(2 * per, width), BF16)],
        "arrange", [state, state_other, total],
    )
    grad, new = call(
        functools.partial(own_body, factor, per), [((per, part), F32), (folded(2 * per, part), BF16)],
        "own", [total, other, state], cost=MAIN,
    )

    lines = 2 * per
    for bits in reversed(halved):
        new_other = swap(new, 0, bits * LOW)
        if bits == halved[0]:
            small, large = call(
                functools.partial(copies_body, lines),
                [(folded(2 * lines, part), BF16), (folded(2 * lines + per, part), BF16)],
                "copies", [new, new_other, grad], cost=MAIN,
            )
        else:
            (new,) = call(functools.partial(join_body, lines), [(folded(2 * lines, part), BF16)],
                          "join", [new, new_other])
        lines *= 2
    lines = 2 * per
    for chip in [bits * LOW for bits in reversed(halved)] + [1]:
        old_other = swap(old, 0, chip)
        shape = (2 * lines, width) if chip == 1 else folded(2 * lines, width)
        (old,) = call(functools.partial(join_body, lines), [(shape, BF16)], "join_old",
                      [old, old_other] + ([] if chip == 1 else [grad]))
        lines *= 2
    old_other = swap(old, 0, 0, 1)
    near = [near[0], *reversed(near[1:])]
    pieces = [small] + [swap(large if dx and not low else small, dx, low) for dx, low in near[1:]]
    new, grad = call(
        functools.partial(across_body, reps, near, per),
        [((rows // 2, width), BF16), ((per, width), F32)],
        "across", [old, *pieces, grad],
    )
    new_other = swap(new, 0, 0, 1)
    (product,) = call(product_body, [((rows, tokens), F32)], "product", [old, old_other, cot],
                      cost=2 * rows * width * tokens)
    outs = [((rows, width), BF16), ((rows, tokens), BF16), *[((per, width), F32)] * 3]
    updated, input_grad, *states = call(
        functools.partial(last_body, per, high), outs,
        "last", [new, new_other, product, grad, *states],
        out_specs=(pl.BlockSpec(memory_space=pltpu.HBM),) * 5,
        scratch_shapes=[*(pltpu.VMEM(*out) for out in outs), pltpu.SemaphoreType.DMA((4 + OUT_COPIES,))],
    )
    return (input_grad.T, *states, updated)


def solution(mesh):
    reps, shards = mesh.shape["rep"], mesh.shape["shard"]
    split = Mesh(mesh.devices.reshape(reps, shards // LOW // CORES, LOW, CORES), (*CHIPS, "core"))
    by_row = P(("high", "low", "core"), None)
    by_token = P((*CHIPS, "core"), None)
    return jax.shard_map(
        local,
        mesh=split,
        in_specs=(by_token, by_token, by_row, by_row, by_row),
        out_specs=(by_token, by_row, by_row, by_row, P()),
        check_vma=False,
    )
```

time: 135 us -> 36.1 us (0.27)
  blocking collectives: 123 us -> 0 us
  starting transfers between devices: 0 us -> 19.5 us
  waiting for transfers between devices: 0 us -> 10.7 us
  Pallas kernels: 0 us -> 5.03 us
  matrix products: 4.83 us -> 0 us
  local copies, waits for them, and re-layouts: 4.73 us -> 0.01 us
    unnamed x1 -> x0, blocking collectives: 74.3 us -> none
    all_gather x2 -> x0, blocking collectives: 39.9 us -> none  [the longest x1 20.7 us: local(): lax.all_gather(master_new.astype(jnp.bfloat16), 'shard', axis=0, tiled=True)]
    ppermute x0 -> x15, starting transfers between devices: none -> 19.5 us  [swap(): lax.ppermute(value, (*CHIPS, 'core'), [(i, i ^ bits) for i in range(count)])]
    ppermute x0 -> x15, waiting for transfers between devices: none -> 10.7 us  [swap(): lax.ppermute(value, (*CHIPS, 'core'), [(i, i ^ bits) for i in range(count)])]
    psum x1 -> x0, blocking collectives: 8.49 us -> none  [local(): lax.psum(partial_rows.astype(jnp.bfloat16), 'rep').astype(jnp.float32)]
    pallas_call x0 -> x12, Pallas kernels: none -> 5.03 us  [call(): pl.pallas_call(body, out_shape=tuple((jax.ShapeDtypeStruct(*out) for out...]
    dot_general x2 -> x0, matrix products: 4.83 us -> none  [the longest x1 2.54 us: local(): lax.dot_general(cotangent, lax.all_gather(weights, 'shard', axis=0, tiled...]
    unnamed x13 -> x6, local copies, waits for them, and re-layouts: 4.69 us -> 0.01 us
  transfers between devices with their start and end apart: 0 -> 15, of which waited for: 0 -> 9; matrix products, arithmetic and copies ran while one was open for 0% -> 0% of each run, Pallas kernels for 0% -> 4%
where the time goes in v1:
time: 36.1 us; the launch traced here: 36 us
  starting transfers between devices  19.5 us (54%)
  waiting for transfers between devices  10.7 us (30%)
  Pallas kernels  5.03 us (14%)
  between operations  0.72 us (2%)
    ppermute x15, starting transfers between devices, swap(): lax.ppermute(value, (*CHIPS, 'core'), [(i, i ^ bits) for i in range(count)])  19.5 us
    ppermute x15, waiting for transfers between devices, swap(): lax.ppermute(value, (*CHIPS, 'core'), [(i, i ^ bits) for i in range(count)])  10.7 us
    pallas_call x12, Pallas kernels, call(): pl.pallas_call(body, out_shape=tuple((jax.ShapeDtypeStruct(*out) for out...  5.03 us
  transfers between devices with their start and end apart: 15, of which 9 were waited for; matrix products, arithmetic and copies ran while one was open for 0% of the time, Pallas kernels for 4%

profile of v1, /device:TPU:0, one launch (start us, length us, event | category | flops | bytes accessed | tf_op | source)
XLA Modules:
  0.0 36.0 jit_solution(14160734050835923558)
XLA Ops:
  0.7 2.2 %partial.1 = (f32[24,5120]{1,0:T(8,128)S(1)}, bf16[24,5120]{1,0:T(8,128)(2,1)S(1)}, bf16[256,5120]{1,0:T(8,128)(2,1)S(1)}) custom-call(bf16[48,256]{1,0:T(8,128)(2,1)} %bitcast.2, bf16[256,5120]{1,0:T(8,128)(2,1)} %cot_hbm.1), custom_call_target="tpu_custom_call" | custom-call | flops 125829120 | bytes 1000000 | tf_op jit(solution)/shard_map/partial/pallas_call | solution.py:24
  2.9 0.5 %collective-permute-start = (bf16[24,5120]{1,0:T(8,128)(2,1)S(1)}, bf16[24,5120]{1,0:T(8,128)(2,1)S(1)}, u32[]{:S(2)}, u32[]{:S(2)}) collective-permute-start(bf16[24,5120]{1,0:T(8,128)(2,1)S(1)} %get-tuple-element.29), channel_id=1, source_target_pairs={{0,1},{1,0},{2,3},{3,2},{4,5},{5,4},{6,7},{7,6},{8,9},{9,8},{10,11... | collective-permute-start | bytes 737288 | tf_op jit(solution)/shard_map/ppermute | solution.py:45
  3.4 1.1 %collective-permute-done.recv_ref = bf16[24,5120]{1,0:T(8,128)(2,1)S(1)} collective-permute-done((bf16[24,5120]{1,0:T(8,128)(2,1)S(1)}, bf16[24,5120]{1,0:T(8,128)(2,1)S(1)}, u32[]{:S(2)}, u32[]{:S(2)}) %collective-permute-start) | collective-permute-done | bytes 245792 | tf_op jit(solution)/shard_map/ppermute | solution.py:45
  4.5 0.1 middle.1
  4.6 3.6 %collective-permute-start.2 = (bf16[24,1280]{1,0:T(8,128)(2,1)S(1)}, bf16[24,1280]{1,0:T(8,128)(2,1)S(1)}, u32[]{:S(2)}, u32[]{:S(2)}) collective-permute-start(bf16[24,1280]{1,0:T(8,128)(2,1)S(1)} %get-tuple-element.32), channel_id=1, source_target_pairs={{0,19},{1,18},{2,17},{3,16},{4,23},{5,22},{6,21},{7,20},{8,27},{9,... | collective-permute-start | bytes 184328 | tf_op jit(solution)/shard_map/ppermute | solution.py:45
  8.3 0.5 %collective-permute-start.3 = (bf16[24,1280]{1,0:T(8,128)(2,1)S(1)}, bf16[24,1280]{1,0:T(8,128)(2,1)S(1)}, u32[]{:S(2)}, u32[]{:S(2)}) collective-permute-start(bf16[24,1280]{1,0:T(8,128)(2,1)S(1)} %get-tuple-element.33), channel_id=1, source_target_pairs={{0,3},{1,2},{2,1},{3,0},{4,7},{5,6},{6,5},{7,4},{8,11},{9,10},{10,... | collective-permute-start | bytes 184328 | tf_op jit(solution)/shard_map/ppermute | solution.py:45
  8.8 0.2 collective-permute-start.4
  8.9 2.4 %collective-permute-start.1 = (bf16[15,2560]{1,0:T(8,128)(2,1)S(1)}, bf16[15,2560]{1,0:T(8,128)(2,1)S(1)}, u32[]{:S(2)}, u32[]{:S(2)}) collective-permute-start(bf16[15,2560]{1,0:T(8,128)(2,1)S(1)} %get-tuple-element.30.state), channel_id=1, source_target_pairs={{0,9},{1,8},{2,11},{3,10},{4,13},{5,12},{6,15},{7,14},{8,1},{9,0},... | collective-permute-start | bytes 230408 | tf_op jit(solution)/shard_map/ppermute | solution.py:45
  11.4 0.8 %collective-permute-done.3.refs_2_ = bf16[24,1280]{1,0:T(8,128)(2,1)S(1)} collective-permute-done((bf16[24,1280]{1,0:T(8,128)(2,1)S(1)}, bf16[24,1280]{1,0:T(8,128)(2,1)S(1)}, u32[]{:S(2)}, u32[]{:S(2)}) %collective-permute-start.3) | collective-permute-done | bytes 61472 | tf_op jit(solution)/shard_map/ppermute | solution.py:45
  12.1 0.9 %collective-permute-done.4.refs_3_ = bf16[24,1280]{1,0:T(8,128)(2,1)S(1)} collective-permute-done((bf16[24,1280]{1,0:T(8,128)(2,1)S(1)}, bf16[24,1280]{1,0:T(8,128)(2,1)S(1)}, u32[]{:S(2)}, u32[]{:S(2)}) %collective-permute-start.4) | collective-permute-done | bytes 61472 | tf_op jit(solution)/shard_map/ppermute | solution.py:45
  13.0 1.0 %collective-permute-start.5 = (bf16[24,640]{1,0:T(8,128)(2,1)S(1)}, bf16[24,640]{1,0:T(8,128)(2,1)S(1)}, u32[]{:S(2)}, u32[]{:S(2)}) collective-permute-start(bf16[24,640]{1,0:T(8,128)(2,1)S(1)} %get-tuple-element.36), channel_id=1, source_target_pairs={{0,5},{1,4},{2,7},{3,6},{4,1},{5,0},{6,3},{7,2},{8,13},{9,12},{10,... | collective-permute-start | bytes 92168 | tf_op jit(solution)/shard_map/ppermute | solution.py:45
  14.0 2.9 %collective-permute-done.5.other = bf16[24,640]{1,0:T(8,128)(2,1)S(1)} collective-permute-done((bf16[24,640]{1,0:T(8,128)(2,1)S(1)}, bf16[24,640]{1,0:T(8,128)(2,1)S(1)}, u32[]{:S(2)}, u32[]{:S(2)}) %collective-permute-start.5) | collective-permute-done | bytes 30752 | tf_op jit(solution)/shard_map/ppermute | solution.py:45
  17.0 2.0 %collective-permute-start.7 = (bf16[24,640]{1,0:T(8,128)(2,1)S(1)}, bf16[24,640]{1,0:T(8,128)(2,1)S(1)}, u32[]{:S(2)}, u32[]{:S(2)}) collective-permute-start(bf16[24,640]{1,0:T(8,128)(2,1)S(1)} %whole.1.refs_0_.mine), channel_id=1, source_target_pairs={{0,9},{1,8},{2,11},{3,10},{4,13},{5,12},{6,15},{7,14},{8,1},{9,0},... | collective-permute-start | bytes 92168 | tf_op jit(solution)/shard_map/ppermute | solution.py:45
  19.0 0.1 arrange.1
  19.1 2.3 %collective-permute-start.6 = (bf16[24,1280]{1,0:T(8,128)(2,1)S(1)}, bf16[24,1280]{1,0:T(8,128)(2,1)S(1)}, u32[]{:S(2)}, u32[]{:S(2)}) collective-permute-start(bf16[24,1280]{1,0:T(8,128)(2,1)S(1)} %get-tuple-element.37.mine), channel_id=1, source_target_pairs={{0,5},{1,4},{2,7},{3,6},{4,1},{5,0},{6,3},{7,2},{8,13},{9,12},{10,... | collective-permute-start | bytes 184328 | tf_op jit(solution)/shard_map/ppermute | solution.py:45
  21.4 0.1 own.1
  21.5 1.8 %collective-permute-start.9 = (bf16[24,640]{1,0:T(8,128)(2,1)S(1)}, bf16[24,640]{1,0:T(8,128)(2,1)S(1)}, u32[]{:S(2)}, u32[]{:S(2)}) collective-permute-start(bf16[24,640]{1,0:T(8,128)(2,1)S(1)} %get-tuple-element.40.mine), channel_id=1, source_target_pairs={{0,5},{1,4},{2,7},{3,6},{4,1},{5,0},{6,3},{7,2},{8,13},{9,12},{10,... | collective-permute-start | bytes 92168 | tf_op jit(solution)/shard_map/ppermute | solution.py:45
  23.3 0.4 %collective-permute-done.6.other = bf16[24,1280]{1,0:T(8,128)(2,1)S(1)} collective-permute-done((bf16[24,1280]{1,0:T(8,128)(2,1)S(1)}, bf16[24,1280]{1,0:T(8,128)(2,1)S(1)}, u32[]{:S(2)}, u32[]{:S(2)}) %collective-permute-start.6) | collective-permute-done | bytes 61472 | tf_op jit(solution)/shard_map/ppermute | solution.py:45
  23.7 0.1 join_old.2.mine
  23.7 1.3 %collective-permute-start.8 = (bf16[24,2560]{1,0:T(8,128)(2,1)S(1)}, bf16[24,2560]{1,0:T(8,128)(2,1)S(1)}, u32[]{:S(2)}, u32[]{:S(2)}) collective-permute-start(bf16[24,2560]{1,0:T(8,128)(2,1)S(1)} %join_old.2.mine), channel_id=1, source_target_pairs={{0,3},{1,2},{2,1},{3,0},{4,7},{5,6},{6,5},{7,4},{8,11},{9,10},{10,... | collective-permute-start | bytes 368648 | tf_op jit(solution)/shard_map/ppermute | solution.py:45
  25.1 1.6 %collective-permute-start.10 = (bf16[15,2560]{1,0:T(8,128)(2,1)S(1)}, bf16[15,2560]{1,0:T(8,128)(2,1)S(1)}, u32[]{:S(2)}, u32[]{:S(2)}) collective-permute-start(bf16[15,2560]{1,0:T(8,128)(2,1)S(1)} %get-tuple-element.42), channel_id=1, source_target_pairs={{0,16},{1,17},{2,18},{3,19},{4,20},{5,21},{6,22},{7,23},{8,24},{9,... | collective-permute-start | bytes 230408 | tf_op jit(solution)/shard_map/ppermute | solution.py:45
  26.7 1.1 %collective-permute-start.12 = (bf16[24,1280]{1,0:T(8,128)(2,1)S(1)}, bf16[24,1280]{1,0:T(8,128)(2,1)S(1)}, u32[]{:S(2)}, u32[]{:S(2)}) collective-permute-start(bf16[24,1280]{1,0:T(8,128)(2,1)S(1)} %get-tuple-element.41.refs_1_), channel_id=1, source_target_pairs={{0,19},{1,18},{2,17},{3,16},{4,23},{5,22},{6,21},{7,20},{8,27},{9,... | collective-permute-start | bytes 184328 | tf_op jit(solution)/shard_map/ppermute | solution.py:45
  27.7 0.6 %collective-permute-start.11 = (bf16[24,1280]{1,0:T(8,128)(2,1)S(1)}, bf16[24,1280]{1,0:T(8,128)(2,1)S(1)}, u32[]{:S(2)}, u32[]{:S(2)}) collective-permute-start(bf16[24,1280]{1,0:T(8,128)(2,1)S(1)} %get-tuple-element.41.refs_1_), channel_id=1, source_target_pairs={{0,3},{1,2},{2,1},{3,0},{4,7},{5,6},{6,5},{7,4},{8,11},{9,10},{10,... | collective-permute-start | bytes 184328 | tf_op jit(solution)/shard_map/ppermute | solution.py:45
  28.4 0.8 %collective-permute-done.8.other = bf16[24,2560]{1,0:T(8,128)(2,1)S(1)} collective-permute-done((bf16[24,2560]{1,0:T(8,128)(2,1)S(1)}, bf16[24,2560]{1,0:T(8,128)(2,1)S(1)}, u32[]{:S(2)}, u32[]{:S(2)}) %collective-permute-start.8) | collective-permute-done | bytes 122912 | tf_op jit(solution)/shard_map/ppermute | solution.py:45
  29.1 0.1 join_old.3.refs_0_.old
  29.2 0.5 %collective-permute-start.14 = (bf16[24,5120]{1,0:T(8,128)(2,1)S(1)}, bf16[24,5120]{1,0:T(8,128)(2,1)S(1)}, u32[]{:S(2)}, u32[]{:S(2)}) collective-permute-start(bf16[24,5120]{1,0:T(8,128)(2,1)S(1)} %join_old.3.refs_0_.old), channel_id=1, source_target_pairs={{0,1},{1,0},{2,3},{3,2},{4,5},{5,4},{6,7},{7,6},{8,9},{9,8},{10,11... | collective-permute-start | bytes 737288 | tf_op jit(solution)/shard_map/ppermute | solution.py:45
  29.7 2.2 %collective-permute-done.12.refs_4_ = bf16[24,1280]{1,0:T(8,128)(2,1)S(1)} collective-permute-done((bf16[24,1280]{1,0:T(8,128)(2,1)S(1)}, bf16[24,1280]{1,0:T(8,128)(2,1)S(1)}, u32[]{:S(2)}, u32[]{:S(2)}) %collective-permute-start.12) | collective-permute-done | bytes 61472 | tf_op jit(solution)/shard_map/ppermute | solution.py:45
  31.9 1.1 %collective-permute-done.11.refs_3_ = bf16[24,1280]{1,0:T(8,128)(2,1)S(1)} collective-permute-done((bf16[24,1280]{1,0:T(8,128)(2,1)S(1)}, bf16[24,1280]{1,0:T(8,128)(2,1)S(1)}, u32[]{:S(2)}, u32[]{:S(2)}) %collective-permute-start.11) | collective-permute-done | bytes 61472 | tf_op jit(solution)/shard_map/ppermute | solution.py:45
  33.1 0.2 collective-permute-start.13
  33.3 0.9 %product.1 = f32[48,256]{1,0:T(8,128)S(1)} custom-call(bf16[24,5120]{1,0:T(8,128)(2,1)S(1)} %join_old.3.refs_0_.old, bf16[24,5120]{1,0:T(8,128)(2,1)S(1)} %collective-permute-done.14.old_other, bf16[256,5120]{1,0:T(8,128)(2,1)S(1)} %get-tuple-element.44.cot), custom_call_target="tpu_custom_call" | custom-call | flops 125829120 | bytes 1000000 | tf_op jit(solution)/shard_map/product/pallas_call | solution.py:24
  34.2 0.5 %collective-permute-done.13.new_other = bf16[24,5120]{1,0:T(8,128)(2,1)S(1)} collective-permute-done((bf16[24,5120]{1,0:T(8,128)(2,1)S(1)}, bf16[24,5120]{1,0:T(8,128)(2,1)S(1)}, u32[]{:S(2)}, u32[]{:S(2)}) %collective-permute-start.13) | collective-permute-done | bytes 245792 | tf_op jit(solution)/shard_map/ppermute | solution.py:45
  34.7 1.3 %last.1 = (bf16[48,5120]{1,0:T(8,128)(2,1)}, bf16[48,256]{1,0:T(8,128)(2,1)}, f32[3,5120]{1,0:T(4,128)}, f32[3,5120]{1,0:T(4,128)}, f32[3,5120]{1,0:T(4,128)}) custom-call(bf16[24,5120]{1,0:T(8,128)(2,1)S(1)} %get-tuple-element.43.new, bf16[24,5120]{1,0:T(8,128)(2,1)S(1)} %collective-permute-done.13.new_other, f32[48,256]{1,0:T(8,128)S(1)} %product.1, ...), custom_call_target="tpu_custom_call" | custom-call | flops 1000000 | bytes 1000000 | tf_op jit(solution)/shard_map/last/pallas_call | solution.py:24
  (16 shorter events, 0.2 us)
Async XLA Ops:
  0.6 3.9 %copy-start.2 = (f32[3,5120]{1,0:T(4,128)S(1)}, f32[3,5120]{1,0:T(4,128)}, u32[]{:S(2)}) copy-start(f32[3,5120]{1,0:T(4,128)} %second.3) | copy-start | bytes 184324
  0.6 3.9 %copy-start.1 = (f32[3,5120]{1,0:T(4,128)S(1)}, f32[3,5120]{1,0:T(4,128)}, u32[]{:S(2)}) copy-start(f32[3,5120]{1,0:T(4,128)} %moment.3) | copy-start | bytes 184324
  0.7 3.9 %copy-start = (f32[3,5120]{1,0:T(4,128)S(1)}, f32[3,5120]{1,0:T(4,128)}, u32[]{:S(2)}) copy-start(f32[3,5120]{1,0:T(4,128)} %master.3) | copy-start | bytes 184324
  2.9 1.7 %collective-permute-start = (bf16[24,5120]{1,0:T(8,128)(2,1)S(1)}, bf16[24,5120]{1,0:T(8,128)(2,1)S(1)}, u32[]{:S(2)}, u32[]{:S(2)}) collective-permute-start(bf16[24,5120]{1,0:T(8,128)(2,1)S(1)} %get-tuple-element.29), channel_id=1, source_target_pairs={{0,1},{1,0},{2,3},{3,2},{4,5},{5,4},{6,7},{7,6},{8,9},{9,8},{10,11... | collective-permute-start | bytes 737288 | tf_op jit(solution)/shard_map/ppermute | solution.py:45
  4.6 6.7 %collective-permute-start.2 = (bf16[24,1280]{1,0:T(8,128)(2,1)S(1)}, bf16[24,1280]{1,0:T(8,128)(2,1)S(1)}, u32[]{:S(2)}, u32[]{:S(2)}) collective-permute-start(bf16[24,1280]{1,0:T(8,128)(2,1)S(1)} %get-tuple-element.32), channel_id=1, source_target_pairs={{0,19},{1,18},{2,17},{3,16},{4,23},{5,22},{6,21},{7,20},{8,27},{9,... | collective-permute-start | bytes 184328 | tf_op jit(solution)/shard_map/ppermute | solution.py:45
  8.3 3.9 %collective-permute-start.3 = (bf16[24,1280]{1,0:T(8,128)(2,1)S(1)}, bf16[24,1280]{1,0:T(8,128)(2,1)S(1)}, u32[]{:S(2)}, u32[]{:S(2)}) collective-permute-start(bf16[24,1280]{1,0:T(8,128)(2,1)S(1)} %get-tuple-element.33), channel_id=1, source_target_pairs={{0,3},{1,2},{2,1},{3,0},{4,7},{5,6},{6,5},{7,4},{8,11},{9,10},{10,... | collective-permute-start | bytes 184328 | tf_op jit(solution)/shard_map/ppermute | solution.py:45
  8.8 4.2 %collective-permute-start.4 = (bf16[24,1280]{1,0:T(8,128)(2,1)S(1)}, bf16[24,1280]{1,0:T(8,128)(2,1)S(1)}, u32[]{:S(2)}, u32[]{:S(2)}) collective-permute-start(bf16[24,1280]{1,0:T(8,128)(2,1)S(1)} %get-tuple-element.34), channel_id=1, source_target_pairs={{0,16},{1,17},{2,18},{3,19},{4,20},{5,21},{6,22},{7,23},{8,24},{9,... | collective-permute-start | bytes 184328 | tf_op jit(solution)/shard_map/ppermute | solution.py:45
  8.9 10.1 %collective-permute-start.1 = (bf16[15,2560]{1,0:T(8,128)(2,1)S(1)}, bf16[15,2560]{1,0:T(8,128)(2,1)S(1)}, u32[]{:S(2)}, u32[]{:S(2)}) collective-permute-start(bf16[15,2560]{1,0:T(8,128)(2,1)S(1)} %get-tuple-element.30.state), channel_id=1, source_target_pairs={{0,9},{1,8},{2,11},{3,10},{4,13},{5,12},{6,15},{7,14},{8,1},{9,0},... | collective-permute-start | bytes 230408 | tf_op jit(solution)/shard_map/ppermute | solution.py:45
  13.0 3.9 %collective-permute-start.5 = (bf16[24,640]{1,0:T(8,128)(2,1)S(1)}, bf16[24,640]{1,0:T(8,128)(2,1)S(1)}, u32[]{:S(2)}, u32[]{:S(2)}) collective-permute-start(bf16[24,640]{1,0:T(8,128)(2,1)S(1)} %get-tuple-element.36), channel_id=1, source_target_pairs={{0,5},{1,4},{2,7},{3,6},{4,1},{5,0},{6,3},{7,2},{8,13},{9,12},{10,... | collective-permute-start | bytes 92168 | tf_op jit(solution)/shard_map/ppermute | solution.py:45
  17.0 4.4 %collective-permute-start.7 = (bf16[24,640]{1,0:T(8,128)(2,1)S(1)}, bf16[24,640]{1,0:T(8,128)(2,1)S(1)}, u32[]{:S(2)}, u32[]{:S(2)}) collective-permute-start(bf16[24,640]{1,0:T(8,128)(2,1)S(1)} %whole.1.refs_0_.mine), channel_id=1, source_target_pairs={{0,9},{1,8},{2,11},{3,10},{4,13},{5,12},{6,15},{7,14},{8,1},{9,0},... | collective-permute-start | bytes 92168 | tf_op jit(solution)/shard_map/ppermute | solution.py:45
  19.1 4.5 %collective-permute-start.6 = (bf16[24,1280]{1,0:T(8,128)(2,1)S(1)}, bf16[24,1280]{1,0:T(8,128)(2,1)S(1)}, u32[]{:S(2)}, u32[]{:S(2)}) collective-permute-start(bf16[24,1280]{1,0:T(8,128)(2,1)S(1)} %get-tuple-element.37.mine), channel_id=1, source_target_pairs={{0,5},{1,4},{2,7},{3,6},{4,1},{5,0},{6,3},{7,2},{8,13},{9,12},{10,... | collective-permute-start | bytes 184328 | tf_op jit(solution)/shard_map/ppermute | solution.py:45
  21.5 3.5 %collective-permute-start.9 = (bf16[24,640]{1,0:T(8,128)(2,1)S(1)}, bf16[24,640]{1,0:T(8,128)(2,1)S(1)}, u32[]{:S(2)}, u32[]{:S(2)}) collective-permute-start(bf16[24,640]{1,0:T(8,128)(2,1)S(1)} %get-tuple-element.40.mine), channel_id=1, source_target_pairs={{0,5},{1,4},{2,7},{3,6},{4,1},{5,0},{6,3},{7,2},{8,13},{9,12},{10,... | collective-permute-start | bytes 92168 | tf_op jit(solution)/shard_map/ppermute | solution.py:45
  23.7 5.4 %collective-permute-start.8 = (bf16[24,2560]{1,0:T(8,128)(2,1)S(1)}, bf16[24,2560]{1,0:T(8,128)(2,1)S(1)}, u32[]{:S(2)}, u32[]{:S(2)}) collective-permute-start(bf16[24,2560]{1,0:T(8,128)(2,1)S(1)} %join_old.2.mine), channel_id=1, source_target_pairs={{0,3},{1,2},{2,1},{3,0},{4,7},{5,6},{6,5},{7,4},{8,11},{9,10},{10,... | collective-permute-start | bytes 368648 | tf_op jit(solution)/shard_map/ppermute | solution.py:45
  25.1 7.9 %collective-permute-start.10 = (bf16[15,2560]{1,0:T(8,128)(2,1)S(1)}, bf16[15,2560]{1,0:T(8,128)(2,1)S(1)}, u32[]{:S(2)}, u32[]{:S(2)}) collective-permute-start(bf16[15,2560]{1,0:T(8,128)(2,1)S(1)} %get-tuple-element.42), channel_id=1, source_target_pairs={{0,16},{1,17},{2,18},{3,19},{4,20},{5,21},{6,22},{7,23},{8,24},{9,... | collective-permute-start | bytes 230408 | tf_op jit(solution)/shard_map/ppermute | solution.py:45
  26.7 5.3 %collective-permute-start.12 = (bf16[24,1280]{1,0:T(8,128)(2,1)S(1)}, bf16[24,1280]{1,0:T(8,128)(2,1)S(1)}, u32[]{:S(2)}, u32[]{:S(2)}) collective-permute-start(bf16[24,1280]{1,0:T(8,128)(2,1)S(1)} %get-tuple-element.41.refs_1_), channel_id=1, source_target_pairs={{0,19},{1,18},{2,17},{3,16},{4,23},{5,22},{6,21},{7,20},{8,27},{9,... | collective-permute-start | bytes 184328 | tf_op jit(solution)/shard_map/ppermute | solution.py:45
  27.7 5.3 %collective-permute-start.11 = (bf16[24,1280]{1,0:T(8,128)(2,1)S(1)}, bf16[24,1280]{1,0:T(8,128)(2,1)S(1)}, u32[]{:S(2)}, u32[]{:S(2)}) collective-permute-start(bf16[24,1280]{1,0:T(8,128)(2,1)S(1)} %get-tuple-element.41.refs_1_), channel_id=1, source_target_pairs={{0,3},{1,2},{2,1},{3,0},{4,7},{5,6},{6,5},{7,4},{8,11},{9,10},{10,... | collective-permute-start | bytes 184328 | tf_op jit(solution)/shard_map/ppermute | solution.py:45
  29.2 4.1 %collective-permute-start.14 = (bf16[24,5120]{1,0:T(8,128)(2,1)S(1)}, bf16[24,5120]{1,0:T(8,128)(2,1)S(1)}, u32[]{:S(2)}, u32[]{:S(2)}) collective-permute-start(bf16[24,5120]{1,0:T(8,128)(2,1)S(1)} %join_old.3.refs_0_.old), channel_id=1, source_target_pairs={{0,1},{1,0},{2,3},{3,2},{4,5},{5,4},{6,7},{7,6},{8,9},{9,8},{10,11... | collective-permute-start | bytes 737288 | tf_op jit(solution)/shard_map/ppermute | solution.py:45
  33.1 1.6 %collective-permute-start.13 = (bf16[24,5120]{1,0:T(8,128)(2,1)S(1)}, bf16[24,5120]{1,0:T(8,128)(2,1)S(1)}, u32[]{:S(2)}, u32[]{:S(2)}) collective-permute-start(bf16[24,5120]{1,0:T(8,128)(2,1)S(1)} %get-tuple-element.43.new), channel_id=1, source_target_pairs={{0,1},{1,0},{2,3},{3,2},{4,5},{5,4},{6,7},{7,6},{8,9},{9,8},{10,11... | collective-permute-start | bytes 737288 | tf_op jit(solution)/shard_map/ppermute | solution.py:45

commit v2 on v1

--- a/solution.py
+++ b/solution.py
@@ -13,7 +13,7 @@
 VMEM = pl.BlockSpec(memory_space=pltpu.VMEM)
 CORES = 2
 LOW = 2
-COT_COPIES = 4
+COT_COPIES = 2
 OUT_COPIES = 5
 MAIN = 3 * 10**9
 CHIPS = ("rep", "high", "low")
@@ -202,27 +202,21 @@
     g = unfold(add([mine, other]), 2 * per) * factor
     g = g.astype(BF16).astype(F32)
     new_ref[...] = fold(adam_update(state[0], state[1], state[2], g)[0]).astype(BF16)
-    grad_ref[...] = jnp.where(is_second(), g[per:], g[:per])
-
-
-def copies_body(rows, mine, other, grad, small, large):
-    new = join([mine, other], rows)
-    small[...] = fold(new).astype(BF16)
-    large[...] = fold(jnp.concatenate([new, grad[...]], axis=0)).astype(BF16)
-
-
-def across_body(reps, near, per, *refs):
-    _, *ins, grad, new, grad_out = refs
+    grad_ref[...] = jnp.where(is_second(), g[per:], g[:per]).astype(BF16)
+
+
+def across_body(reps, near, *refs):
+    *ins, new = refs[-len(near) - 1 :]
     width = new.shape[1] // reps
-    rows = new.shape[0] // LOW
     for dx in range(reps):
-        cols = columns(dx, width)
-        held = [
-            unfold(ins[near.index((dx, low))][...].astype(F32), rows + (per if dx and not low else 0))
-            for low in range(LOW)
-        ]
-        new[:, cols] = jnp.concatenate([h[:rows] for h in held], axis=0).astype(BF16)
-        grad_out[:, cols] = held[0][rows:] if dx else grad[...]
+        pieces = [ins[near.index((dx, low))] for low in range(LOW)]
+        new[:, columns(dx, width)] = join(pieces, new.shape[0] // LOW).astype(BF16)
+
+
+def wide_body(*refs):
+    *ins, out = refs
+    for dx, ref in enumerate(ins):
+        out[:, columns(dx, ref.shape[1])] = ref[...].astype(F32)
 
 
 def product_body(old, old_other, cot, out):
@@ -296,23 +290,16 @@
         "arrange", [state, state_other, total],
     )
     grad, new = call(
-        functools.partial(own_body, factor, per), [((per, part), F32), (folded(2 * per, part), BF16)],
+        functools.partial(own_body, factor, per), [((per, part), BF16), (folded(2 * per, part), BF16)],
         "own", [total, other, state], cost=MAIN,
     )
 
     lines = 2 * per
     for bits in reversed(halved):
-        new_other = swap(new, 0, bits * LOW)
-        if bits == halved[0]:
-            small, large = call(
-                functools.partial(copies_body, lines),
-                [(folded(2 * lines, part), BF16), (folded(2 * lines + per, part), BF16)],
-                "copies", [new, new_other, grad], cost=MAIN,
-            )
-        else:
-            (new,) = call(functools.partial(join_body, lines), [(folded(2 * lines, part), BF16)],
-                          "join", [new, new_other])
+        body = functools.partial(join_body, lines)
         lines *= 2
+        (new,) = call(body, [(folded(lines, part), BF16)], "copies", [new, swap(new, 0, bits * LOW)], cost=MAIN)
+    grads = [grad] + [swap(grad, dx, 0) for dx in range(1, reps)]
     lines = 2 * per
     for chip in [bits * LOW for bits in reversed(halved)] + [1]:
         old_other = swap(old, 0, chip)
@@ -322,15 +309,13 @@
         lines *= 2
     old_other = swap(old, 0, 0, 1)
     near = [near[0], *reversed(near[1:])]
-    pieces = [small] + [swap(large if dx and not low else small, dx, low) for dx, low in near[1:]]
-    new, grad = call(
-        functools.partial(across_body, reps, near, per),
-        [((rows // 2, width), BF16), ((per, width), F32)],
-        "across", [old, *pieces, grad],
-    )
+    pieces = [swap(new, *c) if any(c) else new for c in near]
+    (new,) = call(functools.partial(across_body, reps, near), [((rows // 2, width), BF16)],
+                  "across", [old, *pieces])
     new_other = swap(new, 0, 0, 1)
     (product,) = call(product_body, [((rows, tokens), F32)], "product", [old, old_other, cot],
                       cost=2 * rows * width * tokens)
+    (grad,) = call(wide_body, [((per, width), F32)], "gradient", grads, cost=MAIN)
     outs = [((rows, width), BF16), ((rows, tokens), BF16), *[((per, width), F32)] * 3]
     updated, input_grad, *states = call(
         functools.partial(last_body, per, high), outs,

time: 36.1 us -> 35.4 us (0.981)
  waiting for transfers between devices: 10.7 us -> 7.78 us
  starting transfers between devices: 19.5 us -> 21.7 us
    ppermute x15 -> x16, waiting for transfers between devices: 10.7 us -> 7.78 us  [swap(): lax.ppermute(value, (*CHIPS, 'core'), [(i, i ^ bits) for i in range(count)])]
    ppermute x15 -> x16, starting transfers between devices: 19.5 us -> 21.7 us  [swap(): lax.ppermute(value, (*CHIPS, 'core'), [(i, i ^ bits) for i in range(count)])]
    pallas_call x12 -> x13, Pallas kernels: 5.03 us -> 4.96 us  [call(): pl.pallas_call(body, out_shape=tuple((jax.ShapeDtypeStruct(*out) for out...]
  transfers between devices with their start and end apart: 15 -> 16, of which waited for: 9 -> 9; matrix products, arithmetic and copies ran while one was open for 0% -> 0% of each run, Pallas kernels for 4% -> 4%
where the time goes in v2:
time: 35.4 us; the launch traced here: 35.2 us
  starting transfers between devices  21.7 us (61%)
  waiting for transfers between devices  7.78 us (22%)
  Pallas kernels  4.96 us (14%)
  between operations  0.74 us (2%)
    ppermute x16, starting transfers between devices, swap(): lax.ppermute(value, (*CHIPS, 'core'), [(i, i ^ bits) for i in range(count)])  21.7 us
    ppermute x16, waiting for transfers between devices, swap(): lax.ppermute(value, (*CHIPS, 'core'), [(i, i ^ bits) for i in range(count)])  7.78 us
    pallas_call x13, Pallas kernels, call(): pl.pallas_call(body, out_shape=tuple((jax.ShapeDtypeStruct(*out) for out...  4.96 us
  transfers between devices with their start and end apart: 16, of which 9 were waited for; matrix products, arithmetic and copies ran while one was open for 0% of the time, Pallas kernels for 4%

profile of v2, /device:TPU:0, one launch (start us, length us, event | category | flops | bytes accessed | tf_op | source)
XLA Modules:
  0.0 35.2 jit_solution(14251244313729045115)
XLA Ops:
  0.7 2.1 %partial.1 = (f32[24,5120]{1,0:T(8,128)S(1)}, bf16[24,5120]{1,0:T(8,128)(2,1)S(1)}, bf16[256,5120]{1,0:T(8,128)(2,1)S(1)}) custom-call(bf16[48,256]{1,0:T(8,128)(2,1)} %bitcast.2, bf16[256,5120]{1,0:T(8,128)(2,1)} %cot_hbm.1), custom_call_target="tpu_custom_call" | custom-call | flops 125829120 | bytes 1000000 | tf_op jit(solution)/shard_map/partial/pallas_call | solution.py:24
  2.8 0.5 %collective-permute-start = (bf16[24,5120]{1,0:T(8,128)(2,1)S(1)}, bf16[24,5120]{1,0:T(8,128)(2,1)S(1)}, u32[]{:S(2)}, u32[]{:S(2)}) collective-permute-start(bf16[24,5120]{1,0:T(8,128)(2,1)S(1)} %get-tuple-element.25), channel_id=1, source_target_pairs={{0,1},{1,0},{2,3},{3,2},{4,5},{5,4},{6,7},{7,6},{8,9},{9,8},{10,11... | collective-permute-start | bytes 737288 | tf_op jit(solution)/shard_map/ppermute | solution.py:45
  3.3 1.1 %collective-permute-done.recv_ref = bf16[24,5120]{1,0:T(8,128)(2,1)S(1)} collective-permute-done((bf16[24,5120]{1,0:T(8,128)(2,1)S(1)}, bf16[24,5120]{1,0:T(8,128)(2,1)S(1)}, u32[]{:S(2)}, u32[]{:S(2)}) %collective-permute-start) | collective-permute-done | bytes 245792 | tf_op jit(solution)/shard_map/ppermute | solution.py:45
  4.5 0.1 middle.1
  4.6 3.6 %collective-permute-start.2 = (bf16[24,1280]{1,0:T(8,128)(2,1)S(1)}, bf16[24,1280]{1,0:T(8,128)(2,1)S(1)}, u32[]{:S(2)}, u32[]{:S(2)}) collective-permute-start(bf16[24,1280]{1,0:T(8,128)(2,1)S(1)} %get-tuple-element.28), channel_id=1, source_target_pairs={{0,19},{1,18},{2,17},{3,16},{4,23},{5,22},{6,21},{7,20},{8,27},{9,... | collective-permute-start | bytes 184328 | tf_op jit(solution)/shard_map/ppermute | solution.py:45
  8.2 0.5 %collective-permute-start.3 = (bf16[24,1280]{1,0:T(8,128)(2,1)S(1)}, bf16[24,1280]{1,0:T(8,128)(2,1)S(1)}, u32[]{:S(2)}, u32[]{:S(2)}) collective-permute-start(bf16[24,1280]{1,0:T(8,128)(2,1)S(1)} %get-tuple-element.29), channel_id=1, source_target_pairs={{0,3},{1,2},{2,1},{3,0},{4,7},{5,6},{6,5},{7,4},{8,11},{9,10},{10,... | collective-permute-start | bytes 184328 | tf_op jit(solution)/shard_map/ppermute | solution.py:45
  8.7 0.2 collective-permute-start.4
  8.9 2.4 %collective-permute-start.1 = (bf16[15,2560]{1,0:T(8,128)(2,1)S(1)}, bf16[15,2560]{1,0:T(8,128)(2,1)S(1)}, u32[]{:S(2)}, u32[]{:S(2)}) collective-permute-start(bf16[15,2560]{1,0:T(8,128)(2,1)S(1)} %get-tuple-element.26.state), channel_id=1, source_target_pairs={{0,9},{1,8},{2,11},{3,10},{4,13},{5,12},{6,15},{7,14},{8,1},{9,0},... | collective-permute-start | bytes 230408 | tf_op jit(solution)/shard_map/ppermute | solution.py:45
  11.3 0.8 %collective-permute-done.3.refs_2_ = bf16[24,1280]{1,0:T(8,128)(2,1)S(1)} collective-permute-done((bf16[24,1280]{1,0:T(8,128)(2,1)S(1)}, bf16[24,1280]{1,0:T(8,128)(2,1)S(1)}, u32[]{:S(2)}, u32[]{:S(2)}) %collective-permute-start.3) | collective-permute-done | bytes 61472 | tf_op jit(solution)/shard_map/ppermute | solution.py:45
  12.1 0.9 %collective-permute-done.4.refs_3_ = bf16[24,1280]{1,0:T(8,128)(2,1)S(1)} collective-permute-done((bf16[24,1280]{1,0:T(8,128)(2,1)S(1)}, bf16[24,1280]{1,0:T(8,128)(2,1)S(1)}, u32[]{:S(2)}, u32[]{:S(2)}) %collective-permute-start.4) | collective-permute-done | bytes 61472 | tf_op jit(solution)/shard_map/ppermute | solution.py:45
  13.0 1.0 %collective-permute-start.5 = (bf16[24,640]{1,0:T(8,128)(2,1)S(1)}, bf16[24,640]{1,0:T(8,128)(2,1)S(1)}, u32[]{:S(2)}, u32[]{:S(2)}) collective-permute-start(bf16[24,640]{1,0:T(8,128)(2,1)S(1)} %get-tuple-element.32), channel_id=1, source_target_pairs={{0,5},{1,4},{2,7},{3,6},{4,1},{5,0},{6,3},{7,2},{8,13},{9,12},{10,... | collective-permute-start | bytes 92168 | tf_op jit(solution)/shard_map/ppermute | solution.py:45
  14.0 2.9 %collective-permute-done.5.other = bf16[24,640]{1,0:T(8,128)(2,1)S(1)} collective-permute-done((bf16[24,640]{1,0:T(8,128)(2,1)S(1)}, bf16[24,640]{1,0:T(8,128)(2,1)S(1)}, u32[]{:S(2)}, u32[]{:S(2)}) %collective-permute-start.5) | collective-permute-done | bytes 30752 | tf_op jit(solution)/shard_map/ppermute | solution.py:45
  16.9 2.0 %collective-permute-start.7 = (bf16[24,640]{1,0:T(8,128)(2,1)S(1)}, bf16[24,640]{1,0:T(8,128)(2,1)S(1)}, u32[]{:S(2)}, u32[]{:S(2)}) collective-permute-start(bf16[24,640]{1,0:T(8,128)(2,1)S(1)} %whole.1.refs_0_.mine), channel_id=1, source_target_pairs={{0,9},{1,8},{2,11},{3,10},{4,13},{5,12},{6,15},{7,14},{8,1},{9,0},... | collective-permute-start | bytes 92168 | tf_op jit(solution)/shard_map/ppermute | solution.py:45
  19.0 0.1 arrange.1
  19.1 2.3 %collective-permute-start.6 = (bf16[24,1280]{1,0:T(8,128)(2,1)S(1)}, bf16[24,1280]{1,0:T(8,128)(2,1)S(1)}, u32[]{:S(2)}, u32[]{:S(2)}) collective-permute-start(bf16[24,1280]{1,0:T(8,128)(2,1)S(1)} %get-tuple-element.33.mine), channel_id=1, source_target_pairs={{0,5},{1,4},{2,7},{3,6},{4,1},{5,0},{6,3},{7,2},{8,13},{9,12},{10,... | collective-permute-start | bytes 184328 | tf_op jit(solution)/shard_map/ppermute | solution.py:45
  21.4 0.1 own.1
  21.5 1.8 %collective-permute-start.9 = (bf16[24,640]{1,0:T(8,128)(2,1)S(1)}, bf16[24,640]{1,0:T(8,128)(2,1)S(1)}, u32[]{:S(2)}, u32[]{:S(2)}) collective-permute-start(bf16[24,640]{1,0:T(8,128)(2,1)S(1)} %get-tuple-element.36.mine), channel_id=1, source_target_pairs={{0,5},{1,4},{2,7},{3,6},{4,1},{5,0},{6,3},{7,2},{8,13},{9,12},{10,... | collective-permute-start | bytes 92168 | tf_op jit(solution)/shard_map/ppermute | solution.py:45
  23.2 0.4 %collective-permute-done.6.other = bf16[24,1280]{1,0:T(8,128)(2,1)S(1)} collective-permute-done((bf16[24,1280]{1,0:T(8,128)(2,1)S(1)}, bf16[24,1280]{1,0:T(8,128)(2,1)S(1)}, u32[]{:S(2)}, u32[]{:S(2)}) %collective-permute-start.6) | collective-permute-done | bytes 61472 | tf_op jit(solution)/shard_map/ppermute | solution.py:45
  23.7 1.3 %collective-permute-start.8 = (bf16[24,2560]{1,0:T(8,128)(2,1)S(1)}, bf16[24,2560]{1,0:T(8,128)(2,1)S(1)}, u32[]{:S(2)}, u32[]{:S(2)}) collective-permute-start(bf16[24,2560]{1,0:T(8,128)(2,1)S(1)} %join_old.2.mine), channel_id=1, source_target_pairs={{0,3},{1,2},{2,1},{3,0},{4,7},{5,6},{6,5},{7,4},{8,11},{9,10},{10,... | collective-permute-start | bytes 368648 | tf_op jit(solution)/shard_map/ppermute | solution.py:45
  25.0 2.2 %collective-permute-start.12 = (bf16[24,1280]{1,0:T(8,128)(2,1)S(1)}, bf16[24,1280]{1,0:T(8,128)(2,1)S(1)}, u32[]{:S(2)}, u32[]{:S(2)}) collective-permute-start(bf16[24,1280]{1,0:T(8,128)(2,1)S(1)} %copies.1.refs_1_), channel_id=1, source_target_pairs={{0,19},{1,18},{2,17},{3,16},{4,23},{5,22},{6,21},{7,20},{8,27},{9,... | collective-permute-start | bytes 184328 | tf_op jit(solution)/shard_map/ppermute | solution.py:45
  27.2 0.6 %collective-permute-start.11 = (bf16[24,1280]{1,0:T(8,128)(2,1)S(1)}, bf16[24,1280]{1,0:T(8,128)(2,1)S(1)}, u32[]{:S(2)}, u32[]{:S(2)}) collective-permute-start(bf16[24,1280]{1,0:T(8,128)(2,1)S(1)} %copies.1.refs_1_), channel_id=1, source_target_pairs={{0,3},{1,2},{2,1},{3,0},{4,7},{5,6},{6,5},{7,4},{8,11},{9,10},{10,... | collective-permute-start | bytes 184328 | tf_op jit(solution)/shard_map/ppermute | solution.py:45
  27.8 0.5 %collective-permute-start.10 = (bf16[24,1280]{1,0:T(8,128)(2,1)S(1)}, bf16[24,1280]{1,0:T(8,128)(2,1)S(1)}, u32[]{:S(2)}, u32[]{:S(2)}) collective-permute-start(bf16[24,1280]{1,0:T(8,128)(2,1)S(1)} %copies.1.refs_1_), channel_id=1, source_target_pairs={{0,16},{1,17},{2,18},{3,19},{4,20},{5,21},{6,22},{7,23},{8,24},{9,... | collective-permute-start | bytes 184328 | tf_op jit(solution)/shard_map/ppermute | solution.py:45
  28.3 1.5 %collective-permute-start.15 = (bf16[3,2560]{1,0:T(4,128)(2,1)S(1)}, bf16[3,2560]{1,0:T(4,128)(2,1)S(1)}, u32[]{:S(2)}, u32[]{:S(2)}) collective-permute-start(bf16[3,2560]{1,0:T(4,128)(2,1)S(1)} %get-tuple-element.35.refs_0_), channel_id=1, source_target_pairs={{0,16},{1,17},{2,18},{3,19},{4,20},{5,21},{6,22},{7,23},{8,24},{9,... | collective-permute-start | bytes 46088 | tf_op jit(solution)/shard_map/ppermute | solution.py:45
  29.8 0.1 join_old.3.refs_0_.old
  29.9 1.3 %collective-permute-start.14 = (bf16[24,5120]{1,0:T(8,128)(2,1)S(1)}, bf16[24,5120]{1,0:T(8,128)(2,1)S(1)}, u32[]{:S(2)}, u32[]{:S(2)}) collective-permute-start(bf16[24,5120]{1,0:T(8,128)(2,1)S(1)} %join_old.3.refs_0_.old), channel_id=1, source_target_pairs={{0,1},{1,0},{2,3},{3,2},{4,5},{5,4},{6,7},{7,6},{8,9},{9,8},{10,11... | collective-permute-start | bytes 737288 | tf_op jit(solution)/shard_map/ppermute | solution.py:45
  31.2 0.6 %collective-permute-done.11.refs_3_ = bf16[24,1280]{1,0:T(8,128)(2,1)S(1)} collective-permute-done((bf16[24,1280]{1,0:T(8,128)(2,1)S(1)}, bf16[24,1280]{1,0:T(8,128)(2,1)S(1)}, u32[]{:S(2)}, u32[]{:S(2)}) %collective-permute-start.11) | collective-permute-done | bytes 61472 | tf_op jit(solution)/shard_map/ppermute | solution.py:45
  31.8 0.5 %collective-permute-done.10.refs_2_ = bf16[24,1280]{1,0:T(8,128)(2,1)S(1)} collective-permute-done((bf16[24,1280]{1,0:T(8,128)(2,1)S(1)}, bf16[24,1280]{1,0:T(8,128)(2,1)S(1)}, u32[]{:S(2)}, u32[]{:S(2)}) %collective-permute-start.10) | collective-permute-done | bytes 61472 | tf_op jit(solution)/shard_map/ppermute | solution.py:45
  32.3 0.1 collective-permute-start.13
  32.4 0.1 collective-permute-done.15.refs_1_
  32.5 0.9 %product.1 = f32[48,256]{1,0:T(8,128)S(1)} custom-call(bf16[24,5120]{1,0:T(8,128)(2,1)S(1)} %join_old.3.refs_0_.old, bf16[24,5120]{1,0:T(8,128)(2,1)S(1)} %collective-permute-done.14.old_other, bf16[256,5120]{1,0:T(8,128)(2,1)S(1)} %get-tuple-element.37.cot), custom_call_target="tpu_custom_call" | custom-call | flops 125829120 | bytes 1000000 | tf_op jit(solution)/shard_map/product/pallas_call | solution.py:24
  33.4 0.5 %collective-permute-done.13.new_other = bf16[24,5120]{1,0:T(8,128)(2,1)S(1)} collective-permute-done((bf16[24,5120]{1,0:T(8,128)(2,1)S(1)}, bf16[24,5120]{1,0:T(8,128)(2,1)S(1)}, u32[]{:S(2)}, u32[]{:S(2)}) %collective-permute-start.13) | collective-permute-done | bytes 245792 | tf_op jit(solution)/shard_map/ppermute | solution.py:45
  33.9 1.3 %last.1 = (bf16[48,5120]{1,0:T(8,128)(2,1)}, bf16[48,256]{1,0:T(8,128)(2,1)}, f32[3,5120]{1,0:T(4,128)}, f32[3,5120]{1,0:T(4,128)}, f32[3,5120]{1,0:T(4,128)}) custom-call(bf16[24,5120]{1,0:T(8,128)(2,1)S(1)} %across.1.new, bf16[24,5120]{1,0:T(8,128)(2,1)S(1)} %collective-permute-done.13.new_other, f32[48,256]{1,0:T(8,128)S(1)} %product.1, ...), custom_call_target="tpu_custom_call" | custom-call | flops 1000000 | bytes 1000000 | tf_op jit(solution)/shard_map/last/pallas_call | solution.py:24
  (19 shorter events, 0.3 us)
Async XLA Ops:
  0.6 3.8 %copy-start.2 = (f32[3,5120]{1,0:T(4,128)S(1)}, f32[3,5120]{1,0:T(4,128)}, u32[]{:S(2)}) copy-start(f32[3,5120]{1,0:T(4,128)} %second.3) | copy-start | bytes 184324
  0.6 3.8 %copy-start.1 = (f32[3,5120]{1,0:T(4,128)S(1)}, f32[3,5120]{1,0:T(4,128)}, u32[]{:S(2)}) copy-start(f32[3,5120]{1,0:T(4,128)} %moment.3) | copy-start | bytes 184324
  0.7 3.8 %copy-start = (f32[3,5120]{1,0:T(4,128)S(1)}, f32[3,5120]{1,0:T(4,128)}, u32[]{:S(2)}) copy-start(f32[3,5120]{1,0:T(4,128)} %master.3) | copy-start | bytes 184324
  2.8 1.7 %collective-permute-start = (bf16[24,5120]{1,0:T(8,128)(2,1)S(1)}, bf16[24,5120]{1,0:T(8,128)(2,1)S(1)}, u32[]{:S(2)}, u32[]{:S(2)}) collective-permute-start(bf16[24,5120]{1,0:T(8,128)(2,1)S(1)} %get-tuple-element.25), channel_id=1, source_target_pairs={{0,1},{1,0},{2,3},{3,2},{4,5},{5,4},{6,7},{7,6},{8,9},{9,8},{10,11... | collective-permute-start | bytes 737288 | tf_op jit(solution)/shard_map/ppermute | solution.py:45
  4.6 6.7 %collective-permute-start.2 = (bf16[24,1280]{1,0:T(8,128)(2,1)S(1)}, bf16[24,1280]{1,0:T(8,128)(2,1)S(1)}, u32[]{:S(2)}, u32[]{:S(2)}) collective-permute-start(bf16[24,1280]{1,0:T(8,128)(2,1)S(1)} %get-tuple-element.28), channel_id=1, source_target_pairs={{0,19},{1,18},{2,17},{3,16},{4,23},{5,22},{6,21},{7,20},{8,27},{9,... | collective-permute-start | bytes 184328 | tf_op jit(solution)/shard_map/ppermute | solution.py:45
  8.2 3.9 %collective-permute-start.3 = (bf16[24,1280]{1,0:T(8,128)(2,1)S(1)}, bf16[24,1280]{1,0:T(8,128)(2,1)S(1)}, u32[]{:S(2)}, u32[]{:S(2)}) collective-permute-start(bf16[24,1280]{1,0:T(8,128)(2,1)S(1)} %get-tuple-element.29), channel_id=1, source_target_pairs={{0,3},{1,2},{2,1},{3,0},{4,7},{5,6},{6,5},{7,4},{8,11},{9,10},{10,... | collective-permute-start | bytes 184328 | tf_op jit(solution)/shard_map/ppermute | solution.py:45
  8.7 4.2 %collective-permute-start.4 = (bf16[24,1280]{1,0:T(8,128)(2,1)S(1)}, bf16[24,1280]{1,0:T(8,128)(2,1)S(1)}, u32[]{:S(2)}, u32[]{:S(2)}) collective-permute-start(bf16[24,1280]{1,0:T(8,128)(2,1)S(1)} %get-tuple-element.30), channel_id=1, source_target_pairs={{0,16},{1,17},{2,18},{3,19},{4,20},{5,21},{6,22},{7,23},{8,24},{9,... | collective-permute-start | bytes 184328 | tf_op jit(solution)/shard_map/ppermute | solution.py:45
  8.9 10.1 %collective-permute-start.1 = (bf16[15,2560]{1,0:T(8,128)(2,1)S(1)}, bf16[15,2560]{1,0:T(8,128)(2,1)S(1)}, u32[]{:S(2)}, u32[]{:S(2)}) collective-permute-start(bf16[15,2560]{1,0:T(8,128)(2,1)S(1)} %get-tuple-element.26.state), channel_id=1, source_target_pairs={{0,9},{1,8},{2,11},{3,10},{4,13},{5,12},{6,15},{7,14},{8,1},{9,0},... | collective-permute-start | bytes 230408 | tf_op jit(solution)/shard_map/ppermute | solution.py:45
  13.0 3.9 %collective-permute-start.5 = (bf16[24,640]{1,0:T(8,128)(2,1)S(1)}, bf16[24,640]{1,0:T(8,128)(2,1)S(1)}, u32[]{:S(2)}, u32[]{:S(2)}) collective-permute-start(bf16[24,640]{1,0:T(8,128)(2,1)S(1)} %get-tuple-element.32), channel_id=1, source_target_pairs={{0,5},{1,4},{2,7},{3,6},{4,1},{5,0},{6,3},{7,2},{8,13},{9,12},{10,... | collective-permute-start | bytes 92168 | tf_op jit(solution)/shard_map/ppermute | solution.py:45
  16.9 4.4 %collective-permute-start.7 = (bf16[24,640]{1,0:T(8,128)(2,1)S(1)}, bf16[24,640]{1,0:T(8,128)(2,1)S(1)}, u32[]{:S(2)}, u32[]{:S(2)}) collective-permute-start(bf16[24,640]{1,0:T(8,128)(2,1)S(1)} %whole.1.refs_0_.mine), channel_id=1, source_target_pairs={{0,9},{1,8},{2,11},{3,10},{4,13},{5,12},{6,15},{7,14},{8,1},{9,0},... | collective-permute-start | bytes 92168 | tf_op jit(solution)/shard_map/ppermute | solution.py:45
  19.1 4.5 %collective-permute-start.6 = (bf16[24,1280]{1,0:T(8,128)(2,1)S(1)}, bf16[24,1280]{1,0:T(8,128)(2,1)S(1)}, u32[]{:S(2)}, u32[]{:S(2)}) collective-permute-start(bf16[24,1280]{1,0:T(8,128)(2,1)S(1)} %get-tuple-element.33.mine), channel_id=1, source_target_pairs={{0,5},{1,4},{2,7},{3,6},{4,1},{5,0},{6,3},{7,2},{8,13},{9,12},{10,... | collective-permute-start | bytes 184328 | tf_op jit(solution)/shard_map/ppermute | solution.py:45
  21.5 3.5 %collective-permute-start.9 = (bf16[24,640]{1,0:T(8,128)(2,1)S(1)}, bf16[24,640]{1,0:T(8,128)(2,1)S(1)}, u32[]{:S(2)}, u32[]{:S(2)}) collective-permute-start(bf16[24,640]{1,0:T(8,128)(2,1)S(1)} %get-tuple-element.36.mine), channel_id=1, source_target_pairs={{0,5},{1,4},{2,7},{3,6},{4,1},{5,0},{6,3},{7,2},{8,13},{9,12},{10,... | collective-permute-start | bytes 92168 | tf_op jit(solution)/shard_map/ppermute | solution.py:45
  23.7 6.1 %collective-permute-start.8 = (bf16[24,2560]{1,0:T(8,128)(2,1)S(1)}, bf16[24,2560]{1,0:T(8,128)(2,1)S(1)}, u32[]{:S(2)}, u32[]{:S(2)}) collective-permute-start(bf16[24,2560]{1,0:T(8,128)(2,1)S(1)} %join_old.2.mine), channel_id=1, source_target_pairs={{0,3},{1,2},{2,1},{3,0},{4,7},{5,6},{6,5},{7,4},{8,11},{9,10},{10,... | collective-permute-start | bytes 368648 | tf_op jit(solution)/shard_map/ppermute | solution.py:45
  25.0 6.1 %collective-permute-start.12 = (bf16[24,1280]{1,0:T(8,128)(2,1)S(1)}, bf16[24,1280]{1,0:T(8,128)(2,1)S(1)}, u32[]{:S(2)}, u32[]{:S(2)}) collective-permute-start(bf16[24,1280]{1,0:T(8,128)(2,1)S(1)} %copies.1.refs_1_), channel_id=1, source_target_pairs={{0,19},{1,18},{2,17},{3,16},{4,23},{5,22},{6,21},{7,20},{8,27},{9,... | collective-permute-start | bytes 184328 | tf_op jit(solution)/shard_map/ppermute | solution.py:45
  27.2 4.6 %collective-permute-start.11 = (bf16[24,1280]{1,0:T(8,128)(2,1)S(1)}, bf16[24,1280]{1,0:T(8,128)(2,1)S(1)}, u32[]{:S(2)}, u32[]{:S(2)}) collective-permute-start(bf16[24,1280]{1,0:T(8,128)(2,1)S(1)} %copies.1.refs_1_), channel_id=1, source_target_pairs={{0,3},{1,2},{2,1},{3,0},{4,7},{5,6},{6,5},{7,4},{8,11},{9,10},{10,... | collective-permute-start | bytes 184328 | tf_op jit(solution)/shard_map/ppermute | solution.py:45
  27.8 4.5 %collective-permute-start.10 = (bf16[24,1280]{1,0:T(8,128)(2,1)S(1)}, bf16[24,1280]{1,0:T(8,128)(2,1)S(1)}, u32[]{:S(2)}, u32[]{:S(2)}) collective-permute-start(bf16[24,1280]{1,0:T(8,128)(2,1)S(1)} %copies.1.refs_1_), channel_id=1, source_target_pairs={{0,16},{1,17},{2,18},{3,19},{4,20},{5,21},{6,22},{7,23},{8,24},{9,... | collective-permute-start | bytes 184328 | tf_op jit(solution)/shard_map/ppermute | solution.py:45
  28.3 4.2 %collective-permute-start.15 = (bf16[3,2560]{1,0:T(4,128)(2,1)S(1)}, bf16[3,2560]{1,0:T(4,128)(2,1)S(1)}, u32[]{:S(2)}, u32[]{:S(2)}) collective-permute-start(bf16[3,2560]{1,0:T(4,128)(2,1)S(1)} %get-tuple-element.35.refs_0_), channel_id=1, source_target_pairs={{0,16},{1,17},{2,18},{3,19},{4,20},{5,21},{6,22},{7,23},{8,24},{9,... | collective-permute-start | bytes 46088 | tf_op jit(solution)/shard_map/ppermute | solution.py:45
  29.9 2.6 %collective-permute-start.14 = (bf16[24,5120]{1,0:T(8,128)(2,1)S(1)}, bf16[24,5120]{1,0:T(8,128)(2,1)S(1)}, u32[]{:S(2)}, u32[]{:S(2)}) collective-permute-start(bf16[24,5120]{1,0:T(8,128)(2,1)S(1)} %join_old.3.refs_0_.old), channel_id=1, source_target_pairs={{0,1},{1,0},{2,3},{3,2},{4,5},{5,4},{6,7},{7,6},{8,9},{9,8},{10,11... | collective-permute-start | bytes 737288 | tf_op jit(solution)/shard_map/ppermute | solution.py:45
  32.3 1.6 %collective-permute-start.13 = (bf16[24,5120]{1,0:T(8,128)(2,1)S(1)}, bf16[24,5120]{1,0:T(8,128)(2,1)S(1)}, u32[]{:S(2)}, u32[]{:S(2)}) collective-permute-start(bf16[24,5120]{1,0:T(8,128)(2,1)S(1)} %across.1.new), channel_id=1, source_target_pairs={{0,1},{1,0},{2,3},{3,2},{4,5},{5,4},{6,7},{7,6},{8,9},{9,8},{10,11... | collective-permute-start | bytes 737288 | tf_op jit(solution)/shard_map/ppermute | solution.py:45

commit v3 on v2

--- a/solution.py
+++ b/solution.py
@@ -219,20 +219,20 @@
         out[:, columns(dx, ref.shape[1])] = ref[...].astype(F32)
 
 
-def product_body(old, old_other, cot, out):
+def product_body(per, high, old, old_other, cot, gradient, master, moment, second, grad, *states):
     both = jnp.concatenate([old[...], old_other[...]], axis=0)
-    out[...] = dot(both, cot[...], 1, 1)
-
-
-def last_body(per, high, new, new_other, product, gradient, master, moment, second, *refs):
-    outs, (out, grad, *states), sems = refs[:5], refs[5:10], refs[10]
+    rows = dot(both, cot[...], 1, 1).astype(BF16)
     for ref, value in zip(states, adam_update(master[...], moment[...], second[...], gradient[...])):
         ref[...] = value
-    move = one_hot(out.shape[0], per, high)
-    grad[...] = dot(move, product[...].astype(BF16), 0, 0).astype(BF16)
-    copies = [pltpu.make_async_copy(a, b, sems.at[i]) for i, (a, b) in enumerate(zip((grad, *states), outs[1:]))]
+    grad[...] = dot(one_hot(grad.shape[0], per, high), rows, 0, 0).astype(BF16)
+
+
+def last_body(per, high, new, new_other, *refs):
+    held, outs, (out, sems) = refs[:4], refs[4:9], refs[9:]
+    copies = [pltpu.make_async_copy(a, b, sems.at[i]) for i, (a, b) in enumerate(zip(held, outs[1:]))]
     for copy in copies:
         copy.start()
+    move = one_hot(out.shape[0], per, high)
     tile = out.shape[1] // OUT_COPIES
     half = new.shape[0]
     for i in range(OUT_COPIES):
@@ -308,20 +308,19 @@
                       [old, old_other] + ([] if chip == 1 else [grad]))
         lines *= 2
     old_other = swap(old, 0, 0, 1)
-    near = [near[0], *reversed(near[1:])]
     pieces = [swap(new, *c) if any(c) else new for c in near]
     (new,) = call(functools.partial(across_body, reps, near), [((rows // 2, width), BF16)],
                   "across", [old, *pieces])
     new_other = swap(new, 0, 0, 1)
-    (product,) = call(product_body, [((rows, tokens), F32)], "product", [old, old_other, cot],
-                      cost=2 * rows * width * tokens)
     (grad,) = call(wide_body, [((per, width), F32)], "gradient", grads, cost=MAIN)
-    outs = [((rows, width), BF16), ((rows, tokens), BF16), *[((per, width), F32)] * 3]
+    outs = [((rows, tokens), BF16), *[((per, width), F32)] * 3]
+    held = call(functools.partial(product_body, per, high), outs, "product",
+                [old, old_other, cot, grad, *states], cost=2 * rows * width * tokens)
+    outs = [((rows, width), BF16), *outs]
     updated, input_grad, *states = call(
-        functools.partial(last_body, per, high), outs,
-        "last", [new, new_other, product, grad, *states],
+        functools.partial(last_body, per, high), outs, "last", [new, new_other, *held],
         out_specs=(pl.BlockSpec(memory_space=pltpu.HBM),) * 5,
-        scratch_shapes=[*(pltpu.VMEM(*out) for out in outs), pltpu.SemaphoreType.DMA((4 + OUT_COPIES,))],
+        scratch_shapes=[pltpu.VMEM(*outs[0]), pltpu.SemaphoreType.DMA((4 + OUT_COPIES,))],
     )
     return (input_grad.T, *states, updated)
 

time: 35.4 us -> 35.3 us (level)
  no operation moved by 1% of the time
where the time goes in v3:
time: 35.3 us; the launch traced here: 35.1 us
  starting transfers between devices  21.7 us (61%)
  waiting for transfers between devices  7.62 us (22%)
  Pallas kernels  5.02 us (14%)
  between operations  0.73 us (2%)
    ppermute x16, starting transfers between devices, swap(): lax.ppermute(value, (*CHIPS, 'core'), [(i, i ^ bits) for i in range(count)])  21.7 us
    ppermute x16, waiting for transfers between devices, swap(): lax.ppermute(value, (*CHIPS, 'core'), [(i, i ^ bits) for i in range(count)])  7.62 us
    pallas_call x13, Pallas kernels, call(): pl.pallas_call(body, out_shape=tuple((jax.ShapeDtypeStruct(*out) for out...  5.02 us
  transfers between devices with their start and end apart: 16, of which 9 were waited for; matrix products, arithmetic and copies ran while one was open for 0% of the time, Pallas kernels for 4%

profile of v3, /device:TPU:0, one launch (start us, length us, event | category | flops | bytes accessed | tf_op | source)
XLA Modules:
  0.0 35.1 jit_solution(3860723792201069449)
XLA Ops:
  0.7 2.1 %partial.1 = (f32[24,5120]{1,0:T(8,128)S(1)}, bf16[24,5120]{1,0:T(8,128)(2,1)S(1)}, bf16[256,5120]{1,0:T(8,128)(2,1)S(1)}) custom-call(bf16[48,256]{1,0:T(8,128)(2,1)} %bitcast.2, bf16[256,5120]{1,0:T(8,128)(2,1)} %cot_hbm.1), custom_call_target="tpu_custom_call" | custom-call | flops 125829120 | bytes 1000000 | tf_op jit(solution)/shard_map/partial/pallas_call | solution.py:24
  2.8 0.5 %collective-permute-start = (bf16[24,5120]{1,0:T(8,128)(2,1)S(1)}, bf16[24,5120]{1,0:T(8,128)(2,1)S(1)}, u32[]{:S(2)}, u32[]{:S(2)}) collective-permute-start(bf16[24,5120]{1,0:T(8,128)(2,1)S(1)} %get-tuple-element.29), channel_id=1, source_target_pairs={{0,1},{1,0},{2,3},{3,2},{4,5},{5,4},{6,7},{7,6},{8,9},{9,8},{10,11... | collective-permute-start | bytes 737288 | tf_op jit(solution)/shard_map/ppermute | solution.py:45
  3.3 1.1 %collective-permute-done.recv_ref = bf16[24,5120]{1,0:T(8,128)(2,1)S(1)} collective-permute-done((bf16[24,5120]{1,0:T(8,128)(2,1)S(1)}, bf16[24,5120]{1,0:T(8,128)(2,1)S(1)}, u32[]{:S(2)}, u32[]{:S(2)}) %collective-permute-start) | collective-permute-done | bytes 245792 | tf_op jit(solution)/shard_map/ppermute | solution.py:45
  4.5 0.1 middle.1
  4.6 3.6 %collective-permute-start.2 = (bf16[24,1280]{1,0:T(8,128)(2,1)S(1)}, bf16[24,1280]{1,0:T(8,128)(2,1)S(1)}, u32[]{:S(2)}, u32[]{:S(2)}) collective-permute-start(bf16[24,1280]{1,0:T(8,128)(2,1)S(1)} %get-tuple-element.32), channel_id=1, source_target_pairs={{0,19},{1,18},{2,17},{3,16},{4,23},{5,22},{6,21},{7,20},{8,27},{9,... | collective-permute-start | bytes 184328 | tf_op jit(solution)/shard_map/ppermute | solution.py:45
  8.2 0.5 %collective-permute-start.3 = (bf16[24,1280]{1,0:T(8,128)(2,1)S(1)}, bf16[24,1280]{1,0:T(8,128)(2,1)S(1)}, u32[]{:S(2)}, u32[]{:S(2)}) collective-permute-start(bf16[24,1280]{1,0:T(8,128)(2,1)S(1)} %get-tuple-element.33), channel_id=1, source_target_pairs={{0,3},{1,2},{2,1},{3,0},{4,7},{5,6},{6,5},{7,4},{8,11},{9,10},{10,... | collective-permute-start | bytes 184328 | tf_op jit(solution)/shard_map/ppermute | solution.py:45
  8.7 0.2 collective-permute-start.4
  8.9 2.4 %collective-permute-start.1 = (bf16[15,2560]{1,0:T(8,128)(2,1)S(1)}, bf16[15,2560]{1,0:T(8,128)(2,1)S(1)}, u32[]{:S(2)}, u32[]{:S(2)}) collective-permute-start(bf16[15,2560]{1,0:T(8,128)(2,1)S(1)} %get-tuple-element.30.state), channel_id=1, source_target_pairs={{0,9},{1,8},{2,11},{3,10},{4,13},{5,12},{6,15},{7,14},{8,1},{9,0},... | collective-permute-start | bytes 230408 | tf_op jit(solution)/shard_map/ppermute | solution.py:45
  11.3 0.8 %collective-permute-done.3.refs_2_ = bf16[24,1280]{1,0:T(8,128)(2,1)S(1)} collective-permute-done((bf16[24,1280]{1,0:T(8,128)(2,1)S(1)}, bf16[24,1280]{1,0:T(8,128)(2,1)S(1)}, u32[]{:S(2)}, u32[]{:S(2)}) %collective-permute-start.3) | collective-permute-done | bytes 61472 | tf_op jit(solution)/shard_map/ppermute | solution.py:45
  12.1 0.9 %collective-permute-done.4.refs_3_ = bf16[24,1280]{1,0:T(8,128)(2,1)S(1)} collective-permute-done((bf16[24,1280]{1,0:T(8,128)(2,1)S(1)}, bf16[24,1280]{1,0:T(8,128)(2,1)S(1)}, u32[]{:S(2)}, u32[]{:S(2)}) %collective-permute-start.4) | collective-permute-done | bytes 61472 | tf_op jit(solution)/shard_map/ppermute | solution.py:45
  13.0 1.0 %collective-permute-start.5 = (bf16[24,640]{1,0:T(8,128)(2,1)S(1)}, bf16[24,640]{1,0:T(8,128)(2,1)S(1)}, u32[]{:S(2)}, u32[]{:S(2)}) collective-permute-start(bf16[24,640]{1,0:T(8,128)(2,1)S(1)} %get-tuple-element.36), channel_id=1, source_target_pairs={{0,5},{1,4},{2,7},{3,6},{4,1},{5,0},{6,3},{7,2},{8,13},{9,12},{10,... | collective-permute-start | bytes 92168 | tf_op jit(solution)/shard_map/ppermute | solution.py:45
  14.0 2.9 %collective-permute-done.5.other = bf16[24,640]{1,0:T(8,128)(2,1)S(1)} collective-permute-done((bf16[24,640]{1,0:T(8,128)(2,1)S(1)}, bf16[24,640]{1,0:T(8,128)(2,1)S(1)}, u32[]{:S(2)}, u32[]{:S(2)}) %collective-permute-start.5) | collective-permute-done | bytes 30752 | tf_op jit(solution)/shard_map/ppermute | solution.py:45
  16.9 2.0 %collective-permute-start.7 = (bf16[24,640]{1,0:T(8,128)(2,1)S(1)}, bf16[24,640]{1,0:T(8,128)(2,1)S(1)}, u32[]{:S(2)}, u32[]{:S(2)}) collective-permute-start(bf16[24,640]{1,0:T(8,128)(2,1)S(1)} %whole.1.refs_0_.mine), channel_id=1, source_target_pairs={{0,9},{1,8},{2,11},{3,10},{4,13},{5,12},{6,15},{7,14},{8,1},{9,0},... | collective-permute-start | bytes 92168 | tf_op jit(solution)/shard_map/ppermute | solution.py:45
  19.0 0.1 arrange.1
  19.1 2.3 %collective-permute-start.6 = (bf16[24,1280]{1,0:T(8,128)(2,1)S(1)}, bf16[24,1280]{1,0:T(8,128)(2,1)S(1)}, u32[]{:S(2)}, u32[]{:S(2)}) collective-permute-start(bf16[24,1280]{1,0:T(8,128)(2,1)S(1)} %get-tuple-element.37.mine), channel_id=1, source_target_pairs={{0,5},{1,4},{2,7},{3,6},{4,1},{5,0},{6,3},{7,2},{8,13},{9,12},{10,... | collective-permute-start | bytes 184328 | tf_op jit(solution)/shard_map/ppermute | solution.py:45
  21.4 0.1 own.1
  21.5 1.8 %collective-permute-start.9 = (bf16[24,640]{1,0:T(8,128)(2,1)S(1)}, bf16[24,640]{1,0:T(8,128)(2,1)S(1)}, u32[]{:S(2)}, u32[]{:S(2)}) collective-permute-start(bf16[24,640]{1,0:T(8,128)(2,1)S(1)} %get-tuple-element.40.mine), channel_id=1, source_target_pairs={{0,5},{1,4},{2,7},{3,6},{4,1},{5,0},{6,3},{7,2},{8,13},{9,12},{10,... | collective-permute-start | bytes 92168 | tf_op jit(solution)/shard_map/ppermute | solution.py:45
  23.2 0.4 %collective-permute-done.6.other = bf16[24,1280]{1,0:T(8,128)(2,1)S(1)} collective-permute-done((bf16[24,1280]{1,0:T(8,128)(2,1)S(1)}, bf16[24,1280]{1,0:T(8,128)(2,1)S(1)}, u32[]{:S(2)}, u32[]{:S(2)}) %collective-permute-start.6) | collective-permute-done | bytes 61472 | tf_op jit(solution)/shard_map/ppermute | solution.py:45
  23.7 1.3 %collective-permute-start.8 = (bf16[24,2560]{1,0:T(8,128)(2,1)S(1)}, bf16[24,2560]{1,0:T(8,128)(2,1)S(1)}, u32[]{:S(2)}, u32[]{:S(2)}) collective-permute-start(bf16[24,2560]{1,0:T(8,128)(2,1)S(1)} %join_old.2.mine), channel_id=1, source_target_pairs={{0,3},{1,2},{2,1},{3,0},{4,7},{5,6},{6,5},{7,4},{8,11},{9,10},{10,... | collective-permute-start | bytes 368648 | tf_op jit(solution)/shard_map/ppermute | solution.py:45
  25.0 2.2 %collective-permute-start.10 = (bf16[24,1280]{1,0:T(8,128)(2,1)S(1)}, bf16[24,1280]{1,0:T(8,128)(2,1)S(1)}, u32[]{:S(2)}, u32[]{:S(2)}) collective-permute-start(bf16[24,1280]{1,0:T(8,128)(2,1)S(1)} %copies.1.refs_1_), channel_id=1, source_target_pairs={{0,19},{1,18},{2,17},{3,16},{4,23},{5,22},{6,21},{7,20},{8,27},{9,... | collective-permute-start | bytes 184328 | tf_op jit(solution)/shard_map/ppermute | solution.py:45
  27.2 0.6 %collective-permute-start.11 = (bf16[24,1280]{1,0:T(8,128)(2,1)S(1)}, bf16[24,1280]{1,0:T(8,128)(2,1)S(1)}, u32[]{:S(2)}, u32[]{:S(2)}) collective-permute-start(bf16[24,1280]{1,0:T(8,128)(2,1)S(1)} %copies.1.refs_1_), channel_id=1, source_target_pairs={{0,3},{1,2},{2,1},{3,0},{4,7},{5,6},{6,5},{7,4},{8,11},{9,10},{10,... | collective-permute-start | bytes 184328 | tf_op jit(solution)/shard_map/ppermute | solution.py:45
  27.8 0.5 %collective-permute-start.12 = (bf16[24,1280]{1,0:T(8,128)(2,1)S(1)}, bf16[24,1280]{1,0:T(8,128)(2,1)S(1)}, u32[]{:S(2)}, u32[]{:S(2)}) collective-permute-start(bf16[24,1280]{1,0:T(8,128)(2,1)S(1)} %copies.1.refs_1_), channel_id=1, source_target_pairs={{0,16},{1,17},{2,18},{3,19},{4,20},{5,21},{6,22},{7,23},{8,24},{9,... | collective-permute-start | bytes 184328 | tf_op jit(solution)/shard_map/ppermute | solution.py:45
  28.3 1.5 %collective-permute-start.15 = (bf16[3,2560]{1,0:T(4,128)(2,1)S(1)}, bf16[3,2560]{1,0:T(4,128)(2,1)S(1)}, u32[]{:S(2)}, u32[]{:S(2)}) collective-permute-start(bf16[3,2560]{1,0:T(4,128)(2,1)S(1)} %get-tuple-element.39.refs_0_), channel_id=1, source_target_pairs={{0,16},{1,17},{2,18},{3,19},{4,20},{5,21},{6,22},{7,23},{8,24},{9,... | collective-permute-start | bytes 46088 | tf_op jit(solution)/shard_map/ppermute | solution.py:45
  29.8 0.1 join_old.3.refs_0_.old
  29.9 1.3 %collective-permute-start.14 = (bf16[24,5120]{1,0:T(8,128)(2,1)S(1)}, bf16[24,5120]{1,0:T(8,128)(2,1)S(1)}, u32[]{:S(2)}, u32[]{:S(2)}) collective-permute-start(bf16[24,5120]{1,0:T(8,128)(2,1)S(1)} %join_old.3.refs_0_.old), channel_id=1, source_target_pairs={{0,1},{1,0},{2,3},{3,2},{4,5},{5,4},{6,7},{7,6},{8,9},{9,8},{10,11... | collective-permute-start | bytes 737288 | tf_op jit(solution)/shard_map/ppermute | solution.py:45
  31.2 0.6 %collective-permute-done.11.refs_3_ = bf16[24,1280]{1,0:T(8,128)(2,1)S(1)} collective-permute-done((bf16[24,1280]{1,0:T(8,128)(2,1)S(1)}, bf16[24,1280]{1,0:T(8,128)(2,1)S(1)}, u32[]{:S(2)}, u32[]{:S(2)}) %collective-permute-start.11) | collective-permute-done | bytes 61472 | tf_op jit(solution)/shard_map/ppermute | solution.py:45
  31.8 0.5 %collective-permute-done.12.refs_4_ = bf16[24,1280]{1,0:T(8,128)(2,1)S(1)} collective-permute-done((bf16[24,1280]{1,0:T(8,128)(2,1)S(1)}, bf16[24,1280]{1,0:T(8,128)(2,1)S(1)}, u32[]{:S(2)}, u32[]{:S(2)}) %collective-permute-start.12) | collective-permute-done | bytes 61472 | tf_op jit(solution)/shard_map/ppermute | solution.py:45
  32.3 0.1 collective-permute-start.13
  32.4 0.1 collective-permute-done.15.refs_1_
  32.5 1.0 %product.1 = (bf16[48,256]{1,0:T(8,128)(2,1)S(1)}, f32[3,5120]{1,0:T(4,128)S(1)}, f32[3,5120]{1,0:T(4,128)S(1)}, f32[3,5120]{1,0:T(4,128)S(1)}) custom-call(bf16[24,5120]{1,0:T(8,128)(2,1)S(1)} %join_old.3.refs_0_.old, bf16[24,5120]{1,0:T(8,128)(2,1)S(1)} %collective-permute-done.14.old_other, bf16[256,5120]{1,0:T(8,128)(2,1)S(1)} %get-tuple-element.41.cot, ...), custom_call_target="tpu_custom_call" | custom-call | flops 125829120 | bytes 1000000 | tf_op jit(solution)/shard_map/product/pallas_call | solution.py:24
  33.5 0.4 %collective-permute-done.13.new_other = bf16[24,5120]{1,0:T(8,128)(2,1)S(1)} collective-permute-done((bf16[24,5120]{1,0:T(8,128)(2,1)S(1)}, bf16[24,5120]{1,0:T(8,128)(2,1)S(1)}, u32[]{:S(2)}, u32[]{:S(2)}) %collective-permute-start.13) | collective-permute-done | bytes 245792 | tf_op jit(solution)/shard_map/ppermute | solution.py:45
  33.9 1.2 %last.1 = (bf16[48,5120]{1,0:T(8,128)(2,1)}, bf16[48,256]{1,0:T(8,128)(2,1)}, f32[3,5120]{1,0:T(4,128)}, f32[3,5120]{1,0:T(4,128)}, f32[3,5120]{1,0:T(4,128)}) custom-call(bf16[24,5120]{1,0:T(8,128)(2,1)S(1)} %across.1.new, bf16[24,5120]{1,0:T(8,128)(2,1)S(1)} %collective-permute-done.13.new_other, bf16[48,256]{1,0:T(8,128)(2,1)S(1)} %get-tuple-element.42.refs_0_, ...), custom_call_target="tpu_custom_call" | custom-call | flops 1000000 | bytes 1000000 | tf_op jit(solution)/shard_map/last/pallas_call | solution.py:24
  (19 shorter events, 0.3 us)
Async XLA Ops:
  0.6 3.8 %copy-start = (f32[3,5120]{1,0:T(4,128)S(1)}, f32[3,5120]{1,0:T(4,128)}, u32[]{:S(2)}) copy-start(f32[3,5120]{1,0:T(4,128)} %master.3) | copy-start | bytes 184324
  0.6 3.8 %copy-start.1 = (f32[3,5120]{1,0:T(4,128)S(1)}, f32[3,5120]{1,0:T(4,128)}, u32[]{:S(2)}) copy-start(f32[3,5120]{1,0:T(4,128)} %moment.3) | copy-start | bytes 184324
  0.7 3.8 %copy-start.2 = (f32[3,5120]{1,0:T(4,128)S(1)}, f32[3,5120]{1,0:T(4,128)}, u32[]{:S(2)}) copy-start(f32[3,5120]{1,0:T(4,128)} %second.3) | copy-start | bytes 184324
  2.8 1.7 %collective-permute-start = (bf16[24,5120]{1,0:T(8,128)(2,1)S(1)}, bf16[24,5120]{1,0:T(8,128)(2,1)S(1)}, u32[]{:S(2)}, u32[]{:S(2)}) collective-permute-start(bf16[24,5120]{1,0:T(8,128)(2,1)S(1)} %get-tuple-element.29), channel_id=1, source_target_pairs={{0,1},{1,0},{2,3},{3,2},{4,5},{5,4},{6,7},{7,6},{8,9},{9,8},{10,11... | collective-permute-start | bytes 737288 | tf_op jit(solution)/shard_map/ppermute | solution.py:45
  4.6 6.7 %collective-permute-start.2 = (bf16[24,1280]{1,0:T(8,128)(2,1)S(1)}, bf16[24,1280]{1,0:T(8,128)(2,1)S(1)}, u32[]{:S(2)}, u32[]{:S(2)}) collective-permute-start(bf16[24,1280]{1,0:T(8,128)(2,1)S(1)} %get-tuple-element.32), channel_id=1, source_target_pairs={{0,19},{1,18},{2,17},{3,16},{4,23},{5,22},{6,21},{7,20},{8,27},{9,... | collective-permute-start | bytes 184328 | tf_op jit(solution)/shard_map/ppermute | solution.py:45
  8.2 3.9 %collective-permute-start.3 = (bf16[24,1280]{1,0:T(8,128)(2,1)S(1)}, bf16[24,1280]{1,0:T(8,128)(2,1)S(1)}, u32[]{:S(2)}, u32[]{:S(2)}) collective-permute-start(bf16[24,1280]{1,0:T(8,128)(2,1)S(1)} %get-tuple-element.33), channel_id=1, source_target_pairs={{0,3},{1,2},{2,1},{3,0},{4,7},{5,6},{6,5},{7,4},{8,11},{9,10},{10,... | collective-permute-start | bytes 184328 | tf_op jit(solution)/shard_map/ppermute | solution.py:45
  8.7 4.2 %collective-permute-start.4 = (bf16[24,1280]{1,0:T(8,128)(2,1)S(1)}, bf16[24,1280]{1,0:T(8,128)(2,1)S(1)}, u32[]{:S(2)}, u32[]{:S(2)}) collective-permute-start(bf16[24,1280]{1,0:T(8,128)(2,1)S(1)} %get-tuple-element.34), channel_id=1, source_target_pairs={{0,16},{1,17},{2,18},{3,19},{4,20},{5,21},{6,22},{7,23},{8,24},{9,... | collective-permute-start | bytes 184328 | tf_op jit(solution)/shard_map/ppermute | solution.py:45
  8.9 10.1 %collective-permute-start.1 = (bf16[15,2560]{1,0:T(8,128)(2,1)S(1)}, bf16[15,2560]{1,0:T(8,128)(2,1)S(1)}, u32[]{:S(2)}, u32[]{:S(2)}) collective-permute-start(bf16[15,2560]{1,0:T(8,128)(2,1)S(1)} %get-tuple-element.30.state), channel_id=1, source_target_pairs={{0,9},{1,8},{2,11},{3,10},{4,13},{5,12},{6,15},{7,14},{8,1},{9,0},... | collective-permute-start | bytes 230408 | tf_op jit(solution)/shard_map/ppermute | solution.py:45
  13.0 3.9 %collective-permute-start.5 = (bf16[24,640]{1,0:T(8,128)(2,1)S(1)}, bf16[24,640]{1,0:T(8,128)(2,1)S(1)}, u32[]{:S(2)}, u32[]{:S(2)}) collective-permute-start(bf16[24,640]{1,0:T(8,128)(2,1)S(1)} %get-tuple-element.36), channel_id=1, source_target_pairs={{0,5},{1,4},{2,7},{3,6},{4,1},{5,0},{6,3},{7,2},{8,13},{9,12},{10,... | collective-permute-start | bytes 92168 | tf_op jit(solution)/shard_map/ppermute | solution.py:45
  16.9 4.4 %collective-permute-start.7 = (bf16[24,640]{1,0:T(8,128)(2,1)S(1)}, bf16[24,640]{1,0:T(8,128)(2,1)S(1)}, u32[]{:S(2)}, u32[]{:S(2)}) collective-permute-start(bf16[24,640]{1,0:T(8,128)(2,1)S(1)} %whole.1.refs_0_.mine), channel_id=1, source_target_pairs={{0,9},{1,8},{2,11},{3,10},{4,13},{5,12},{6,15},{7,14},{8,1},{9,0},... | collective-permute-start | bytes 92168 | tf_op jit(solution)/shard_map/ppermute | solution.py:45
  19.1 4.5 %collective-permute-start.6 = (bf16[24,1280]{1,0:T(8,128)(2,1)S(1)}, bf16[24,1280]{1,0:T(8,128)(2,1)S(1)}, u32[]{:S(2)}, u32[]{:S(2)}) collective-permute-start(bf16[24,1280]{1,0:T(8,128)(2,1)S(1)} %get-tuple-element.37.mine), channel_id=1, source_target_pairs={{0,5},{1,4},{2,7},{3,6},{4,1},{5,0},{6,3},{7,2},{8,13},{9,12},{10,... | collective-permute-start | bytes 184328 | tf_op jit(solution)/shard_map/ppermute | solution.py:45
  21.5 3.5 %collective-permute-start.9 = (bf16[24,640]{1,0:T(8,128)(2,1)S(1)}, bf16[24,640]{1,0:T(8,128)(2,1)S(1)}, u32[]{:S(2)}, u32[]{:S(2)}) collective-permute-start(bf16[24,640]{1,0:T(8,128)(2,1)S(1)} %get-tuple-element.40.mine), channel_id=1, source_target_pairs={{0,5},{1,4},{2,7},{3,6},{4,1},{5,0},{6,3},{7,2},{8,13},{9,12},{10,... | collective-permute-start | bytes 92168 | tf_op jit(solution)/shard_map/ppermute | solution.py:45
  23.7 6.1 %collective-permute-start.8 = (bf16[24,2560]{1,0:T(8,128)(2,1)S(1)}, bf16[24,2560]{1,0:T(8,128)(2,1)S(1)}, u32[]{:S(2)}, u32[]{:S(2)}) collective-permute-start(bf16[24,2560]{1,0:T(8,128)(2,1)S(1)} %join_old.2.mine), channel_id=1, source_target_pairs={{0,3},{1,2},{2,1},{3,0},{4,7},{5,6},{6,5},{7,4},{8,11},{9,10},{10,... | collective-permute-start | bytes 368648 | tf_op jit(solution)/shard_map/ppermute | solution.py:45
  25.0 6.1 %collective-permute-start.10 = (bf16[24,1280]{1,0:T(8,128)(2,1)S(1)}, bf16[24,1280]{1,0:T(8,128)(2,1)S(1)}, u32[]{:S(2)}, u32[]{:S(2)}) collective-permute-start(bf16[24,1280]{1,0:T(8,128)(2,1)S(1)} %copies.1.refs_1_), channel_id=1, source_target_pairs={{0,19},{1,18},{2,17},{3,16},{4,23},{5,22},{6,21},{7,20},{8,27},{9,... | collective-permute-start | bytes 184328 | tf_op jit(solution)/shard_map/ppermute | solution.py:45
  27.2 4.6 %collective-permute-start.11 = (bf16[24,1280]{1,0:T(8,128)(2,1)S(1)}, bf16[24,1280]{1,0:T(8,128)(2,1)S(1)}, u32[]{:S(2)}, u32[]{:S(2)}) collective-permute-start(bf16[24,1280]{1,0:T(8,128)(2,1)S(1)} %copies.1.refs_1_), channel_id=1, source_target_pairs={{0,3},{1,2},{2,1},{3,0},{4,7},{5,6},{6,5},{7,4},{8,11},{9,10},{10,... | collective-permute-start | bytes 184328 | tf_op jit(solution)/shard_map/ppermute | solution.py:45
  27.8 4.5 %collective-permute-start.12 = (bf16[24,1280]{1,0:T(8,128)(2,1)S(1)}, bf16[24,1280]{1,0:T(8,128)(2,1)S(1)}, u32[]{:S(2)}, u32[]{:S(2)}) collective-permute-start(bf16[24,1280]{1,0:T(8,128)(2,1)S(1)} %copies.1.refs_1_), channel_id=1, source_target_pairs={{0,16},{1,17},{2,18},{3,19},{4,20},{5,21},{6,22},{7,23},{8,24},{9,... | collective-permute-start | bytes 184328 | tf_op jit(solution)/shard_map/ppermute | solution.py:45
  28.3 4.2 %collective-permute-start.15 = (bf16[3,2560]{1,0:T(4,128)(2,1)S(1)}, bf16[3,2560]{1,0:T(4,128)(2,1)S(1)}, u32[]{:S(2)}, u32[]{:S(2)}) collective-permute-start(bf16[3,2560]{1,0:T(4,128)(2,1)S(1)} %get-tuple-element.39.refs_0_), channel_id=1, source_target_pairs={{0,16},{1,17},{2,18},{3,19},{4,20},{5,21},{6,22},{7,23},{8,24},{9,... | collective-permute-start | bytes 46088 | tf_op jit(solution)/shard_map/ppermute | solution.py:45
  29.9 2.6 %collective-permute-start.14 = (bf16[24,5120]{1,0:T(8,128)(2,1)S(1)}, bf16[24,5120]{1,0:T(8,128)(2,1)S(1)}, u32[]{:S(2)}, u32[]{:S(2)}) collective-permute-start(bf16[24,5120]{1,0:T(8,128)(2,1)S(1)} %join_old.3.refs_0_.old), channel_id=1, source_target_pairs={{0,1},{1,0},{2,3},{3,2},{4,5},{5,4},{6,7},{7,6},{8,9},{9,8},{10,11... | collective-permute-start | bytes 737288 | tf_op jit(solution)/shard_map/ppermute | solution.py:45
  32.3 1.6 %collective-permute-start.13 = (bf16[24,5120]{1,0:T(8,128)(2,1)S(1)}, bf16[24,5120]{1,0:T(8,128)(2,1)S(1)}, u32[]{:S(2)}, u32[]{:S(2)}) collective-permute-start(bf16[24,5120]{1,0:T(8,128)(2,1)S(1)} %across.1.new), channel_id=1, source_target_pairs={{0,1},{1,0},{2,3},{3,2},{4,5},{5,4},{6,7},{7,6},{8,9},{9,8},{10,11... | collective-permute-start | bytes 737288 | tf_op jit(solution)/shard_map/ppermute | solution.py:45

commit v4 on v3

--- a/solution.py
+++ b/solution.py
@@ -14,6 +14,7 @@
 CORES = 2
 LOW = 2
 COT_COPIES = 2
+ROW_COPIES = 4
 OUT_COPIES = 5
 MAIN = 3 * 10**9
 CHIPS = ("rep", "high", "low")
@@ -92,12 +93,12 @@
 
 def partial_body(per, high, hid_hbm, cot_hbm, keep_ref, send_ref, cot_ref, hid, sems):
     rows, width = hid.shape[0], cot_ref.shape[1]
-    tile = width // COT_COPIES
+    tile, lines = width // COT_COPIES, cot_ref.shape[0] // ROW_COPIES
     pieces = [(hid_hbm, hid)]
-    pieces += [
-        (cot_hbm.at[:, pl.ds(i * tile, tile)], cot_ref.at[:, pl.ds(i * tile, tile)])
-        for i in range(COT_COPIES)
-    ]
+    for i in range(COT_COPIES):
+        for j in range(ROW_COPIES):
+            part = (pl.ds(j * lines, lines), pl.ds(i * tile, tile))
+            pieces.append((cot_hbm.at[part], cot_ref.at[part]))
     copies = [pltpu.make_async_copy(a, b, sems.at[i]) for i, (a, b) in enumerate(pieces)]
     for copy in copies:
         copy.start()
@@ -105,7 +106,8 @@
     copies[0].wait()
     moved = dot(move, hid[...], 1, 0).astype(BF16)
     for i in range(COT_COPIES):
-        copies[1 + i].wait()
+        for copy in copies[1 + i * ROW_COPIES : 1 + (i + 1) * ROW_COPIES]:
+            copy.wait()
         cols = pl.ds(i * tile, tile)
         g = dot(moved, cot_ref[:, cols], 1, 0)
         keep_ref[:, cols] = g[: rows // 2]
@@ -265,7 +267,7 @@
         "partial", ins,
         cost=2 * rows * width * tokens,
         in_specs=[pl.BlockSpec(memory_space=pltpu.HBM)] * 2,
-        scratch_shapes=[pltpu.VMEM((rows, tokens), BF16), pltpu.SemaphoreType.DMA((COT_COPIES + 1,))],
+        scratch_shapes=[pltpu.VMEM((rows, tokens), BF16), pltpu.SemaphoreType.DMA((COT_COPIES * ROW_COPIES + 1,))],
     )
 
     recv = swap(send, 0, 0, 1)

time: 35.3 us -> 35.3 us (level)
  no operation moved by 1% of the time
where the time goes in v4:
time: 35.3 us; the launch traced here: 35.1 us
  starting transfers between devices  21.7 us (61%)
  waiting for transfers between devices  7.62 us (22%)
  Pallas kernels  5.03 us (14%)
  between operations  0.73 us (2%)
    ppermute x16, starting transfers between devices, swap(): lax.ppermute(value, (*CHIPS, 'core'), [(i, i ^ bits) for i in range(count)])  21.7 us
    ppermute x16, waiting for transfers between devices, swap(): lax.ppermute(value, (*CHIPS, 'core'), [(i, i ^ bits) for i in range(count)])  7.62 us
    pallas_call x13, Pallas kernels, call(): pl.pallas_call(body, out_shape=tuple((jax.ShapeDtypeStruct(*out) for out...  5.03 us
  transfers between devices with their start and end apart: 16, of which 9 were waited for; matrix products, arithmetic and copies ran while one was open for 0% of the time, Pallas kernels for 4%

profile of v4, /device:TPU:0, one launch (start us, length us, event | category | flops | bytes accessed | tf_op | source)
XLA Modules:
  0.0 35.1 jit_solution(14008350179729426757)
XLA Ops:
  0.7 2.1 %partial.1 = (f32[24,5120]{1,0:T(8,128)S(1)}, bf16[24,5120]{1,0:T(8,128)(2,1)S(1)}, bf16[256,5120]{1,0:T(8,128)(2,1)S(1)}) custom-call(bf16[48,256]{1,0:T(8,128)(2,1)} %bitcast.2, bf16[256,5120]{1,0:T(8,128)(2,1)} %cot_hbm.1), custom_call_target="tpu_custom_call" | custom-call | flops 125829120 | bytes 1000000 | tf_op jit(solution)/shard_map/partial/pallas_call | solution.py:25
  2.8 0.5 %collective-permute-start = (bf16[24,5120]{1,0:T(8,128)(2,1)S(1)}, bf16[24,5120]{1,0:T(8,128)(2,1)S(1)}, u32[]{:S(2)}, u32[]{:S(2)}) collective-permute-start(bf16[24,5120]{1,0:T(8,128)(2,1)S(1)} %get-tuple-element.29), channel_id=1, source_target_pairs={{0,1},{1,0},{2,3},{3,2},{4,5},{5,4},{6,7},{7,6},{8,9},{9,8},{10,11... | collective-permute-start | bytes 737288 | tf_op jit(solution)/shard_map/ppermute | solution.py:46
  3.3 1.1 %collective-permute-done.recv_ref = bf16[24,5120]{1,0:T(8,128)(2,1)S(1)} collective-permute-done((bf16[24,5120]{1,0:T(8,128)(2,1)S(1)}, bf16[24,5120]{1,0:T(8,128)(2,1)S(1)}, u32[]{:S(2)}, u32[]{:S(2)}) %collective-permute-start) | collective-permute-done | bytes 245792 | tf_op jit(solution)/shard_map/ppermute | solution.py:46
  4.5 0.1 middle.1
  4.6 3.6 %collective-permute-start.2 = (bf16[24,1280]{1,0:T(8,128)(2,1)S(1)}, bf16[24,1280]{1,0:T(8,128)(2,1)S(1)}, u32[]{:S(2)}, u32[]{:S(2)}) collective-permute-start(bf16[24,1280]{1,0:T(8,128)(2,1)S(1)} %get-tuple-element.32), channel_id=1, source_target_pairs={{0,19},{1,18},{2,17},{3,16},{4,23},{5,22},{6,21},{7,20},{8,27},{9,... | collective-permute-start | bytes 184328 | tf_op jit(solution)/shard_map/ppermute | solution.py:46
  8.2 0.5 %collective-permute-start.3 = (bf16[24,1280]{1,0:T(8,128)(2,1)S(1)}, bf16[24,1280]{1,0:T(8,128)(2,1)S(1)}, u32[]{:S(2)}, u32[]{:S(2)}) collective-permute-start(bf16[24,1280]{1,0:T(8,128)(2,1)S(1)} %get-tuple-element.33), channel_id=1, source_target_pairs={{0,3},{1,2},{2,1},{3,0},{4,7},{5,6},{6,5},{7,4},{8,11},{9,10},{10,... | collective-permute-start | bytes 184328 | tf_op jit(solution)/shard_map/ppermute | solution.py:46
  8.7 0.2 collective-permute-start.4
  8.9 2.4 %collective-permute-start.1 = (bf16[15,2560]{1,0:T(8,128)(2,1)S(1)}, bf16[15,2560]{1,0:T(8,128)(2,1)S(1)}, u32[]{:S(2)}, u32[]{:S(2)}) collective-permute-start(bf16[15,2560]{1,0:T(8,128)(2,1)S(1)} %get-tuple-element.30.state), channel_id=1, source_target_pairs={{0,9},{1,8},{2,11},{3,10},{4,13},{5,12},{6,15},{7,14},{8,1},{9,0},... | collective-permute-start | bytes 230408 | tf_op jit(solution)/shard_map/ppermute | solution.py:46
  11.3 0.8 %collective-permute-done.3.refs_2_ = bf16[24,1280]{1,0:T(8,128)(2,1)S(1)} collective-permute-done((bf16[24,1280]{1,0:T(8,128)(2,1)S(1)}, bf16[24,1280]{1,0:T(8,128)(2,1)S(1)}, u32[]{:S(2)}, u32[]{:S(2)}) %collective-permute-start.3) | collective-permute-done | bytes 61472 | tf_op jit(solution)/shard_map/ppermute | solution.py:46
  12.1 0.9 %collective-permute-done.4.refs_3_ = bf16[24,1280]{1,0:T(8,128)(2,1)S(1)} collective-permute-done((bf16[24,1280]{1,0:T(8,128)(2,1)S(1)}, bf16[24,1280]{1,0:T(8,128)(2,1)S(1)}, u32[]{:S(2)}, u32[]{:S(2)}) %collective-permute-start.4) | collective-permute-done | bytes 61472 | tf_op jit(solution)/shard_map/ppermute | solution.py:46
  13.0 1.0 %collective-permute-start.5 = (bf16[24,640]{1,0:T(8,128)(2,1)S(1)}, bf16[24,640]{1,0:T(8,128)(2,1)S(1)}, u32[]{:S(2)}, u32[]{:S(2)}) collective-permute-start(bf16[24,640]{1,0:T(8,128)(2,1)S(1)} %get-tuple-element.36), channel_id=1, source_target_pairs={{0,5},{1,4},{2,7},{3,6},{4,1},{5,0},{6,3},{7,2},{8,13},{9,12},{10,... | collective-permute-start | bytes 92168 | tf_op jit(solution)/shard_map/ppermute | solution.py:46
  14.0 2.9 %collective-permute-done.5.other = bf16[24,640]{1,0:T(8,128)(2,1)S(1)} collective-permute-done((bf16[24,640]{1,0:T(8,128)(2,1)S(1)}, bf16[24,640]{1,0:T(8,128)(2,1)S(1)}, u32[]{:S(2)}, u32[]{:S(2)}) %collective-permute-start.5) | collective-permute-done | bytes 30752 | tf_op jit(solution)/shard_map/ppermute | solution.py:46
  16.9 2.0 %collective-permute-start.7 = (bf16[24,640]{1,0:T(8,128)(2,1)S(1)}, bf16[24,640]{1,0:T(8,128)(2,1)S(1)}, u32[]{:S(2)}, u32[]{:S(2)}) collective-permute-start(bf16[24,640]{1,0:T(8,128)(2,1)S(1)} %whole.1.refs_0_.mine), channel_id=1, source_target_pairs={{0,9},{1,8},{2,11},{3,10},{4,13},{5,12},{6,15},{7,14},{8,1},{9,0},... | collective-permute-start | bytes 92168 | tf_op jit(solution)/shard_map/ppermute | solution.py:46
  19.0 0.1 arrange.1
  19.1 2.3 %collective-permute-start.6 = (bf16[24,1280]{1,0:T(8,128)(2,1)S(1)}, bf16[24,1280]{1,0:T(8,128)(2,1)S(1)}, u32[]{:S(2)}, u32[]{:S(2)}) collective-permute-start(bf16[24,1280]{1,0:T(8,128)(2,1)S(1)} %get-tuple-element.37.mine), channel_id=1, source_target_pairs={{0,5},{1,4},{2,7},{3,6},{4,1},{5,0},{6,3},{7,2},{8,13},{9,12},{10,... | collective-permute-start | bytes 184328 | tf_op jit(solution)/shard_map/ppermute | solution.py:46
  21.4 0.1 own.1
  21.5 1.8 %collective-permute-start.9 = (bf16[24,640]{1,0:T(8,128)(2,1)S(1)}, bf16[24,640]{1,0:T(8,128)(2,1)S(1)}, u32[]{:S(2)}, u32[]{:S(2)}) collective-permute-start(bf16[24,640]{1,0:T(8,128)(2,1)S(1)} %get-tuple-element.40.mine), channel_id=1, source_target_pairs={{0,5},{1,4},{2,7},{3,6},{4,1},{5,0},{6,3},{7,2},{8,13},{9,12},{10,... | collective-permute-start | bytes 92168 | tf_op jit(solution)/shard_map/ppermute | solution.py:46
  23.3 0.4 %collective-permute-done.6.other = bf16[24,1280]{1,0:T(8,128)(2,1)S(1)} collective-permute-done((bf16[24,1280]{1,0:T(8,128)(2,1)S(1)}, bf16[24,1280]{1,0:T(8,128)(2,1)S(1)}, u32[]{:S(2)}, u32[]{:S(2)}) %collective-permute-start.6) | collective-permute-done | bytes 61472 | tf_op jit(solution)/shard_map/ppermute | solution.py:46
  23.7 1.3 %collective-permute-start.8 = (bf16[24,2560]{1,0:T(8,128)(2,1)S(1)}, bf16[24,2560]{1,0:T(8,128)(2,1)S(1)}, u32[]{:S(2)}, u32[]{:S(2)}) collective-permute-start(bf16[24,2560]{1,0:T(8,128)(2,1)S(1)} %join_old.2.mine), channel_id=1, source_target_pairs={{0,3},{1,2},{2,1},{3,0},{4,7},{5,6},{6,5},{7,4},{8,11},{9,10},{10,... | collective-permute-start | bytes 368648 | tf_op jit(solution)/shard_map/ppermute | solution.py:46
  25.0 2.2 %collective-permute-start.10 = (bf16[24,1280]{1,0:T(8,128)(2,1)S(1)}, bf16[24,1280]{1,0:T(8,128)(2,1)S(1)}, u32[]{:S(2)}, u32[]{:S(2)}) collective-permute-start(bf16[24,1280]{1,0:T(8,128)(2,1)S(1)} %copies.1.refs_1_), channel_id=1, source_target_pairs={{0,19},{1,18},{2,17},{3,16},{4,23},{5,22},{6,21},{7,20},{8,27},{9,... | collective-permute-start | bytes 184328 | tf_op jit(solution)/shard_map/ppermute | solution.py:46
  27.2 0.6 %collective-permute-start.11 = (bf16[24,1280]{1,0:T(8,128)(2,1)S(1)}, bf16[24,1280]{1,0:T(8,128)(2,1)S(1)}, u32[]{:S(2)}, u32[]{:S(2)}) collective-permute-start(bf16[24,1280]{1,0:T(8,128)(2,1)S(1)} %copies.1.refs_1_), channel_id=1, source_target_pairs={{0,3},{1,2},{2,1},{3,0},{4,7},{5,6},{6,5},{7,4},{8,11},{9,10},{10,... | collective-permute-start | bytes 184328 | tf_op jit(solution)/shard_map/ppermute | solution.py:46
  27.8 0.5 %collective-permute-start.12 = (bf16[24,1280]{1,0:T(8,128)(2,1)S(1)}, bf16[24,1280]{1,0:T(8,128)(2,1)S(1)}, u32[]{:S(2)}, u32[]{:S(2)}) collective-permute-start(bf16[24,1280]{1,0:T(8,128)(2,1)S(1)} %copies.1.refs_1_), channel_id=1, source_target_pairs={{0,16},{1,17},{2,18},{3,19},{4,20},{5,21},{6,22},{7,23},{8,24},{9,... | collective-permute-start | bytes 184328 | tf_op jit(solution)/shard_map/ppermute | solution.py:46
  28.3 1.5 %collective-permute-start.15 = (bf16[3,2560]{1,0:T(4,128)(2,1)S(1)}, bf16[3,2560]{1,0:T(4,128)(2,1)S(1)}, u32[]{:S(2)}, u32[]{:S(2)}) collective-permute-start(bf16[3,2560]{1,0:T(4,128)(2,1)S(1)} %get-tuple-element.39.refs_0_), channel_id=1, source_target_pairs={{0,16},{1,17},{2,18},{3,19},{4,20},{5,21},{6,22},{7,23},{8,24},{9,... | collective-permute-start | bytes 46088 | tf_op jit(solution)/shard_map/ppermute | solution.py:46
  29.8 0.1 join_old.3.refs_0_.old
  29.9 1.3 %collective-permute-start.14 = (bf16[24,5120]{1,0:T(8,128)(2,1)S(1)}, bf16[24,5120]{1,0:T(8,128)(2,1)S(1)}, u32[]{:S(2)}, u32[]{:S(2)}) collective-permute-start(bf16[24,5120]{1,0:T(8,128)(2,1)S(1)} %join_old.3.refs_0_.old), channel_id=1, source_target_pairs={{0,1},{1,0},{2,3},{3,2},{4,5},{5,4},{6,7},{7,6},{8,9},{9,8},{10,11... | collective-permute-start | bytes 737288 | tf_op jit(solution)/shard_map/ppermute | solution.py:46
  31.2 0.6 %collective-permute-done.11.refs_3_ = bf16[24,1280]{1,0:T(8,128)(2,1)S(1)} collective-permute-done((bf16[24,1280]{1,0:T(8,128)(2,1)S(1)}, bf16[24,1280]{1,0:T(8,128)(2,1)S(1)}, u32[]{:S(2)}, u32[]{:S(2)}) %collective-permute-start.11) | collective-permute-done | bytes 61472 | tf_op jit(solution)/shard_map/ppermute | solution.py:46
  31.8 0.5 %collective-permute-done.12.refs_4_ = bf16[24,1280]{1,0:T(8,128)(2,1)S(1)} collective-permute-done((bf16[24,1280]{1,0:T(8,128)(2,1)S(1)}, bf16[24,1280]{1,0:T(8,128)(2,1)S(1)}, u32[]{:S(2)}, u32[]{:S(2)}) %collective-permute-start.12) | collective-permute-done | bytes 61472 | tf_op jit(solution)/shard_map/ppermute | solution.py:46
  32.3 0.1 collective-permute-start.13
  32.4 0.1 collective-permute-done.15.refs_1_
  32.5 1.0 %product.1 = (bf16[48,256]{1,0:T(8,128)(2,1)S(1)}, f32[3,5120]{1,0:T(4,128)S(1)}, f32[3,5120]{1,0:T(4,128)S(1)}, f32[3,5120]{1,0:T(4,128)S(1)}) custom-call(bf16[24,5120]{1,0:T(8,128)(2,1)S(1)} %join_old.3.refs_0_.old, bf16[24,5120]{1,0:T(8,128)(2,1)S(1)} %collective-permute-done.14.old_other, bf16[256,5120]{1,0:T(8,128)(2,1)S(1)} %get-tuple-element.41.cot, ...), custom_call_target="tpu_custom_call" | custom-call | flops 125829120 | bytes 1000000 | tf_op jit(solution)/shard_map/product/pallas_call | solution.py:25
  33.5 0.4 %collective-permute-done.13.new_other = bf16[24,5120]{1,0:T(8,128)(2,1)S(1)} collective-permute-done((bf16[24,5120]{1,0:T(8,128)(2,1)S(1)}, bf16[24,5120]{1,0:T(8,128)(2,1)S(1)}, u32[]{:S(2)}, u32[]{:S(2)}) %collective-permute-start.13) | collective-permute-done | bytes 245792 | tf_op jit(solution)/shard_map/ppermute | solution.py:46
  33.9 1.2 %last.1 = (bf16[48,5120]{1,0:T(8,128)(2,1)}, bf16[48,256]{1,0:T(8,128)(2,1)}, f32[3,5120]{1,0:T(4,128)}, f32[3,5120]{1,0:T(4,128)}, f32[3,5120]{1,0:T(4,128)}) custom-call(bf16[24,5120]{1,0:T(8,128)(2,1)S(1)} %across.1.new, bf16[24,5120]{1,0:T(8,128)(2,1)S(1)} %collective-permute-done.13.new_other, bf16[48,256]{1,0:T(8,128)(2,1)S(1)} %get-tuple-element.42.refs_0_, ...), custom_call_target="tpu_custom_call" | custom-call | flops 1000000 | bytes 1000000 | tf_op jit(solution)/shard_map/last/pallas_call | solution.py:25
  (19 shorter events, 0.3 us)
Async XLA Ops:
  0.6 3.8 %copy-start = (f32[3,5120]{1,0:T(4,128)S(1)}, f32[3,5120]{1,0:T(4,128)}, u32[]{:S(2)}) copy-start(f32[3,5120]{1,0:T(4,128)} %master.3) | copy-start | bytes 184324
  0.6 3.8 %copy-start.1 = (f32[3,5120]{1,0:T(4,128)S(1)}, f32[3,5120]{1,0:T(4,128)}, u32[]{:S(2)}) copy-start(f32[3,5120]{1,0:T(4,128)} %moment.3) | copy-start | bytes 184324
  0.7 3.8 %copy-start.2 = (f32[3,5120]{1,0:T(4,128)S(1)}, f32[3,5120]{1,0:T(4,128)}, u32[]{:S(2)}) copy-start(f32[3,5120]{1,0:T(4,128)} %second.3) | copy-start | bytes 184324
  2.8 1.7 %collective-permute-start = (bf16[24,5120]{1,0:T(8,128)(2,1)S(1)}, bf16[24,5120]{1,0:T(8,128)(2,1)S(1)}, u32[]{:S(2)}, u32[]{:S(2)}) collective-permute-start(bf16[24,5120]{1,0:T(8,128)(2,1)S(1)} %get-tuple-element.29), channel_id=1, source_target_pairs={{0,1},{1,0},{2,3},{3,2},{4,5},{5,4},{6,7},{7,6},{8,9},{9,8},{10,11... | collective-permute-start | bytes 737288 | tf_op jit(solution)/shard_map/ppermute | solution.py:46
  4.6 6.7 %collective-permute-start.2 = (bf16[24,1280]{1,0:T(8,128)(2,1)S(1)}, bf16[24,1280]{1,0:T(8,128)(2,1)S(1)}, u32[]{:S(2)}, u32[]{:S(2)}) collective-permute-start(bf16[24,1280]{1,0:T(8,128)(2,1)S(1)} %get-tuple-element.32), channel_id=1, source_target_pairs={{0,19},{1,18},{2,17},{3,16},{4,23},{5,22},{6,21},{7,20},{8,27},{9,... | collective-permute-start | bytes 184328 | tf_op jit(solution)/shard_map/ppermute | solution.py:46
  8.2 3.9 %collective-permute-start.3 = (bf16[24,1280]{1,0:T(8,128)(2,1)S(1)}, bf16[24,1280]{1,0:T(8,128)(2,1)S(1)}, u32[]{:S(2)}, u32[]{:S(2)}) collective-permute-start(bf16[24,1280]{1,0:T(8,128)(2,1)S(1)} %get-tuple-element.33), channel_id=1, source_target_pairs={{0,3},{1,2},{2,1},{3,0},{4,7},{5,6},{6,5},{7,4},{8,11},{9,10},{10,... | collective-permute-start | bytes 184328 | tf_op jit(solution)/shard_map/ppermute | solution.py:46
  8.7 4.2 %collective-permute-start.4 = (bf16[24,1280]{1,0:T(8,128)(2,1)S(1)}, bf16[24,1280]{1,0:T(8,128)(2,1)S(1)}, u32[]{:S(2)}, u32[]{:S(2)}) collective-permute-start(bf16[24,1280]{1,0:T(8,128)(2,1)S(1)} %get-tuple-element.34), channel_id=1, source_target_pairs={{0,16},{1,17},{2,18},{3,19},{4,20},{5,21},{6,22},{7,23},{8,24},{9,... | collective-permute-start | bytes 184328 | tf_op jit(solution)/shard_map/ppermute | solution.py:46
  8.9 10.1 %collective-permute-start.1 = (bf16[15,2560]{1,0:T(8,128)(2,1)S(1)}, bf16[15,2560]{1,0:T(8,128)(2,1)S(1)}, u32[]{:S(2)}, u32[]{:S(2)}) collective-permute-start(bf16[15,2560]{1,0:T(8,128)(2,1)S(1)} %get-tuple-element.30.state), channel_id=1, source_target_pairs={{0,9},{1,8},{2,11},{3,10},{4,13},{5,12},{6,15},{7,14},{8,1},{9,0},... | collective-permute-start | bytes 230408 | tf_op jit(solution)/shard_map/ppermute | solution.py:46
  13.0 3.9 %collective-permute-start.5 = (bf16[24,640]{1,0:T(8,128)(2,1)S(1)}, bf16[24,640]{1,0:T(8,128)(2,1)S(1)}, u32[]{:S(2)}, u32[]{:S(2)}) collective-permute-start(bf16[24,640]{1,0:T(8,128)(2,1)S(1)} %get-tuple-element.36), channel_id=1, source_target_pairs={{0,5},{1,4},{2,7},{3,6},{4,1},{5,0},{6,3},{7,2},{8,13},{9,12},{10,... | collective-permute-start | bytes 92168 | tf_op jit(solution)/shard_map/ppermute | solution.py:46
  16.9 4.4 %collective-permute-start.7 = (bf16[24,640]{1,0:T(8,128)(2,1)S(1)}, bf16[24,640]{1,0:T(8,128)(2,1)S(1)}, u32[]{:S(2)}, u32[]{:S(2)}) collective-permute-start(bf16[24,640]{1,0:T(8,128)(2,1)S(1)} %whole.1.refs_0_.mine), channel_id=1, source_target_pairs={{0,9},{1,8},{2,11},{3,10},{4,13},{5,12},{6,15},{7,14},{8,1},{9,0},... | collective-permute-start | bytes 92168 | tf_op jit(solution)/shard_map/ppermute | solution.py:46
  19.1 4.5 %collective-permute-start.6 = (bf16[24,1280]{1,0:T(8,128)(2,1)S(1)}, bf16[24,1280]{1,0:T(8,128)(2,1)S(1)}, u32[]{:S(2)}, u32[]{:S(2)}) collective-permute-start(bf16[24,1280]{1,0:T(8,128)(2,1)S(1)} %get-tuple-element.37.mine), channel_id=1, source_target_pairs={{0,5},{1,4},{2,7},{3,6},{4,1},{5,0},{6,3},{7,2},{8,13},{9,12},{10,... | collective-permute-start | bytes 184328 | tf_op jit(solution)/shard_map/ppermute | solution.py:46
  21.5 3.5 %collective-permute-start.9 = (bf16[24,640]{1,0:T(8,128)(2,1)S(1)}, bf16[24,640]{1,0:T(8,128)(2,1)S(1)}, u32[]{:S(2)}, u32[]{:S(2)}) collective-permute-start(bf16[24,640]{1,0:T(8,128)(2,1)S(1)} %get-tuple-element.40.mine), channel_id=1, source_target_pairs={{0,5},{1,4},{2,7},{3,6},{4,1},{5,0},{6,3},{7,2},{8,13},{9,12},{10,... | collective-permute-start | bytes 92168 | tf_op jit(solution)/shard_map/ppermute | solution.py:46
  23.7 6.1 %collective-permute-start.8 = (bf16[24,2560]{1,0:T(8,128)(2,1)S(1)}, bf16[24,2560]{1,0:T(8,128)(2,1)S(1)}, u32[]{:S(2)}, u32[]{:S(2)}) collective-permute-start(bf16[24,2560]{1,0:T(8,128)(2,1)S(1)} %join_old.2.mine), channel_id=1, source_target_pairs={{0,3},{1,2},{2,1},{3,0},{4,7},{5,6},{6,5},{7,4},{8,11},{9,10},{10,... | collective-permute-start | bytes 368648 | tf_op jit(solution)/shard_map/ppermute | solution.py:46
  25.0 6.1 %collective-permute-start.10 = (bf16[24,1280]{1,0:T(8,128)(2,1)S(1)}, bf16[24,1280]{1,0:T(8,128)(2,1)S(1)}, u32[]{:S(2)}, u32[]{:S(2)}) collective-permute-start(bf16[24,1280]{1,0:T(8,128)(2,1)S(1)} %copies.1.refs_1_), channel_id=1, source_target_pairs={{0,19},{1,18},{2,17},{3,16},{4,23},{5,22},{6,21},{7,20},{8,27},{9,... | collective-permute-start | bytes 184328 | tf_op jit(solution)/shard_map/ppermute | solution.py:46
  27.2 4.6 %collective-permute-start.11 = (bf16[24,1280]{1,0:T(8,128)(2,1)S(1)}, bf16[24,1280]{1,0:T(8,128)(2,1)S(1)}, u32[]{:S(2)}, u32[]{:S(2)}) collective-permute-start(bf16[24,1280]{1,0:T(8,128)(2,1)S(1)} %copies.1.refs_1_), channel_id=1, source_target_pairs={{0,3},{1,2},{2,1},{3,0},{4,7},{5,6},{6,5},{7,4},{8,11},{9,10},{10,... | collective-permute-start | bytes 184328 | tf_op jit(solution)/shard_map/ppermute | solution.py:46
  27.8 4.5 %collective-permute-start.12 = (bf16[24,1280]{1,0:T(8,128)(2,1)S(1)}, bf16[24,1280]{1,0:T(8,128)(2,1)S(1)}, u32[]{:S(2)}, u32[]{:S(2)}) collective-permute-start(bf16[24,1280]{1,0:T(8,128)(2,1)S(1)} %copies.1.refs_1_), channel_id=1, source_target_pairs={{0,16},{1,17},{2,18},{3,19},{4,20},{5,21},{6,22},{7,23},{8,24},{9,... | collective-permute-start | bytes 184328 | tf_op jit(solution)/shard_map/ppermute | solution.py:46
  28.3 4.2 %collective-permute-start.15 = (bf16[3,2560]{1,0:T(4,128)(2,1)S(1)}, bf16[3,2560]{1,0:T(4,128)(2,1)S(1)}, u32[]{:S(2)}, u32[]{:S(2)}) collective-permute-start(bf16[3,2560]{1,0:T(4,128)(2,1)S(1)} %get-tuple-element.39.refs_0_), channel_id=1, source_target_pairs={{0,16},{1,17},{2,18},{3,19},{4,20},{5,21},{6,22},{7,23},{8,24},{9,... | collective-permute-start | bytes 46088 | tf_op jit(solution)/shard_map/ppermute | solution.py:46
  29.9 2.6 %collective-permute-start.14 = (bf16[24,5120]{1,0:T(8,128)(2,1)S(1)}, bf16[24,5120]{1,0:T(8,128)(2,1)S(1)}, u32[]{:S(2)}, u32[]{:S(2)}) collective-permute-start(bf16[24,5120]{1,0:T(8,128)(2,1)S(1)} %join_old.3.refs_0_.old), channel_id=1, source_target_pairs={{0,1},{1,0},{2,3},{3,2},{4,5},{5,4},{6,7},{7,6},{8,9},{9,8},{10,11... | collective-permute-start | bytes 737288 | tf_op jit(solution)/shard_map/ppermute | solution.py:46
  32.3 1.6 %collective-permute-start.13 = (bf16[24,5120]{1,0:T(8,128)(2,1)S(1)}, bf16[24,5120]{1,0:T(8,128)(2,1)S(1)}, u32[]{:S(2)}, u32[]{:S(2)}) collective-permute-start(bf16[24,5120]{1,0:T(8,128)(2,1)S(1)} %across.1.new), channel_id=1, source_target_pairs={{0,1},{1,0},{2,3},{3,2},{4,5},{5,4},{6,7},{7,6},{8,9},{9,8},{10,11... | collective-permute-start | bytes 737288 | tf_op jit(solution)/shard_map/ppermute | solution.py:46

commit v5 on v3

--- a/solution.py
+++ b/solution.py
@@ -255,7 +255,7 @@
     far = [1 << i for i in range(high.bit_length() - 1)]
     halved, last = far[:-1], far[-1]
     near = sorted(((dx, low) for dx in range(reps) for low in range(LOW)),
-                  key=lambda c: (c != (0, 0), -bool(c[0]) - bool(c[1]), c))
+                  key=lambda c: (c != (0, 0), -bool(c[0]) - bool(c[1]), c[::-1]))
     states = (master, moment, second)
 
     ins = [pltpu.with_memory_space_constraint(x, pltpu.HBM) for x in (hidden.T, cotangent)]

time: 35.3 us -> 34.6 us (0.980)
  starting transfers between devices: 21.7 us -> 21 us
    ppermute x16, starting transfers between devices: 21.7 us -> 21 us  [swap(): lax.ppermute(value, (*CHIPS, 'core'), [(i, i ^ bits) for i in range(count)])]
  transfers between devices with their start and end apart: 16 -> 16, of which waited for: 9 -> 9; matrix products, arithmetic and copies ran while one was open for 0% -> 0% of each run, Pallas kernels for 4% -> 5%
where the time goes in v5:
time: 34.6 us; the launch traced here: 34.4 us
  starting transfers between devices  21 us (61%)
  waiting for transfers between devices  7.72 us (22%)
  Pallas kernels  5.02 us (15%)
  between operations  0.73 us (2%)
    ppermute x16, starting transfers between devices, swap(): lax.ppermute(value, (*CHIPS, 'core'), [(i, i ^ bits) for i in range(count)])  21 us
    ppermute x16, waiting for transfers between devices, swap(): lax.ppermute(value, (*CHIPS, 'core'), [(i, i ^ bits) for i in range(count)])  7.72 us
    pallas_call x13, Pallas kernels, call(): pl.pallas_call(body, out_shape=tuple((jax.ShapeDtypeStruct(*out) for out...  5.02 us
  transfers between devices with their start and end apart: 16, of which 9 were waited for; matrix products, arithmetic and copies ran while one was open for 0% of the time, Pallas kernels for 5%

profile of v5, /device:TPU:0, one launch (start us, length us, event | category | flops | bytes accessed | tf_op | source)
XLA Modules:
  0.0 34.4 jit_solution(17416185505877390771)
XLA Ops:
  0.7 2.1 %partial.1 = (f32[24,5120]{1,0:T(8,128)S(1)}, bf16[24,5120]{1,0:T(8,128)(2,1)S(1)}, bf16[256,5120]{1,0:T(8,128)(2,1)S(1)}) custom-call(bf16[48,256]{1,0:T(8,128)(2,1)} %bitcast.2, bf16[256,5120]{1,0:T(8,128)(2,1)} %cot_hbm.1), custom_call_target="tpu_custom_call" | custom-call | flops 125829120 | bytes 1000000 | tf_op jit(solution)/shard_map/partial/pallas_call | solution.py:24
  2.8 0.5 %collective-permute-start = (bf16[24,5120]{1,0:T(8,128)(2,1)S(1)}, bf16[24,5120]{1,0:T(8,128)(2,1)S(1)}, u32[]{:S(2)}, u32[]{:S(2)}) collective-permute-start(bf16[24,5120]{1,0:T(8,128)(2,1)S(1)} %get-tuple-element.29), channel_id=1, source_target_pairs={{0,1},{1,0},{2,3},{3,2},{4,5},{5,4},{6,7},{7,6},{8,9},{9,8},{10,11... | collective-permute-start | bytes 737288 | tf_op jit(solution)/shard_map/ppermute | solution.py:45
  3.3 1.1 %collective-permute-done.recv_ref = bf16[24,5120]{1,0:T(8,128)(2,1)S(1)} collective-permute-done((bf16[24,5120]{1,0:T(8,128)(2,1)S(1)}, bf16[24,5120]{1,0:T(8,128)(2,1)S(1)}, u32[]{:S(2)}, u32[]{:S(2)}) %collective-permute-start) | collective-permute-done | bytes 245792 | tf_op jit(solution)/shard_map/ppermute | solution.py:45
  4.5 0.1 middle.1
  4.6 3.6 %collective-permute-start.2 = (bf16[24,1280]{1,0:T(8,128)(2,1)S(1)}, bf16[24,1280]{1,0:T(8,128)(2,1)S(1)}, u32[]{:S(2)}, u32[]{:S(2)}) collective-permute-start(bf16[24,1280]{1,0:T(8,128)(2,1)S(1)} %get-tuple-element.32), channel_id=1, source_target_pairs={{0,19},{1,18},{2,17},{3,16},{4,23},{5,22},{6,21},{7,20},{8,27},{9,... | collective-permute-start | bytes 184328 | tf_op jit(solution)/shard_map/ppermute | solution.py:45
  8.2 0.6 %collective-permute-start.3 = (bf16[24,1280]{1,0:T(8,128)(2,1)S(1)}, bf16[24,1280]{1,0:T(8,128)(2,1)S(1)}, u32[]{:S(2)}, u32[]{:S(2)}) collective-permute-start(bf16[24,1280]{1,0:T(8,128)(2,1)S(1)} %get-tuple-element.33), channel_id=1, source_target_pairs={{0,16},{1,17},{2,18},{3,19},{4,20},{5,21},{6,22},{7,23},{8,24},{9,... | collective-permute-start | bytes 184328 | tf_op jit(solution)/shard_map/ppermute | solution.py:45
  8.8 2.8 %collective-permute-start.1 = (bf16[15,2560]{1,0:T(8,128)(2,1)S(1)}, bf16[15,2560]{1,0:T(8,128)(2,1)S(1)}, u32[]{:S(2)}, u32[]{:S(2)}) collective-permute-start(bf16[15,2560]{1,0:T(8,128)(2,1)S(1)} %get-tuple-element.30.state), channel_id=1, source_target_pairs={{0,9},{1,8},{2,11},{3,10},{4,13},{5,12},{6,15},{7,14},{8,1},{9,0},... | collective-permute-start | bytes 230408 | tf_op jit(solution)/shard_map/ppermute | solution.py:45
  11.6 1.0 %collective-permute-done.3.refs_2_ = bf16[24,1280]{1,0:T(8,128)(2,1)S(1)} collective-permute-done((bf16[24,1280]{1,0:T(8,128)(2,1)S(1)}, bf16[24,1280]{1,0:T(8,128)(2,1)S(1)}, u32[]{:S(2)}, u32[]{:S(2)}) %collective-permute-start.3) | collective-permute-done | bytes 61472 | tf_op jit(solution)/shard_map/ppermute | solution.py:45
  12.6 0.2 collective-permute-done.4.refs_3_
  12.9 1.6 %collective-permute-start.5 = (bf16[24,640]{1,0:T(8,128)(2,1)S(1)}, bf16[24,640]{1,0:T(8,128)(2,1)S(1)}, u32[]{:S(2)}, u32[]{:S(2)}) collective-permute-start(bf16[24,640]{1,0:T(8,128)(2,1)S(1)} %get-tuple-element.36), channel_id=1, source_target_pairs={{0,5},{1,4},{2,7},{3,6},{4,1},{5,0},{6,3},{7,2},{8,13},{9,12},{10,... | collective-permute-start | bytes 92168 | tf_op jit(solution)/shard_map/ppermute | solution.py:45
  14.5 2.4 %collective-permute-done.5.other = bf16[24,640]{1,0:T(8,128)(2,1)S(1)} collective-permute-done((bf16[24,640]{1,0:T(8,128)(2,1)S(1)}, bf16[24,640]{1,0:T(8,128)(2,1)S(1)}, u32[]{:S(2)}, u32[]{:S(2)}) %collective-permute-start.5) | collective-permute-done | bytes 30752 | tf_op jit(solution)/shard_map/ppermute | solution.py:45
  16.9 2.0 %collective-permute-start.7 = (bf16[24,640]{1,0:T(8,128)(2,1)S(1)}, bf16[24,640]{1,0:T(8,128)(2,1)S(1)}, u32[]{:S(2)}, u32[]{:S(2)}) collective-permute-start(bf16[24,640]{1,0:T(8,128)(2,1)S(1)} %whole.1.refs_0_.mine), channel_id=1, source_target_pairs={{0,9},{1,8},{2,11},{3,10},{4,13},{5,12},{6,15},{7,14},{8,1},{9,0},... | collective-permute-start | bytes 92168 | tf_op jit(solution)/shard_map/ppermute | solution.py:45
  18.9 0.1 arrange.1
  19.0 1.8 %collective-permute-start.6 = (bf16[24,1280]{1,0:T(8,128)(2,1)S(1)}, bf16[24,1280]{1,0:T(8,128)(2,1)S(1)}, u32[]{:S(2)}, u32[]{:S(2)}) collective-permute-start(bf16[24,1280]{1,0:T(8,128)(2,1)S(1)} %get-tuple-element.37.mine), channel_id=1, source_target_pairs={{0,5},{1,4},{2,7},{3,6},{4,1},{5,0},{6,3},{7,2},{8,13},{9,12},{10,... | collective-permute-start | bytes 184328 | tf_op jit(solution)/shard_map/ppermute | solution.py:45
  20.9 0.3 collective-permute-done.7.other
  21.2 0.1 own.1
  21.3 1.1 %collective-permute-start.9 = (bf16[24,640]{1,0:T(8,128)(2,1)S(1)}, bf16[24,640]{1,0:T(8,128)(2,1)S(1)}, u32[]{:S(2)}, u32[]{:S(2)}) collective-permute-start(bf16[24,640]{1,0:T(8,128)(2,1)S(1)} %get-tuple-element.40.mine), channel_id=1, source_target_pairs={{0,5},{1,4},{2,7},{3,6},{4,1},{5,0},{6,3},{7,2},{8,13},{9,12},{10,... | collective-permute-start | bytes 92168 | tf_op jit(solution)/shard_map/ppermute | solution.py:45
  22.4 0.6 %collective-permute-done.6.other = bf16[24,1280]{1,0:T(8,128)(2,1)S(1)} collective-permute-done((bf16[24,1280]{1,0:T(8,128)(2,1)S(1)}, bf16[24,1280]{1,0:T(8,128)(2,1)S(1)}, u32[]{:S(2)}, u32[]{:S(2)}) %collective-permute-start.6) | collective-permute-done | bytes 61472 | tf_op jit(solution)/shard_map/ppermute | solution.py:45
  23.1 0.1 join_old.2.mine
  23.1 1.5 %collective-permute-start.8 = (bf16[24,2560]{1,0:T(8,128)(2,1)S(1)}, bf16[24,2560]{1,0:T(8,128)(2,1)S(1)}, u32[]{:S(2)}, u32[]{:S(2)}) collective-permute-start(bf16[24,2560]{1,0:T(8,128)(2,1)S(1)} %join_old.2.mine), channel_id=1, source_target_pairs={{0,3},{1,2},{2,1},{3,0},{4,7},{5,6},{6,5},{7,4},{8,11},{9,10},{10,... | collective-permute-start | bytes 368648 | tf_op jit(solution)/shard_map/ppermute | solution.py:45
  24.7 2.2 %collective-permute-start.10 = (bf16[24,1280]{1,0:T(8,128)(2,1)S(1)}, bf16[24,1280]{1,0:T(8,128)(2,1)S(1)}, u32[]{:S(2)}, u32[]{:S(2)}) collective-permute-start(bf16[24,1280]{1,0:T(8,128)(2,1)S(1)} %copies.1.refs_1_), channel_id=1, source_target_pairs={{0,19},{1,18},{2,17},{3,16},{4,23},{5,22},{6,21},{7,20},{8,27},{9,... | collective-permute-start | bytes 184328 | tf_op jit(solution)/shard_map/ppermute | solution.py:45
  26.9 0.6 %collective-permute-start.11 = (bf16[24,1280]{1,0:T(8,128)(2,1)S(1)}, bf16[24,1280]{1,0:T(8,128)(2,1)S(1)}, u32[]{:S(2)}, u32[]{:S(2)}) collective-permute-start(bf16[24,1280]{1,0:T(8,128)(2,1)S(1)} %copies.1.refs_1_), channel_id=1, source_target_pairs={{0,16},{1,17},{2,18},{3,19},{4,20},{5,21},{6,22},{7,23},{8,24},{9,... | collective-permute-start | bytes 184328 | tf_op jit(solution)/shard_map/ppermute | solution.py:45
  27.5 0.2 collective-permute-start.12
  27.7 1.5 %collective-permute-start.15 = (bf16[3,2560]{1,0:T(4,128)(2,1)S(1)}, bf16[3,2560]{1,0:T(4,128)(2,1)S(1)}, u32[]{:S(2)}, u32[]{:S(2)}) collective-permute-start(bf16[3,2560]{1,0:T(4,128)(2,1)S(1)} %get-tuple-element.39.refs_0_), channel_id=1, source_target_pairs={{0,16},{1,17},{2,18},{3,19},{4,20},{5,21},{6,22},{7,23},{8,24},{9,... | collective-permute-start | bytes 46088 | tf_op jit(solution)/shard_map/ppermute | solution.py:45
  29.3 0.3 collective-permute-done.8.other
  29.6 0.1 join_old.3.refs_0_.old
  29.6 0.4 %collective-permute-start.14 = (bf16[24,5120]{1,0:T(8,128)(2,1)S(1)}, bf16[24,5120]{1,0:T(8,128)(2,1)S(1)}, u32[]{:S(2)}, u32[]{:S(2)}) collective-permute-start(bf16[24,5120]{1,0:T(8,128)(2,1)S(1)} %join_old.3.refs_0_.old), channel_id=1, source_target_pairs={{0,1},{1,0},{2,3},{3,2},{4,5},{5,4},{6,7},{7,6},{8,9},{9,8},{10,11... | collective-permute-start | bytes 737288 | tf_op jit(solution)/shard_map/ppermute | solution.py:45
  30.0 1.6 %collective-permute-done.11.refs_3_ = bf16[24,1280]{1,0:T(8,128)(2,1)S(1)} collective-permute-done((bf16[24,1280]{1,0:T(8,128)(2,1)S(1)}, bf16[24,1280]{1,0:T(8,128)(2,1)S(1)}, u32[]{:S(2)}, u32[]{:S(2)}) %collective-permute-start.11) | collective-permute-done | bytes 61472 | tf_op jit(solution)/shard_map/ppermute | solution.py:45
  31.7 0.4 %collective-permute-start.13 = (bf16[24,5120]{1,0:T(8,128)(2,1)S(1)}, bf16[24,5120]{1,0:T(8,128)(2,1)S(1)}, u32[]{:S(2)}, u32[]{:S(2)}) collective-permute-start(bf16[24,5120]{1,0:T(8,128)(2,1)S(1)} %across.1.new), channel_id=1, source_target_pairs={{0,1},{1,0},{2,3},{3,2},{4,5},{5,4},{6,7},{7,6},{8,9},{9,8},{10,11... | collective-permute-start | bytes 737288 | tf_op jit(solution)/shard_map/ppermute | solution.py:45
  32.1 1.0 %product.1 = (bf16[48,256]{1,0:T(8,128)(2,1)S(1)}, f32[3,5120]{1,0:T(4,128)S(1)}, f32[3,5120]{1,0:T(4,128)S(1)}, f32[3,5120]{1,0:T(4,128)S(1)}) custom-call(bf16[24,5120]{1,0:T(8,128)(2,1)S(1)} %join_old.3.refs_0_.old, bf16[24,5120]{1,0:T(8,128)(2,1)S(1)} %collective-permute-done.14.old_other, bf16[256,5120]{1,0:T(8,128)(2,1)S(1)} %get-tuple-element.41.cot, ...), custom_call_target="tpu_custom_call" | custom-call | flops 125829120 | bytes 1000000 | tf_op jit(solution)/shard_map/product/pallas_call | solution.py:24
  33.1 0.1 collective-permute-done.13.new_other
  33.2 1.2 %last.1 = (bf16[48,5120]{1,0:T(8,128)(2,1)}, bf16[48,256]{1,0:T(8,128)(2,1)}, f32[3,5120]{1,0:T(4,128)}, f32[3,5120]{1,0:T(4,128)}, f32[3,5120]{1,0:T(4,128)}) custom-call(bf16[24,5120]{1,0:T(8,128)(2,1)S(1)} %across.1.new, bf16[24,5120]{1,0:T(8,128)(2,1)S(1)} %collective-permute-done.13.new_other, bf16[48,256]{1,0:T(8,128)(2,1)S(1)} %get-tuple-element.42.refs_0_, ...), custom_call_target="tpu_custom_call" | custom-call | flops 1000000 | bytes 1000000 | tf_op jit(solution)/shard_map/last/pallas_call | solution.py:24
  (19 shorter events, 0.2 us)
Async XLA Ops:
  0.6 3.8 %copy-start = (f32[3,5120]{1,0:T(4,128)S(1)}, f32[3,5120]{1,0:T(4,128)}, u32[]{:S(2)}) copy-start(f32[3,5120]{1,0:T(4,128)} %master.3) | copy-start | bytes 184324
  0.6 3.8 %copy-start.1 = (f32[3,5120]{1,0:T(4,128)S(1)}, f32[3,5120]{1,0:T(4,128)}, u32[]{:S(2)}) copy-start(f32[3,5120]{1,0:T(4,128)} %moment.3) | copy-start | bytes 184324
  0.7 3.8 %copy-start.2 = (f32[3,5120]{1,0:T(4,128)S(1)}, f32[3,5120]{1,0:T(4,128)}, u32[]{:S(2)}) copy-start(f32[3,5120]{1,0:T(4,128)} %second.3) | copy-start | bytes 184324
  2.8 1.7 %collective-permute-start = (bf16[24,5120]{1,0:T(8,128)(2,1)S(1)}, bf16[24,5120]{1,0:T(8,128)(2,1)S(1)}, u32[]{:S(2)}, u32[]{:S(2)}) collective-permute-start(bf16[24,5120]{1,0:T(8,128)(2,1)S(1)} %get-tuple-element.29), channel_id=1, source_target_pairs={{0,1},{1,0},{2,3},{3,2},{4,5},{5,4},{6,7},{7,6},{8,9},{9,8},{10,11... | collective-permute-start | bytes 737288 | tf_op jit(solution)/shard_map/ppermute | solution.py:45
  4.6 7.0 %collective-permute-start.2 = (bf16[24,1280]{1,0:T(8,128)(2,1)S(1)}, bf16[24,1280]{1,0:T(8,128)(2,1)S(1)}, u32[]{:S(2)}, u32[]{:S(2)}) collective-permute-start(bf16[24,1280]{1,0:T(8,128)(2,1)S(1)} %get-tuple-element.32), channel_id=1, source_target_pairs={{0,19},{1,18},{2,17},{3,16},{4,23},{5,22},{6,21},{7,20},{8,27},{9,... | collective-permute-start | bytes 184328 | tf_op jit(solution)/shard_map/ppermute | solution.py:45
  8.2 4.4 %collective-permute-start.3 = (bf16[24,1280]{1,0:T(8,128)(2,1)S(1)}, bf16[24,1280]{1,0:T(8,128)(2,1)S(1)}, u32[]{:S(2)}, u32[]{:S(2)}) collective-permute-start(bf16[24,1280]{1,0:T(8,128)(2,1)S(1)} %get-tuple-element.33), channel_id=1, source_target_pairs={{0,16},{1,17},{2,18},{3,19},{4,20},{5,21},{6,22},{7,23},{8,24},{9,... | collective-permute-start | bytes 184328 | tf_op jit(solution)/shard_map/ppermute | solution.py:45
  8.8 4.0 %collective-permute-start.4 = (bf16[24,1280]{1,0:T(8,128)(2,1)S(1)}, bf16[24,1280]{1,0:T(8,128)(2,1)S(1)}, u32[]{:S(2)}, u32[]{:S(2)}) collective-permute-start(bf16[24,1280]{1,0:T(8,128)(2,1)S(1)} %get-tuple-element.34), channel_id=1, source_target_pairs={{0,3},{1,2},{2,1},{3,0},{4,7},{5,6},{6,5},{7,4},{8,11},{9,10},{10,... | collective-permute-start | bytes 184328 | tf_op jit(solution)/shard_map/ppermute | solution.py:45
  8.8 10.1 %collective-permute-start.1 = (bf16[15,2560]{1,0:T(8,128)(2,1)S(1)}, bf16[15,2560]{1,0:T(8,128)(2,1)S(1)}, u32[]{:S(2)}, u32[]{:S(2)}) collective-permute-start(bf16[15,2560]{1,0:T(8,128)(2,1)S(1)} %get-tuple-element.30.state), channel_id=1, source_target_pairs={{0,9},{1,8},{2,11},{3,10},{4,13},{5,12},{6,15},{7,14},{8,1},{9,0},... | collective-permute-start | bytes 230408 | tf_op jit(solution)/shard_map/ppermute | solution.py:45
  12.9 4.0 %collective-permute-start.5 = (bf16[24,640]{1,0:T(8,128)(2,1)S(1)}, bf16[24,640]{1,0:T(8,128)(2,1)S(1)}, u32[]{:S(2)}, u32[]{:S(2)}) collective-permute-start(bf16[24,640]{1,0:T(8,128)(2,1)S(1)} %get-tuple-element.36), channel_id=1, source_target_pairs={{0,5},{1,4},{2,7},{3,6},{4,1},{5,0},{6,3},{7,2},{8,13},{9,12},{10,... | collective-permute-start | bytes 92168 | tf_op jit(solution)/shard_map/ppermute | solution.py:45
  16.9 4.3 %collective-permute-start.7 = (bf16[24,640]{1,0:T(8,128)(2,1)S(1)}, bf16[24,640]{1,0:T(8,128)(2,1)S(1)}, u32[]{:S(2)}, u32[]{:S(2)}) collective-permute-start(bf16[24,640]{1,0:T(8,128)(2,1)S(1)} %whole.1.refs_0_.mine), channel_id=1, source_target_pairs={{0,9},{1,8},{2,11},{3,10},{4,13},{5,12},{6,15},{7,14},{8,1},{9,0},... | collective-permute-start | bytes 92168 | tf_op jit(solution)/shard_map/ppermute | solution.py:45
  19.0 4.0 %collective-permute-start.6 = (bf16[24,1280]{1,0:T(8,128)(2,1)S(1)}, bf16[24,1280]{1,0:T(8,128)(2,1)S(1)}, u32[]{:S(2)}, u32[]{:S(2)}) collective-permute-start(bf16[24,1280]{1,0:T(8,128)(2,1)S(1)} %get-tuple-element.37.mine), channel_id=1, source_target_pairs={{0,5},{1,4},{2,7},{3,6},{4,1},{5,0},{6,3},{7,2},{8,13},{9,12},{10,... | collective-permute-start | bytes 184328 | tf_op jit(solution)/shard_map/ppermute | solution.py:45
  21.3 3.4 %collective-permute-start.9 = (bf16[24,640]{1,0:T(8,128)(2,1)S(1)}, bf16[24,640]{1,0:T(8,128)(2,1)S(1)}, u32[]{:S(2)}, u32[]{:S(2)}) collective-permute-start(bf16[24,640]{1,0:T(8,128)(2,1)S(1)} %get-tuple-element.40.mine), channel_id=1, source_target_pairs={{0,5},{1,4},{2,7},{3,6},{4,1},{5,0},{6,3},{7,2},{8,13},{9,12},{10,... | collective-permute-start | bytes 92168 | tf_op jit(solution)/shard_map/ppermute | solution.py:45
  23.1 6.4 %collective-permute-start.8 = (bf16[24,2560]{1,0:T(8,128)(2,1)S(1)}, bf16[24,2560]{1,0:T(8,128)(2,1)S(1)}, u32[]{:S(2)}, u32[]{:S(2)}) collective-permute-start(bf16[24,2560]{1,0:T(8,128)(2,1)S(1)} %join_old.2.mine), channel_id=1, source_target_pairs={{0,3},{1,2},{2,1},{3,0},{4,7},{5,6},{6,5},{7,4},{8,11},{9,10},{10,... | collective-permute-start | bytes 368648 | tf_op jit(solution)/shard_map/ppermute | solution.py:45
  24.7 5.3 %collective-permute-start.10 = (bf16[24,1280]{1,0:T(8,128)(2,1)S(1)}, bf16[24,1280]{1,0:T(8,128)(2,1)S(1)}, u32[]{:S(2)}, u32[]{:S(2)}) collective-permute-start(bf16[24,1280]{1,0:T(8,128)(2,1)S(1)} %copies.1.refs_1_), channel_id=1, source_target_pairs={{0,19},{1,18},{2,17},{3,16},{4,23},{5,22},{6,21},{7,20},{8,27},{9,... | collective-permute-start | bytes 184328 | tf_op jit(solution)/shard_map/ppermute | solution.py:45
  26.9 4.7 %collective-permute-start.11 = (bf16[24,1280]{1,0:T(8,128)(2,1)S(1)}, bf16[24,1280]{1,0:T(8,128)(2,1)S(1)}, u32[]{:S(2)}, u32[]{:S(2)}) collective-permute-start(bf16[24,1280]{1,0:T(8,128)(2,1)S(1)} %copies.1.refs_1_), channel_id=1, source_target_pairs={{0,16},{1,17},{2,18},{3,19},{4,20},{5,21},{6,22},{7,23},{8,24},{9,... | collective-permute-start | bytes 184328 | tf_op jit(solution)/shard_map/ppermute | solution.py:45
  27.5 4.1 %collective-permute-start.12 = (bf16[24,1280]{1,0:T(8,128)(2,1)S(1)}, bf16[24,1280]{1,0:T(8,128)(2,1)S(1)}, u32[]{:S(2)}, u32[]{:S(2)}) collective-permute-start(bf16[24,1280]{1,0:T(8,128)(2,1)S(1)} %copies.1.refs_1_), channel_id=1, source_target_pairs={{0,3},{1,2},{2,1},{3,0},{4,7},{5,6},{6,5},{7,4},{8,11},{9,10},{10,... | collective-permute-start | bytes 184328 | tf_op jit(solution)/shard_map/ppermute | solution.py:45
  27.7 4.3 %collective-permute-start.15 = (bf16[3,2560]{1,0:T(4,128)(2,1)S(1)}, bf16[3,2560]{1,0:T(4,128)(2,1)S(1)}, u32[]{:S(2)}, u32[]{:S(2)}) collective-permute-start(bf16[3,2560]{1,0:T(4,128)(2,1)S(1)} %get-tuple-element.39.refs_0_), channel_id=1, source_target_pairs={{0,16},{1,17},{2,18},{3,19},{4,20},{5,21},{6,22},{7,23},{8,24},{9,... | collective-permute-start | bytes 46088 | tf_op jit(solution)/shard_map/ppermute | solution.py:45
  29.6 2.4 %collective-permute-start.14 = (bf16[24,5120]{1,0:T(8,128)(2,1)S(1)}, bf16[24,5120]{1,0:T(8,128)(2,1)S(1)}, u32[]{:S(2)}, u32[]{:S(2)}) collective-permute-start(bf16[24,5120]{1,0:T(8,128)(2,1)S(1)} %join_old.3.refs_0_.old), channel_id=1, source_target_pairs={{0,1},{1,0},{2,3},{3,2},{4,5},{5,4},{6,7},{7,6},{8,9},{9,8},{10,11... | collective-permute-start | bytes 737288 | tf_op jit(solution)/shard_map/ppermute | solution.py:45
  31.7 1.6 %collective-permute-start.13 = (bf16[24,5120]{1,0:T(8,128)(2,1)S(1)}, bf16[24,5120]{1,0:T(8,128)(2,1)S(1)}, u32[]{:S(2)}, u32[]{:S(2)}) collective-permute-start(bf16[24,5120]{1,0:T(8,128)(2,1)S(1)} %across.1.new), channel_id=1, source_target_pairs={{0,1},{1,0},{2,3},{3,2},{4,5},{5,4},{6,7},{7,6},{8,9},{9,8},{10,11... | collective-permute-start | bytes 737288 | tf_op jit(solution)/shard_map/ppermute | solution.py:45

commit v6 on v5

--- a/solution.py
+++ b/solution.py
@@ -229,9 +229,7 @@
 
 def last_body(per, high, new, new_other, *refs):
     held, outs, (out, sems) = refs[:4], refs[4:9], refs[9:]
-    copies = [pltpu.make_async_copy(a, b, sems.at[i]) for i, (a, b) in enumerate(zip(held, outs[1:]))]
-    for copy in copies:
-        copy.start()
+    copies = []
     move = one_hot(out.shape[0], per, high)
     tile = out.shape[1] // OUT_COPIES
     half = new.shape[0]
@@ -241,6 +239,9 @@
         out[:, cols] = chunk.astype(BF16)
         copies.append(pltpu.make_async_copy(out.at[:, cols], outs[0].at[:, cols], sems.at[4 + i]))
         copies[-1].start()
+        if i < len(held):
+            copies.append(pltpu.make_async_copy(held[i], outs[1 + i], sems.at[i]))
+            copies[-1].start()
     for copy in copies:
         copy.wait()
 

time: 34.6 us -> 34.6 us (level)
  no operation moved by 1% of the time
where the time goes in v6:
time: 34.6 us; the launch traced here: 34.5 us
  starting transfers between devices  21 us (61%)
  waiting for transfers between devices  7.72 us (22%)
  Pallas kernels  5.05 us (15%)
  between operations  0.73 us (2%)
    ppermute x16, starting transfers between devices, swap(): lax.ppermute(value, (*CHIPS, 'core'), [(i, i ^ bits) for i in range(count)])  21 us
    ppermute x16, waiting for transfers between devices, swap(): lax.ppermute(value, (*CHIPS, 'core'), [(i, i ^ bits) for i in range(count)])  7.72 us
    pallas_call x13, Pallas kernels, call(): pl.pallas_call(body, out_shape=tuple((jax.ShapeDtypeStruct(*out) for out...  5.05 us
  transfers between devices with their start and end apart: 16, of which 9 were waited for; matrix products, arithmetic and copies ran while one was open for 0% of the time, Pallas kernels for 5%

profile of v6, /device:TPU:0, one launch (start us, length us, event | category | flops | bytes accessed | tf_op | source)
XLA Modules:
  0.0 34.5 jit_solution(10656172310921560262)
XLA Ops:
  0.7 2.1 %partial.1 = (f32[24,5120]{1,0:T(8,128)S(1)}, bf16[24,5120]{1,0:T(8,128)(2,1)S(1)}, bf16[256,5120]{1,0:T(8,128)(2,1)S(1)}) custom-call(bf16[48,256]{1,0:T(8,128)(2,1)} %bitcast.2, bf16[256,5120]{1,0:T(8,128)(2,1)} %cot_hbm.1), custom_call_target="tpu_custom_call" | custom-call | flops 125829120 | bytes 1000000 | tf_op jit(solution)/shard_map/partial/pallas_call | solution.py:24
  2.8 0.5 %collective-permute-start = (bf16[24,5120]{1,0:T(8,128)(2,1)S(1)}, bf16[24,5120]{1,0:T(8,128)(2,1)S(1)}, u32[]{:S(2)}, u32[]{:S(2)}) collective-permute-start(bf16[24,5120]{1,0:T(8,128)(2,1)S(1)} %get-tuple-element.29), channel_id=1, source_target_pairs={{0,1},{1,0},{2,3},{3,2},{4,5},{5,4},{6,7},{7,6},{8,9},{9,8},{10,11... | collective-permute-start | bytes 737288 | tf_op jit(solution)/shard_map/ppermute | solution.py:45
  3.3 1.1 %collective-permute-done.recv_ref = bf16[24,5120]{1,0:T(8,128)(2,1)S(1)} collective-permute-done((bf16[24,5120]{1,0:T(8,128)(2,1)S(1)}, bf16[24,5120]{1,0:T(8,128)(2,1)S(1)}, u32[]{:S(2)}, u32[]{:S(2)}) %collective-permute-start) | collective-permute-done | bytes 245792 | tf_op jit(solution)/shard_map/ppermute | solution.py:45
  4.5 0.1 middle.1
  4.6 3.6 %collective-permute-start.2 = (bf16[24,1280]{1,0:T(8,128)(2,1)S(1)}, bf16[24,1280]{1,0:T(8,128)(2,1)S(1)}, u32[]{:S(2)}, u32[]{:S(2)}) collective-permute-start(bf16[24,1280]{1,0:T(8,128)(2,1)S(1)} %get-tuple-element.32), channel_id=1, source_target_pairs={{0,19},{1,18},{2,17},{3,16},{4,23},{5,22},{6,21},{7,20},{8,27},{9,... | collective-permute-start | bytes 184328 | tf_op jit(solution)/shard_map/ppermute | solution.py:45
  8.2 0.6 %collective-permute-start.3 = (bf16[24,1280]{1,0:T(8,128)(2,1)S(1)}, bf16[24,1280]{1,0:T(8,128)(2,1)S(1)}, u32[]{:S(2)}, u32[]{:S(2)}) collective-permute-start(bf16[24,1280]{1,0:T(8,128)(2,1)S(1)} %get-tuple-element.33), channel_id=1, source_target_pairs={{0,16},{1,17},{2,18},{3,19},{4,20},{5,21},{6,22},{7,23},{8,24},{9,... | collective-permute-start | bytes 184328 | tf_op jit(solution)/shard_map/ppermute | solution.py:45
  8.8 2.8 %collective-permute-start.1 = (bf16[15,2560]{1,0:T(8,128)(2,1)S(1)}, bf16[15,2560]{1,0:T(8,128)(2,1)S(1)}, u32[]{:S(2)}, u32[]{:S(2)}) collective-permute-start(bf16[15,2560]{1,0:T(8,128)(2,1)S(1)} %get-tuple-element.30.state), channel_id=1, source_target_pairs={{0,9},{1,8},{2,11},{3,10},{4,13},{5,12},{6,15},{7,14},{8,1},{9,0},... | collective-permute-start | bytes 230408 | tf_op jit(solution)/shard_map/ppermute | solution.py:45
  11.6 1.0 %collective-permute-done.3.refs_2_ = bf16[24,1280]{1,0:T(8,128)(2,1)S(1)} collective-permute-done((bf16[24,1280]{1,0:T(8,128)(2,1)S(1)}, bf16[24,1280]{1,0:T(8,128)(2,1)S(1)}, u32[]{:S(2)}, u32[]{:S(2)}) %collective-permute-start.3) | collective-permute-done | bytes 61472 | tf_op jit(solution)/shard_map/ppermute | solution.py:45
  12.6 0.2 collective-permute-done.4.refs_3_
  12.9 1.6 %collective-permute-start.5 = (bf16[24,640]{1,0:T(8,128)(2,1)S(1)}, bf16[24,640]{1,0:T(8,128)(2,1)S(1)}, u32[]{:S(2)}, u32[]{:S(2)}) collective-permute-start(bf16[24,640]{1,0:T(8,128)(2,1)S(1)} %get-tuple-element.36), channel_id=1, source_target_pairs={{0,5},{1,4},{2,7},{3,6},{4,1},{5,0},{6,3},{7,2},{8,13},{9,12},{10,... | collective-permute-start | bytes 92168 | tf_op jit(solution)/shard_map/ppermute | solution.py:45
  14.5 2.4 %collective-permute-done.5.other = bf16[24,640]{1,0:T(8,128)(2,1)S(1)} collective-permute-done((bf16[24,640]{1,0:T(8,128)(2,1)S(1)}, bf16[24,640]{1,0:T(8,128)(2,1)S(1)}, u32[]{:S(2)}, u32[]{:S(2)}) %collective-permute-start.5) | collective-permute-done | bytes 30752 | tf_op jit(solution)/shard_map/ppermute | solution.py:45
  16.9 2.0 %collective-permute-start.7 = (bf16[24,640]{1,0:T(8,128)(2,1)S(1)}, bf16[24,640]{1,0:T(8,128)(2,1)S(1)}, u32[]{:S(2)}, u32[]{:S(2)}) collective-permute-start(bf16[24,640]{1,0:T(8,128)(2,1)S(1)} %whole.1.refs_0_.mine), channel_id=1, source_target_pairs={{0,9},{1,8},{2,11},{3,10},{4,13},{5,12},{6,15},{7,14},{8,1},{9,0},... | collective-permute-start | bytes 92168 | tf_op jit(solution)/shard_map/ppermute | solution.py:45
  18.9 0.1 arrange.1
  19.0 1.8 %collective-permute-start.6 = (bf16[24,1280]{1,0:T(8,128)(2,1)S(1)}, bf16[24,1280]{1,0:T(8,128)(2,1)S(1)}, u32[]{:S(2)}, u32[]{:S(2)}) collective-permute-start(bf16[24,1280]{1,0:T(8,128)(2,1)S(1)} %get-tuple-element.37.mine), channel_id=1, source_target_pairs={{0,5},{1,4},{2,7},{3,6},{4,1},{5,0},{6,3},{7,2},{8,13},{9,12},{10,... | collective-permute-start | bytes 184328 | tf_op jit(solution)/shard_map/ppermute | solution.py:45
  20.9 0.3 collective-permute-done.7.other
  21.2 0.1 own.1
  21.3 1.1 %collective-permute-start.9 = (bf16[24,640]{1,0:T(8,128)(2,1)S(1)}, bf16[24,640]{1,0:T(8,128)(2,1)S(1)}, u32[]{:S(2)}, u32[]{:S(2)}) collective-permute-start(bf16[24,640]{1,0:T(8,128)(2,1)S(1)} %get-tuple-element.40.mine), channel_id=1, source_target_pairs={{0,5},{1,4},{2,7},{3,6},{4,1},{5,0},{6,3},{7,2},{8,13},{9,12},{10,... | collective-permute-start | bytes 92168 | tf_op jit(solution)/shard_map/ppermute | solution.py:45
  22.4 0.6 %collective-permute-done.6.other = bf16[24,1280]{1,0:T(8,128)(2,1)S(1)} collective-permute-done((bf16[24,1280]{1,0:T(8,128)(2,1)S(1)}, bf16[24,1280]{1,0:T(8,128)(2,1)S(1)}, u32[]{:S(2)}, u32[]{:S(2)}) %collective-permute-start.6) | collective-permute-done | bytes 61472 | tf_op jit(solution)/shard_map/ppermute | solution.py:45
  23.1 0.1 join_old.2.mine
  23.1 1.5 %collective-permute-start.8 = (bf16[24,2560]{1,0:T(8,128)(2,1)S(1)}, bf16[24,2560]{1,0:T(8,128)(2,1)S(1)}, u32[]{:S(2)}, u32[]{:S(2)}) collective-permute-start(bf16[24,2560]{1,0:T(8,128)(2,1)S(1)} %join_old.2.mine), channel_id=1, source_target_pairs={{0,3},{1,2},{2,1},{3,0},{4,7},{5,6},{6,5},{7,4},{8,11},{9,10},{10,... | collective-permute-start | bytes 368648 | tf_op jit(solution)/shard_map/ppermute | solution.py:45
  24.7 2.2 %collective-permute-start.10 = (bf16[24,1280]{1,0:T(8,128)(2,1)S(1)}, bf16[24,1280]{1,0:T(8,128)(2,1)S(1)}, u32[]{:S(2)}, u32[]{:S(2)}) collective-permute-start(bf16[24,1280]{1,0:T(8,128)(2,1)S(1)} %copies.1.refs_1_), channel_id=1, source_target_pairs={{0,19},{1,18},{2,17},{3,16},{4,23},{5,22},{6,21},{7,20},{8,27},{9,... | collective-permute-start | bytes 184328 | tf_op jit(solution)/shard_map/ppermute | solution.py:45
  26.9 0.6 %collective-permute-start.11 = (bf16[24,1280]{1,0:T(8,128)(2,1)S(1)}, bf16[24,1280]{1,0:T(8,128)(2,1)S(1)}, u32[]{:S(2)}, u32[]{:S(2)}) collective-permute-start(bf16[24,1280]{1,0:T(8,128)(2,1)S(1)} %copies.1.refs_1_), channel_id=1, source_target_pairs={{0,16},{1,17},{2,18},{3,19},{4,20},{5,21},{6,22},{7,23},{8,24},{9,... | collective-permute-start | bytes 184328 | tf_op jit(solution)/shard_map/ppermute | solution.py:45
  27.5 0.2 collective-permute-start.12
  27.7 1.5 %collective-permute-start.15 = (bf16[3,2560]{1,0:T(4,128)(2,1)S(1)}, bf16[3,2560]{1,0:T(4,128)(2,1)S(1)}, u32[]{:S(2)}, u32[]{:S(2)}) collective-permute-start(bf16[3,2560]{1,0:T(4,128)(2,1)S(1)} %get-tuple-element.39.refs_0_), channel_id=1, source_target_pairs={{0,16},{1,17},{2,18},{3,19},{4,20},{5,21},{6,22},{7,23},{8,24},{9,... | collective-permute-start | bytes 46088 | tf_op jit(solution)/shard_map/ppermute | solution.py:45
  29.3 0.3 collective-permute-done.8.other
  29.6 0.1 join_old.3.refs_0_.old
  29.6 0.4 %collective-permute-start.14 = (bf16[24,5120]{1,0:T(8,128)(2,1)S(1)}, bf16[24,5120]{1,0:T(8,128)(2,1)S(1)}, u32[]{:S(2)}, u32[]{:S(2)}) collective-permute-start(bf16[24,5120]{1,0:T(8,128)(2,1)S(1)} %join_old.3.refs_0_.old), channel_id=1, source_target_pairs={{0,1},{1,0},{2,3},{3,2},{4,5},{5,4},{6,7},{7,6},{8,9},{9,8},{10,11... | collective-permute-start | bytes 737288 | tf_op jit(solution)/shard_map/ppermute | solution.py:45
  30.0 1.6 %collective-permute-done.11.refs_3_ = bf16[24,1280]{1,0:T(8,128)(2,1)S(1)} collective-permute-done((bf16[24,1280]{1,0:T(8,128)(2,1)S(1)}, bf16[24,1280]{1,0:T(8,128)(2,1)S(1)}, u32[]{:S(2)}, u32[]{:S(2)}) %collective-permute-start.11) | collective-permute-done | bytes 61472 | tf_op jit(solution)/shard_map/ppermute | solution.py:45
  31.7 0.4 %collective-permute-start.13 = (bf16[24,5120]{1,0:T(8,128)(2,1)S(1)}, bf16[24,5120]{1,0:T(8,128)(2,1)S(1)}, u32[]{:S(2)}, u32[]{:S(2)}) collective-permute-start(bf16[24,5120]{1,0:T(8,128)(2,1)S(1)} %across.1.new), channel_id=1, source_target_pairs={{0,1},{1,0},{2,3},{3,2},{4,5},{5,4},{6,7},{7,6},{8,9},{9,8},{10,11... | collective-permute-start | bytes 737288 | tf_op jit(solution)/shard_map/ppermute | solution.py:45
  32.1 1.0 %product.1 = (bf16[48,256]{1,0:T(8,128)(2,1)S(1)}, f32[3,5120]{1,0:T(4,128)S(1)}, f32[3,5120]{1,0:T(4,128)S(1)}, f32[3,5120]{1,0:T(4,128)S(1)}) custom-call(bf16[24,5120]{1,0:T(8,128)(2,1)S(1)} %join_old.3.refs_0_.old, bf16[24,5120]{1,0:T(8,128)(2,1)S(1)} %collective-permute-done.14.old_other, bf16[256,5120]{1,0:T(8,128)(2,1)S(1)} %get-tuple-element.41.cot, ...), custom_call_target="tpu_custom_call" | custom-call | flops 125829120 | bytes 1000000 | tf_op jit(solution)/shard_map/product/pallas_call | solution.py:24
  33.1 0.1 collective-permute-done.13.new_other
  33.2 1.2 %last.1 = (bf16[48,5120]{1,0:T(8,128)(2,1)}, bf16[48,256]{1,0:T(8,128)(2,1)}, f32[3,5120]{1,0:T(4,128)}, f32[3,5120]{1,0:T(4,128)}, f32[3,5120]{1,0:T(4,128)}) custom-call(bf16[24,5120]{1,0:T(8,128)(2,1)S(1)} %across.1.new, bf16[24,5120]{1,0:T(8,128)(2,1)S(1)} %collective-permute-done.13.new_other, bf16[48,256]{1,0:T(8,128)(2,1)S(1)} %get-tuple-element.42.refs_0_, ...), custom_call_target="tpu_custom_call" | custom-call | flops 1000000 | bytes 1000000 | tf_op jit(solution)/shard_map/last/pallas_call | solution.py:24
  (19 shorter events, 0.2 us)
Async XLA Ops:
  0.6 3.8 %copy-start = (f32[3,5120]{1,0:T(4,128)S(1)}, f32[3,5120]{1,0:T(4,128)}, u32[]{:S(2)}) copy-start(f32[3,5120]{1,0:T(4,128)} %master.3) | copy-start | bytes 184324
  0.6 3.8 %copy-start.1 = (f32[3,5120]{1,0:T(4,128)S(1)}, f32[3,5120]{1,0:T(4,128)}, u32[]{:S(2)}) copy-start(f32[3,5120]{1,0:T(4,128)} %moment.3) | copy-start | bytes 184324
  0.7 3.8 %copy-start.2 = (f32[3,5120]{1,0:T(4,128)S(1)}, f32[3,5120]{1,0:T(4,128)}, u32[]{:S(2)}) copy-start(f32[3,5120]{1,0:T(4,128)} %second.3) | copy-start | bytes 184324
  2.8 1.7 %collective-permute-start = (bf16[24,5120]{1,0:T(8,128)(2,1)S(1)}, bf16[24,5120]{1,0:T(8,128)(2,1)S(1)}, u32[]{:S(2)}, u32[]{:S(2)}) collective-permute-start(bf16[24,5120]{1,0:T(8,128)(2,1)S(1)} %get-tuple-element.29), channel_id=1, source_target_pairs={{0,1},{1,0},{2,3},{3,2},{4,5},{5,4},{6,7},{7,6},{8,9},{9,8},{10,11... | collective-permute-start | bytes 737288 | tf_op jit(solution)/shard_map/ppermute | solution.py:45
  4.6 7.0 %collective-permute-start.2 = (bf16[24,1280]{1,0:T(8,128)(2,1)S(1)}, bf16[24,1280]{1,0:T(8,128)(2,1)S(1)}, u32[]{:S(2)}, u32[]{:S(2)}) collective-permute-start(bf16[24,1280]{1,0:T(8,128)(2,1)S(1)} %get-tuple-element.32), channel_id=1, source_target_pairs={{0,19},{1,18},{2,17},{3,16},{4,23},{5,22},{6,21},{7,20},{8,27},{9,... | collective-permute-start | bytes 184328 | tf_op jit(solution)/shard_map/ppermute | solution.py:45
  8.2 4.4 %collective-permute-start.3 = (bf16[24,1280]{1,0:T(8,128)(2,1)S(1)}, bf16[24,1280]{1,0:T(8,128)(2,1)S(1)}, u32[]{:S(2)}, u32[]{:S(2)}) collective-permute-start(bf16[24,1280]{1,0:T(8,128)(2,1)S(1)} %get-tuple-element.33), channel_id=1, source_target_pairs={{0,16},{1,17},{2,18},{3,19},{4,20},{5,21},{6,22},{7,23},{8,24},{9,... | collective-permute-start | bytes 184328 | tf_op jit(solution)/shard_map/ppermute | solution.py:45
  8.8 4.0 %collective-permute-start.4 = (bf16[24,1280]{1,0:T(8,128)(2,1)S(1)}, bf16[24,1280]{1,0:T(8,128)(2,1)S(1)}, u32[]{:S(2)}, u32[]{:S(2)}) collective-permute-start(bf16[24,1280]{1,0:T(8,128)(2,1)S(1)} %get-tuple-element.34), channel_id=1, source_target_pairs={{0,3},{1,2},{2,1},{3,0},{4,7},{5,6},{6,5},{7,4},{8,11},{9,10},{10,... | collective-permute-start | bytes 184328 | tf_op jit(solution)/shard_map/ppermute | solution.py:45
  8.8 10.1 %collective-permute-start.1 = (bf16[15,2560]{1,0:T(8,128)(2,1)S(1)}, bf16[15,2560]{1,0:T(8,128)(2,1)S(1)}, u32[]{:S(2)}, u32[]{:S(2)}) collective-permute-start(bf16[15,2560]{1,0:T(8,128)(2,1)S(1)} %get-tuple-element.30.state), channel_id=1, source_target_pairs={{0,9},{1,8},{2,11},{3,10},{4,13},{5,12},{6,15},{7,14},{8,1},{9,0},... | collective-permute-start | bytes 230408 | tf_op jit(solution)/shard_map/ppermute | solution.py:45
  12.9 4.0 %collective-permute-start.5 = (bf16[24,640]{1,0:T(8,128)(2,1)S(1)}, bf16[24,640]{1,0:T(8,128)(2,1)S(1)}, u32[]{:S(2)}, u32[]{:S(2)}) collective-permute-start(bf16[24,640]{1,0:T(8,128)(2,1)S(1)} %get-tuple-element.36), channel_id=1, source_target_pairs={{0,5},{1,4},{2,7},{3,6},{4,1},{5,0},{6,3},{7,2},{8,13},{9,12},{10,... | collective-permute-start | bytes 92168 | tf_op jit(solution)/shard_map/ppermute | solution.py:45
  16.9 4.3 %collective-permute-start.7 = (bf16[24,640]{1,0:T(8,128)(2,1)S(1)}, bf16[24,640]{1,0:T(8,128)(2,1)S(1)}, u32[]{:S(2)}, u32[]{:S(2)}) collective-permute-start(bf16[24,640]{1,0:T(8,128)(2,1)S(1)} %whole.1.refs_0_.mine), channel_id=1, source_target_pairs={{0,9},{1,8},{2,11},{3,10},{4,13},{5,12},{6,15},{7,14},{8,1},{9,0},... | collective-permute-start | bytes 92168 | tf_op jit(solution)/shard_map/ppermute | solution.py:45
  19.0 4.0 %collective-permute-start.6 = (bf16[24,1280]{1,0:T(8,128)(2,1)S(1)}, bf16[24,1280]{1,0:T(8,128)(2,1)S(1)}, u32[]{:S(2)}, u32[]{:S(2)}) collective-permute-start(bf16[24,1280]{1,0:T(8,128)(2,1)S(1)} %get-tuple-element.37.mine), channel_id=1, source_target_pairs={{0,5},{1,4},{2,7},{3,6},{4,1},{5,0},{6,3},{7,2},{8,13},{9,12},{10,... | collective-permute-start | bytes 184328 | tf_op jit(solution)/shard_map/ppermute | solution.py:45
  21.3 3.4 %collective-permute-start.9 = (bf16[24,640]{1,0:T(8,128)(2,1)S(1)}, bf16[24,640]{1,0:T(8,128)(2,1)S(1)}, u32[]{:S(2)}, u32[]{:S(2)}) collective-permute-start(bf16[24,640]{1,0:T(8,128)(2,1)S(1)} %get-tuple-element.40.mine), channel_id=1, source_target_pairs={{0,5},{1,4},{2,7},{3,6},{4,1},{5,0},{6,3},{7,2},{8,13},{9,12},{10,... | collective-permute-start | bytes 92168 | tf_op jit(solution)/shard_map/ppermute | solution.py:45
  23.1 6.4 %collective-permute-start.8 = (bf16[24,2560]{1,0:T(8,128)(2,1)S(1)}, bf16[24,2560]{1,0:T(8,128)(2,1)S(1)}, u32[]{:S(2)}, u32[]{:S(2)}) collective-permute-start(bf16[24,2560]{1,0:T(8,128)(2,1)S(1)} %join_old.2.mine), channel_id=1, source_target_pairs={{0,3},{1,2},{2,1},{3,0},{4,7},{5,6},{6,5},{7,4},{8,11},{9,10},{10,... | collective-permute-start | bytes 368648 | tf_op jit(solution)/shard_map/ppermute | solution.py:45
  24.7 5.3 %collective-permute-start.10 = (bf16[24,1280]{1,0:T(8,128)(2,1)S(1)}, bf16[24,1280]{1,0:T(8,128)(2,1)S(1)}, u32[]{:S(2)}, u32[]{:S(2)}) collective-permute-start(bf16[24,1280]{1,0:T(8,128)(2,1)S(1)} %copies.1.refs_1_), channel_id=1, source_target_pairs={{0,19},{1,18},{2,17},{3,16},{4,23},{5,22},{6,21},{7,20},{8,27},{9,... | collective-permute-start | bytes 184328 | tf_op jit(solution)/shard_map/ppermute | solution.py:45
  26.9 4.7 %collective-permute-start.11 = (bf16[24,1280]{1,0:T(8,128)(2,1)S(1)}, bf16[24,1280]{1,0:T(8,128)(2,1)S(1)}, u32[]{:S(2)}, u32[]{:S(2)}) collective-permute-start(bf16[24,1280]{1,0:T(8,128)(2,1)S(1)} %copies.1.refs_1_), channel_id=1, source_target_pairs={{0,16},{1,17},{2,18},{3,19},{4,20},{5,21},{6,22},{7,23},{8,24},{9,... | collective-permute-start | bytes 184328 | tf_op jit(solution)/shard_map/ppermute | solution.py:45
  27.5 4.1 %collective-permute-start.12 = (bf16[24,1280]{1,0:T(8,128)(2,1)S(1)}, bf16[24,1280]{1,0:T(8,128)(2,1)S(1)}, u32[]{:S(2)}, u32[]{:S(2)}) collective-permute-start(bf16[24,1280]{1,0:T(8,128)(2,1)S(1)} %copies.1.refs_1_), channel_id=1, source_target_pairs={{0,3},{1,2},{2,1},{3,0},{4,7},{5,6},{6,5},{7,4},{8,11},{9,10},{10,... | collective-permute-start | bytes 184328 | tf_op jit(solution)/shard_map/ppermute | solution.py:45
  27.7 4.3 %collective-permute-start.15 = (bf16[3,2560]{1,0:T(4,128)(2,1)S(1)}, bf16[3,2560]{1,0:T(4,128)(2,1)S(1)}, u32[]{:S(2)}, u32[]{:S(2)}) collective-permute-start(bf16[3,2560]{1,0:T(4,128)(2,1)S(1)} %get-tuple-element.39.refs_0_), channel_id=1, source_target_pairs={{0,16},{1,17},{2,18},{3,19},{4,20},{5,21},{6,22},{7,23},{8,24},{9,... | collective-permute-start | bytes 46088 | tf_op jit(solution)/shard_map/ppermute | solution.py:45
  29.6 2.4 %collective-permute-start.14 = (bf16[24,5120]{1,0:T(8,128)(2,1)S(1)}, bf16[24,5120]{1,0:T(8,128)(2,1)S(1)}, u32[]{:S(2)}, u32[]{:S(2)}) collective-permute-start(bf16[24,5120]{1,0:T(8,128)(2,1)S(1)} %join_old.3.refs_0_.old), channel_id=1, source_target_pairs={{0,1},{1,0},{2,3},{3,2},{4,5},{5,4},{6,7},{7,6},{8,9},{9,8},{10,11... | collective-permute-start | bytes 737288 | tf_op jit(solution)/shard_map/ppermute | solution.py:45
  31.7 1.6 %collective-permute-start.13 = (bf16[24,5120]{1,0:T(8,128)(2,1)S(1)}, bf16[24,5120]{1,0:T(8,128)(2,1)S(1)}, u32[]{:S(2)}, u32[]{:S(2)}) collective-permute-start(bf16[24,5120]{1,0:T(8,128)(2,1)S(1)} %across.1.new), channel_id=1, source_target_pairs={{0,1},{1,0},{2,3},{3,2},{4,5},{5,4},{6,7},{7,6},{8,9},{9,8},{10,11... | collective-permute-start | bytes 737288 | tf_op jit(solution)/shard_map/ppermute | solution.py:45

commit v7 on v6

--- a/solution.py
+++ b/solution.py
@@ -219,18 +219,19 @@
         out[:, columns(dx, ref.shape[1])] = ref[...].astype(F32)
 
 
-def product_body(per, high, old, old_other, cot, gradient, master, moment, second, grad, *states):
+def product_body(per, high, old, old_other, cot, gradient, master, moment, second, move, grad, *states):
+    move[...] = one_hot(grad.shape[0], per, high)
     both = jnp.concatenate([old[...], old_other[...]], axis=0)
     rows = dot(both, cot[...], 1, 1).astype(BF16)
     for ref, value in zip(states, adam_update(master[...], moment[...], second[...], gradient[...])):
         ref[...] = value
-    grad[...] = dot(one_hot(grad.shape[0], per, high), rows, 0, 0).astype(BF16)
-
-
-def last_body(per, high, new, new_other, *refs):
+    grad[...] = dot(move[...], rows, 0, 0).astype(BF16)
+
+
+def last_body(new, new_other, order, *refs):
     held, outs, (out, sems) = refs[:4], refs[4:9], refs[9:]
     copies = []
-    move = one_hot(out.shape[0], per, high)
+    move = order[...]
     tile = out.shape[1] // OUT_COPIES
     half = new.shape[0]
     for i in range(OUT_COPIES):
@@ -315,11 +316,11 @@
     new_other = swap(new, 0, 0, 1)
     (grad,) = call(wide_body, [((per, width), F32)], "gradient", grads, cost=MAIN)
     outs = [((rows, tokens), BF16), *[((per, width), F32)] * 3]
-    held = call(functools.partial(product_body, per, high), outs, "product",
+    order, *held = call(functools.partial(product_body, per, high), [((rows, rows), BF16), *outs], "product",
                 [old, old_other, cot, grad, *states], cost=2 * rows * width * tokens)
     outs = [((rows, width), BF16), *outs]
     updated, input_grad, *states = call(
-        functools.partial(last_body, per, high), outs, "last", [new, new_other, *held],
+        last_body, outs, "last", [new, new_other, order, *held],
         out_specs=(pl.BlockSpec(memory_space=pltpu.HBM),) * 5,
         scratch_shapes=[pltpu.VMEM(*outs[0]), pltpu.SemaphoreType.DMA((4 + OUT_COPIES,))],
     )

time: 34.6 us -> 34.6 us (level)
  no operation moved by 1% of the time
where the time goes in v7:
time: 34.6 us; the launch traced here: 34.4 us
  starting transfers between devices  21 us (61%)
  waiting for transfers between devices  7.71 us (22%)
  Pallas kernels  5.02 us (15%)
  between operations  0.73 us (2%)
    ppermute x16, starting transfers between devices, swap(): lax.ppermute(value, (*CHIPS, 'core'), [(i, i ^ bits) for i in range(count)])  21 us
    ppermute x16, waiting for transfers between devices, swap(): lax.ppermute(value, (*CHIPS, 'core'), [(i, i ^ bits) for i in range(count)])  7.71 us
    pallas_call x13, Pallas kernels, call(): pl.pallas_call(body, out_shape=tuple((jax.ShapeDtypeStruct(*out) for out...  5.02 us
  transfers between devices with their start and end apart: 16, of which 9 were waited for; matrix products, arithmetic and copies ran while one was open for 0% of the time, Pallas kernels for 5%

profile of v7, /device:TPU:0, one launch (start us, length us, event | category | flops | bytes accessed | tf_op | source)
XLA Modules:
  0.0 34.4 jit_solution(7566804926911893714)
XLA Ops:
  0.7 2.1 %partial.1 = (f32[24,5120]{1,0:T(8,128)S(1)}, bf16[24,5120]{1,0:T(8,128)(2,1)S(1)}, bf16[256,5120]{1,0:T(8,128)(2,1)S(1)}) custom-call(bf16[48,256]{1,0:T(8,128)(2,1)} %bitcast.2, bf16[256,5120]{1,0:T(8,128)(2,1)} %cot_hbm.1), custom_call_target="tpu_custom_call" | custom-call | flops 125829120 | bytes 1000000 | tf_op jit(solution)/shard_map/partial/pallas_call | solution.py:24
  2.8 0.5 %collective-permute-start = (bf16[24,5120]{1,0:T(8,128)(2,1)S(1)}, bf16[24,5120]{1,0:T(8,128)(2,1)S(1)}, u32[]{:S(2)}, u32[]{:S(2)}) collective-permute-start(bf16[24,5120]{1,0:T(8,128)(2,1)S(1)} %get-tuple-element.30), channel_id=1, source_target_pairs={{0,1},{1,0},{2,3},{3,2},{4,5},{5,4},{6,7},{7,6},{8,9},{9,8},{10,11... | collective-permute-start | bytes 737288 | tf_op jit(solution)/shard_map/ppermute | solution.py:45
  3.3 1.1 %collective-permute-done.recv_ref = bf16[24,5120]{1,0:T(8,128)(2,1)S(1)} collective-permute-done((bf16[24,5120]{1,0:T(8,128)(2,1)S(1)}, bf16[24,5120]{1,0:T(8,128)(2,1)S(1)}, u32[]{:S(2)}, u32[]{:S(2)}) %collective-permute-start) | collective-permute-done | bytes 245792 | tf_op jit(solution)/shard_map/ppermute | solution.py:45
  4.5 0.1 middle.1
  4.6 3.6 %collective-permute-start.2 = (bf16[24,1280]{1,0:T(8,128)(2,1)S(1)}, bf16[24,1280]{1,0:T(8,128)(2,1)S(1)}, u32[]{:S(2)}, u32[]{:S(2)}) collective-permute-start(bf16[24,1280]{1,0:T(8,128)(2,1)S(1)} %get-tuple-element.33), channel_id=1, source_target_pairs={{0,19},{1,18},{2,17},{3,16},{4,23},{5,22},{6,21},{7,20},{8,27},{9,... | collective-permute-start | bytes 184328 | tf_op jit(solution)/shard_map/ppermute | solution.py:45
  8.2 0.6 %collective-permute-start.3 = (bf16[24,1280]{1,0:T(8,128)(2,1)S(1)}, bf16[24,1280]{1,0:T(8,128)(2,1)S(1)}, u32[]{:S(2)}, u32[]{:S(2)}) collective-permute-start(bf16[24,1280]{1,0:T(8,128)(2,1)S(1)} %get-tuple-element.34), channel_id=1, source_target_pairs={{0,16},{1,17},{2,18},{3,19},{4,20},{5,21},{6,22},{7,23},{8,24},{9,... | collective-permute-start | bytes 184328 | tf_op jit(solution)/shard_map/ppermute | solution.py:45
  8.8 2.8 %collective-permute-start.1 = (bf16[15,2560]{1,0:T(8,128)(2,1)S(1)}, bf16[15,2560]{1,0:T(8,128)(2,1)S(1)}, u32[]{:S(2)}, u32[]{:S(2)}) collective-permute-start(bf16[15,2560]{1,0:T(8,128)(2,1)S(1)} %get-tuple-element.31.state), channel_id=1, source_target_pairs={{0,9},{1,8},{2,11},{3,10},{4,13},{5,12},{6,15},{7,14},{8,1},{9,0},... | collective-permute-start | bytes 230408 | tf_op jit(solution)/shard_map/ppermute | solution.py:45
  11.6 1.0 %collective-permute-done.3.refs_2_ = bf16[24,1280]{1,0:T(8,128)(2,1)S(1)} collective-permute-done((bf16[24,1280]{1,0:T(8,128)(2,1)S(1)}, bf16[24,1280]{1,0:T(8,128)(2,1)S(1)}, u32[]{:S(2)}, u32[]{:S(2)}) %collective-permute-start.3) | collective-permute-done | bytes 61472 | tf_op jit(solution)/shard_map/ppermute | solution.py:45
  12.6 0.2 collective-permute-done.4.refs_3_
  12.9 1.6 %collective-permute-start.5 = (bf16[24,640]{1,0:T(8,128)(2,1)S(1)}, bf16[24,640]{1,0:T(8,128)(2,1)S(1)}, u32[]{:S(2)}, u32[]{:S(2)}) collective-permute-start(bf16[24,640]{1,0:T(8,128)(2,1)S(1)} %get-tuple-element.37), channel_id=1, source_target_pairs={{0,5},{1,4},{2,7},{3,6},{4,1},{5,0},{6,3},{7,2},{8,13},{9,12},{10,... | collective-permute-start | bytes 92168 | tf_op jit(solution)/shard_map/ppermute | solution.py:45
  14.5 2.4 %collective-permute-done.5.other = bf16[24,640]{1,0:T(8,128)(2,1)S(1)} collective-permute-done((bf16[24,640]{1,0:T(8,128)(2,1)S(1)}, bf16[24,640]{1,0:T(8,128)(2,1)S(1)}, u32[]{:S(2)}, u32[]{:S(2)}) %collective-permute-start.5) | collective-permute-done | bytes 30752 | tf_op jit(solution)/shard_map/ppermute | solution.py:45
  16.9 2.0 %collective-permute-start.7 = (bf16[24,640]{1,0:T(8,128)(2,1)S(1)}, bf16[24,640]{1,0:T(8,128)(2,1)S(1)}, u32[]{:S(2)}, u32[]{:S(2)}) collective-permute-start(bf16[24,640]{1,0:T(8,128)(2,1)S(1)} %whole.1.refs_0_.mine), channel_id=1, source_target_pairs={{0,9},{1,8},{2,11},{3,10},{4,13},{5,12},{6,15},{7,14},{8,1},{9,0},... | collective-permute-start | bytes 92168 | tf_op jit(solution)/shard_map/ppermute | solution.py:45
  18.9 0.1 arrange.1
  19.0 1.8 %collective-permute-start.6 = (bf16[24,1280]{1,0:T(8,128)(2,1)S(1)}, bf16[24,1280]{1,0:T(8,128)(2,1)S(1)}, u32[]{:S(2)}, u32[]{:S(2)}) collective-permute-start(bf16[24,1280]{1,0:T(8,128)(2,1)S(1)} %get-tuple-element.38.mine), channel_id=1, source_target_pairs={{0,5},{1,4},{2,7},{3,6},{4,1},{5,0},{6,3},{7,2},{8,13},{9,12},{10,... | collective-permute-start | bytes 184328 | tf_op jit(solution)/shard_map/ppermute | solution.py:45
  20.9 0.3 collective-permute-done.7.other
  21.2 0.1 own.1
  21.3 1.1 %collective-permute-start.9 = (bf16[24,640]{1,0:T(8,128)(2,1)S(1)}, bf16[24,640]{1,0:T(8,128)(2,1)S(1)}, u32[]{:S(2)}, u32[]{:S(2)}) collective-permute-start(bf16[24,640]{1,0:T(8,128)(2,1)S(1)} %get-tuple-element.41.mine), channel_id=1, source_target_pairs={{0,5},{1,4},{2,7},{3,6},{4,1},{5,0},{6,3},{7,2},{8,13},{9,12},{10,... | collective-permute-start | bytes 92168 | tf_op jit(solution)/shard_map/ppermute | solution.py:45
  22.4 0.6 %collective-permute-done.6.other = bf16[24,1280]{1,0:T(8,128)(2,1)S(1)} collective-permute-done((bf16[24,1280]{1,0:T(8,128)(2,1)S(1)}, bf16[24,1280]{1,0:T(8,128)(2,1)S(1)}, u32[]{:S(2)}, u32[]{:S(2)}) %collective-permute-start.6) | collective-permute-done | bytes 61472 | tf_op jit(solution)/shard_map/ppermute | solution.py:45
  23.1 0.1 join_old.2.mine
  23.1 1.5 %collective-permute-start.8 = (bf16[24,2560]{1,0:T(8,128)(2,1)S(1)}, bf16[24,2560]{1,0:T(8,128)(2,1)S(1)}, u32[]{:S(2)}, u32[]{:S(2)}) collective-permute-start(bf16[24,2560]{1,0:T(8,128)(2,1)S(1)} %join_old.2.mine), channel_id=1, source_target_pairs={{0,3},{1,2},{2,1},{3,0},{4,7},{5,6},{6,5},{7,4},{8,11},{9,10},{10,... | collective-permute-start | bytes 368648 | tf_op jit(solution)/shard_map/ppermute | solution.py:45
  24.7 2.2 %collective-permute-start.10 = (bf16[24,1280]{1,0:T(8,128)(2,1)S(1)}, bf16[24,1280]{1,0:T(8,128)(2,1)S(1)}, u32[]{:S(2)}, u32[]{:S(2)}) collective-permute-start(bf16[24,1280]{1,0:T(8,128)(2,1)S(1)} %copies.1.refs_1_), channel_id=1, source_target_pairs={{0,19},{1,18},{2,17},{3,16},{4,23},{5,22},{6,21},{7,20},{8,27},{9,... | collective-permute-start | bytes 184328 | tf_op jit(solution)/shard_map/ppermute | solution.py:45
  26.9 0.6 %collective-permute-start.11 = (bf16[24,1280]{1,0:T(8,128)(2,1)S(1)}, bf16[24,1280]{1,0:T(8,128)(2,1)S(1)}, u32[]{:S(2)}, u32[]{:S(2)}) collective-permute-start(bf16[24,1280]{1,0:T(8,128)(2,1)S(1)} %copies.1.refs_1_), channel_id=1, source_target_pairs={{0,16},{1,17},{2,18},{3,19},{4,20},{5,21},{6,22},{7,23},{8,24},{9,... | collective-permute-start | bytes 184328 | tf_op jit(solution)/shard_map/ppermute | solution.py:45
  27.5 0.2 collective-permute-start.12
  27.7 1.5 %collective-permute-start.15 = (bf16[3,2560]{1,0:T(4,128)(2,1)S(1)}, bf16[3,2560]{1,0:T(4,128)(2,1)S(1)}, u32[]{:S(2)}, u32[]{:S(2)}) collective-permute-start(bf16[3,2560]{1,0:T(4,128)(2,1)S(1)} %get-tuple-element.40.refs_0_), channel_id=1, source_target_pairs={{0,16},{1,17},{2,18},{3,19},{4,20},{5,21},{6,22},{7,23},{8,24},{9,... | collective-permute-start | bytes 46088 | tf_op jit(solution)/shard_map/ppermute | solution.py:45
  29.3 0.3 collective-permute-done.8.other
  29.6 0.1 join_old.3.refs_0_.old
  29.6 0.4 %collective-permute-start.14 = (bf16[24,5120]{1,0:T(8,128)(2,1)S(1)}, bf16[24,5120]{1,0:T(8,128)(2,1)S(1)}, u32[]{:S(2)}, u32[]{:S(2)}) collective-permute-start(bf16[24,5120]{1,0:T(8,128)(2,1)S(1)} %join_old.3.refs_0_.old), channel_id=1, source_target_pairs={{0,1},{1,0},{2,3},{3,2},{4,5},{5,4},{6,7},{7,6},{8,9},{9,8},{10,11... | collective-permute-start | bytes 737288 | tf_op jit(solution)/shard_map/ppermute | solution.py:45
  30.0 1.6 %collective-permute-done.11.refs_3_ = bf16[24,1280]{1,0:T(8,128)(2,1)S(1)} collective-permute-done((bf16[24,1280]{1,0:T(8,128)(2,1)S(1)}, bf16[24,1280]{1,0:T(8,128)(2,1)S(1)}, u32[]{:S(2)}, u32[]{:S(2)}) %collective-permute-start.11) | collective-permute-done | bytes 61472 | tf_op jit(solution)/shard_map/ppermute | solution.py:45
  31.7 0.4 %collective-permute-start.13 = (bf16[24,5120]{1,0:T(8,128)(2,1)S(1)}, bf16[24,5120]{1,0:T(8,128)(2,1)S(1)}, u32[]{:S(2)}, u32[]{:S(2)}) collective-permute-start(bf16[24,5120]{1,0:T(8,128)(2,1)S(1)} %across.1.new), channel_id=1, source_target_pairs={{0,1},{1,0},{2,3},{3,2},{4,5},{5,4},{6,7},{7,6},{8,9},{9,8},{10,11... | collective-permute-start | bytes 737288 | tf_op jit(solution)/shard_map/ppermute | solution.py:45
  32.1 1.0 %product.1 = (bf16[48,48]{1,0:T(8,128)(2,1)S(1)}, bf16[48,256]{1,0:T(8,128)(2,1)S(1)}, f32[3,5120]{1,0:T(4,128)S(1)}, f32[3,5120]{1,0:T(4,128)S(1)}, f32[3,5120]{1,0:T(4,128)S(1)}) custom-call(bf16[24,5120]{1,0:T(8,128)(2,1)S(1)} %join_old.3.refs_0_.old, bf16[24,5120]{1,0:T(8,128)(2,1)S(1)} %collective-permute-done.14.old_other, ...), custom_call_target="tpu_custom_call" | custom-call | flops 125829120 | bytes 1000000 | tf_op jit(solution)/shard_map/product/pallas_call | solution.py:24
  33.1 0.1 collective-permute-done.13.new_other
  33.2 1.2 %last.1 = (bf16[48,5120]{1,0:T(8,128)(2,1)}, bf16[48,256]{1,0:T(8,128)(2,1)}, f32[3,5120]{1,0:T(4,128)}, f32[3,5120]{1,0:T(4,128)}, f32[3,5120]{1,0:T(4,128)}) custom-call(bf16[24,5120]{1,0:T(8,128)(2,1)S(1)} %across.1.new, bf16[24,5120]{1,0:T(8,128)(2,1)S(1)} %collective-permute-done.13.new_other, bf16[48,48]{1,0:T(8,128)(2,1)S(1)} %get-tuple-element.43.order, ...), custom_call_target="tpu_custom_call" | custom-call | flops 1000000 | bytes 1000000 | tf_op jit(solution)/shard_map/last/pallas_call | solution.py:24
  (19 shorter events, 0.2 us)
Async XLA Ops:
  0.6 3.8 %copy-start = (f32[3,5120]{1,0:T(4,128)S(1)}, f32[3,5120]{1,0:T(4,128)}, u32[]{:S(2)}) copy-start(f32[3,5120]{1,0:T(4,128)} %master.3) | copy-start | bytes 184324
  0.6 3.8 %copy-start.1 = (f32[3,5120]{1,0:T(4,128)S(1)}, f32[3,5120]{1,0:T(4,128)}, u32[]{:S(2)}) copy-start(f32[3,5120]{1,0:T(4,128)} %moment.3) | copy-start | bytes 184324
  0.7 3.8 %copy-start.2 = (f32[3,5120]{1,0:T(4,128)S(1)}, f32[3,5120]{1,0:T(4,128)}, u32[]{:S(2)}) copy-start(f32[3,5120]{1,0:T(4,128)} %second.3) | copy-start | bytes 184324
  2.8 1.7 %collective-permute-start = (bf16[24,5120]{1,0:T(8,128)(2,1)S(1)}, bf16[24,5120]{1,0:T(8,128)(2,1)S(1)}, u32[]{:S(2)}, u32[]{:S(2)}) collective-permute-start(bf16[24,5120]{1,0:T(8,128)(2,1)S(1)} %get-tuple-element.30), channel_id=1, source_target_pairs={{0,1},{1,0},{2,3},{3,2},{4,5},{5,4},{6,7},{7,6},{8,9},{9,8},{10,11... | collective-permute-start | bytes 737288 | tf_op jit(solution)/shard_map/ppermute | solution.py:45
  4.6 7.0 %collective-permute-start.2 = (bf16[24,1280]{1,0:T(8,128)(2,1)S(1)}, bf16[24,1280]{1,0:T(8,128)(2,1)S(1)}, u32[]{:S(2)}, u32[]{:S(2)}) collective-permute-start(bf16[24,1280]{1,0:T(8,128)(2,1)S(1)} %get-tuple-element.33), channel_id=1, source_target_pairs={{0,19},{1,18},{2,17},{3,16},{4,23},{5,22},{6,21},{7,20},{8,27},{9,... | collective-permute-start | bytes 184328 | tf_op jit(solution)/shard_map/ppermute | solution.py:45
  8.2 4.4 %collective-permute-start.3 = (bf16[24,1280]{1,0:T(8,128)(2,1)S(1)}, bf16[24,1280]{1,0:T(8,128)(2,1)S(1)}, u32[]{:S(2)}, u32[]{:S(2)}) collective-permute-start(bf16[24,1280]{1,0:T(8,128)(2,1)S(1)} %get-tuple-element.34), channel_id=1, source_target_pairs={{0,16},{1,17},{2,18},{3,19},{4,20},{5,21},{6,22},{7,23},{8,24},{9,... | collective-permute-start | bytes 184328 | tf_op jit(solution)/shard_map/ppermute | solution.py:45
  8.8 4.0 %collective-permute-start.4 = (bf16[24,1280]{1,0:T(8,128)(2,1)S(1)}, bf16[24,1280]{1,0:T(8,128)(2,1)S(1)}, u32[]{:S(2)}, u32[]{:S(2)}) collective-permute-start(bf16[24,1280]{1,0:T(8,128)(2,1)S(1)} %get-tuple-element.35), channel_id=1, source_target_pairs={{0,3},{1,2},{2,1},{3,0},{4,7},{5,6},{6,5},{7,4},{8,11},{9,10},{10,... | collective-permute-start | bytes 184328 | tf_op jit(solution)/shard_map/ppermute | solution.py:45
  8.8 10.1 %collective-permute-start.1 = (bf16[15,2560]{1,0:T(8,128)(2,1)S(1)}, bf16[15,2560]{1,0:T(8,128)(2,1)S(1)}, u32[]{:S(2)}, u32[]{:S(2)}) collective-permute-start(bf16[15,2560]{1,0:T(8,128)(2,1)S(1)} %get-tuple-element.31.state), channel_id=1, source_target_pairs={{0,9},{1,8},{2,11},{3,10},{4,13},{5,12},{6,15},{7,14},{8,1},{9,0},... | collective-permute-start | bytes 230408 | tf_op jit(solution)/shard_map/ppermute | solution.py:45
  12.9 4.0 %collective-permute-start.5 = (bf16[24,640]{1,0:T(8,128)(2,1)S(1)}, bf16[24,640]{1,0:T(8,128)(2,1)S(1)}, u32[]{:S(2)}, u32[]{:S(2)}) collective-permute-start(bf16[24,640]{1,0:T(8,128)(2,1)S(1)} %get-tuple-element.37), channel_id=1, source_target_pairs={{0,5},{1,4},{2,7},{3,6},{4,1},{5,0},{6,3},{7,2},{8,13},{9,12},{10,... | collective-permute-start | bytes 92168 | tf_op jit(solution)/shard_map/ppermute | solution.py:45
  16.9 4.3 %collective-permute-start.7 = (bf16[24,640]{1,0:T(8,128)(2,1)S(1)}, bf16[24,640]{1,0:T(8,128)(2,1)S(1)}, u32[]{:S(2)}, u32[]{:S(2)}) collective-permute-start(bf16[24,640]{1,0:T(8,128)(2,1)S(1)} %whole.1.refs_0_.mine), channel_id=1, source_target_pairs={{0,9},{1,8},{2,11},{3,10},{4,13},{5,12},{6,15},{7,14},{8,1},{9,0},... | collective-permute-start | bytes 92168 | tf_op jit(solution)/shard_map/ppermute | solution.py:45
  19.0 4.0 %collective-permute-start.6 = (bf16[24,1280]{1,0:T(8,128)(2,1)S(1)}, bf16[24,1280]{1,0:T(8,128)(2,1)S(1)}, u32[]{:S(2)}, u32[]{:S(2)}) collective-permute-start(bf16[24,1280]{1,0:T(8,128)(2,1)S(1)} %get-tuple-element.38.mine), channel_id=1, source_target_pairs={{0,5},{1,4},{2,7},{3,6},{4,1},{5,0},{6,3},{7,2},{8,13},{9,12},{10,... | collective-permute-start | bytes 184328 | tf_op jit(solution)/shard_map/ppermute | solution.py:45
  21.3 3.4 %collective-permute-start.9 = (bf16[24,640]{1,0:T(8,128)(2,1)S(1)}, bf16[24,640]{1,0:T(8,128)(2,1)S(1)}, u32[]{:S(2)}, u32[]{:S(2)}) collective-permute-start(bf16[24,640]{1,0:T(8,128)(2,1)S(1)} %get-tuple-element.41.mine), channel_id=1, source_target_pairs={{0,5},{1,4},{2,7},{3,6},{4,1},{5,0},{6,3},{7,2},{8,13},{9,12},{10,... | collective-permute-start | bytes 92168 | tf_op jit(solution)/shard_map/ppermute | solution.py:45
  23.1 6.4 %collective-permute-start.8 = (bf16[24,2560]{1,0:T(8,128)(2,1)S(1)}, bf16[24,2560]{1,0:T(8,128)(2,1)S(1)}, u32[]{:S(2)}, u32[]{:S(2)}) collective-permute-start(bf16[24,2560]{1,0:T(8,128)(2,1)S(1)} %join_old.2.mine), channel_id=1, source_target_pairs={{0,3},{1,2},{2,1},{3,0},{4,7},{5,6},{6,5},{7,4},{8,11},{9,10},{10,... | collective-permute-start | bytes 368648 | tf_op jit(solution)/shard_map/ppermute | solution.py:45
  24.7 5.3 %collective-permute-start.10 = (bf16[24,1280]{1,0:T(8,128)(2,1)S(1)}, bf16[24,1280]{1,0:T(8,128)(2,1)S(1)}, u32[]{:S(2)}, u32[]{:S(2)}) collective-permute-start(bf16[24,1280]{1,0:T(8,128)(2,1)S(1)} %copies.1.refs_1_), channel_id=1, source_target_pairs={{0,19},{1,18},{2,17},{3,16},{4,23},{5,22},{6,21},{7,20},{8,27},{9,... | collective-permute-start | bytes 184328 | tf_op jit(solution)/shard_map/ppermute | solution.py:45
  26.9 4.7 %collective-permute-start.11 = (bf16[24,1280]{1,0:T(8,128)(2,1)S(1)}, bf16[24,1280]{1,0:T(8,128)(2,1)S(1)}, u32[]{:S(2)}, u32[]{:S(2)}) collective-permute-start(bf16[24,1280]{1,0:T(8,128)(2,1)S(1)} %copies.1.refs_1_), channel_id=1, source_target_pairs={{0,16},{1,17},{2,18},{3,19},{4,20},{5,21},{6,22},{7,23},{8,24},{9,... | collective-permute-start | bytes 184328 | tf_op jit(solution)/shard_map/ppermute | solution.py:45
  27.5 4.1 %collective-permute-start.12 = (bf16[24,1280]{1,0:T(8,128)(2,1)S(1)}, bf16[24,1280]{1,0:T(8,128)(2,1)S(1)}, u32[]{:S(2)}, u32[]{:S(2)}) collective-permute-start(bf16[24,1280]{1,0:T(8,128)(2,1)S(1)} %copies.1.refs_1_), channel_id=1, source_target_pairs={{0,3},{1,2},{2,1},{3,0},{4,7},{5,6},{6,5},{7,4},{8,11},{9,10},{10,... | collective-permute-start | bytes 184328 | tf_op jit(solution)/shard_map/ppermute | solution.py:45
  27.7 4.3 %collective-permute-start.15 = (bf16[3,2560]{1,0:T(4,128)(2,1)S(1)}, bf16[3,2560]{1,0:T(4,128)(2,1)S(1)}, u32[]{:S(2)}, u32[]{:S(2)}) collective-permute-start(bf16[3,2560]{1,0:T(4,128)(2,1)S(1)} %get-tuple-element.40.refs_0_), channel_id=1, source_target_pairs={{0,16},{1,17},{2,18},{3,19},{4,20},{5,21},{6,22},{7,23},{8,24},{9,... | collective-permute-start | bytes 46088 | tf_op jit(solution)/shard_map/ppermute | solution.py:45
  29.6 2.4 %collective-permute-start.14 = (bf16[24,5120]{1,0:T(8,128)(2,1)S(1)}, bf16[24,5120]{1,0:T(8,128)(2,1)S(1)}, u32[]{:S(2)}, u32[]{:S(2)}) collective-permute-start(bf16[24,5120]{1,0:T(8,128)(2,1)S(1)} %join_old.3.refs_0_.old), channel_id=1, source_target_pairs={{0,1},{1,0},{2,3},{3,2},{4,5},{5,4},{6,7},{7,6},{8,9},{9,8},{10,11... | collective-permute-start | bytes 737288 | tf_op jit(solution)/shard_map/ppermute | solution.py:45
  31.7 1.6 %collective-permute-start.13 = (bf16[24,5120]{1,0:T(8,128)(2,1)S(1)}, bf16[24,5120]{1,0:T(8,128)(2,1)S(1)}, u32[]{:S(2)}, u32[]{:S(2)}) collective-permute-start(bf16[24,5120]{1,0:T(8,128)(2,1)S(1)} %across.1.new), channel_id=1, source_target_pairs={{0,1},{1,0},{2,3},{3,2},{4,5},{5,4},{6,7},{7,6},{8,9},{9,8},{10,11... | collective-permute-start | bytes 737288 | tf_op jit(solution)/shard_map/ppermute | solution.py:45
